TPU v7x, 32 devices: a whole 2x2x4 slice. The times are simulated.
32 devices in a mesh: label: 8 (over z, y), doc: 4 (over x, core).
Axes of the slice: x: 2, y: 2, z: 4, core: 2. Of those that a mesh axis runs over, the one named last changes fastest.
Arguments:
- doc_embed: bfloat16 [512, 768], P(('doc', 'label')), may hold values from -1 to 1
- classifier: bfloat16 [256, 64, 768], P('label'), may hold values from -3 to 3
- shortlist: int32 [4, 8, 32], P('doc', 'label'), may hold values from 0 to 255, as said below
- positives: int32 [512, 8], P('doc'), may hold values from 0 to 16383, as said below
Outputs:
- doc_grad: bfloat16 [512, 768], P(('doc', 'label'))
- class_grad: float32 [256, 64, 768], P(('label', 'doc'))
- mean_loss: float32 [], replicated
Inputs may be any that keep to these rules, and one draw needn't show every extreme that they name: `shortlist`: tile t belongs to the device with label index t // 32. One device's 32 tile ids are distinct; at most 8 of them belong to one owner, and in every device exactly 8 belong to some owner. `positives`: every positive label lies in a tile listed by some device of the document's block.
All inputs are finite; a program needn't handle non-finite values.
Results may differ from a plain program's by a relative error of at most 0.0075.
Values may be sent and summed in bfloat16 or wider, within the bound.
No kernel may reach another device: no remote copies, remote signals or barrier semaphores. Data moves between devices by JAX's collectives and lax.ppermute only.
A program may use at most 128 MiB of HBM per device.

v0:
```python
import math

import jax
import jax.numpy as jnp
from jax import lax
from jax.sharding import PartitionSpec as P


def score_blocks(doc_panel, wanted, tile_rows, label_ids, live):
    total_rows = doc_panel.shape[0]
    row_step = math.gcd(total_rows, 512)
    block_count = total_rows // row_step
    panels = doc_panel.reshape(block_count, row_step, doc_panel.shape[1])
    wanted_blocks = wanted.reshape(block_count, row_step, wanted.shape[1])

    def score_one(pair):
        row_block, wanted_rows = pair
        scores = lax.dot_general(
            row_block, tile_rows, (((1,), (1,)), ((), ())), preferred_element_type=jnp.float32
        )
        targets = jnp.zeros(scores.shape, jnp.float32)
        for column in range(wanted_rows.shape[1]):
            targets = jnp.maximum(
                targets, (wanted_rows[:, column, None] == label_ids[None, :]).astype(jnp.float32)
            )
        losses = (jax.nn.softplus(scores) - targets * scores) * live[None, :]
        score_grad = ((jax.nn.sigmoid(scores) - targets) * 0.125 * live[None, :]).astype(
            jnp.bfloat16
        )
        return (score_grad, jnp.sum(losses))

    grads_all, loss_parts = lax.map(score_one, (panels, wanted_blocks))
    return (grads_all.reshape(total_rows, tile_rows.shape[0]), jnp.sum(loss_parts))


def slot_grads(score_grad, doc_panel, tile_size):
    columns = score_grad.shape[1]
    col_width = min(1024, columns)
    group_count = columns // col_width

    def group_one(group_index):
        row_part = lax.dynamic_slice_in_dim(score_grad, group_index * col_width, col_width, 1)
        summed = lax.dot_general(
            row_part, doc_panel, (((0,), (0,)), ((), ())), preferred_element_type=jnp.float32
        )
        return summed.astype(jnp.bfloat16)

    grouped = lax.map(group_one, jnp.arange(group_count, dtype=jnp.int32))
    return grouped.reshape(columns // tile_size, tile_size, doc_panel.shape[1])


def accumulate(tile_grads, target_ids, tiles_dev):
    slot_total = target_ids.shape[0]
    selector = (jnp.arange(tiles_dev, dtype=jnp.int32)[:, None] == target_ids[None, :]).astype(
        jnp.bfloat16
    )
    flat = tile_grads.reshape(slot_total, tile_grads.shape[1] * tile_grads.shape[2])
    summed = jnp.dot(selector, flat, preferred_element_type=jnp.float32)
    return summed.reshape(tiles_dev, tile_grads.shape[1], tile_grads.shape[2])


def per_device(doc_embed, classifier, shortlist, positives):
    label_count = lax.axis_size("label")
    doc_count = lax.axis_size("doc")
    tiles_dev = classifier.shape[0]
    tile_size = classifier.shape[1]
    emb_width = classifier.shape[2]
    tile_ids = shortlist.reshape(-1)
    listed = tile_ids.shape[0]
    capacity = max(2, 2 * listed // label_count)
    owners = tile_ids // tiles_dev
    local_ids = tile_ids % tiles_dev
    positions = jnp.arange(listed, dtype=jnp.int32)
    same_owner = (owners[:, None] == owners[None, :]) & (positions[:, None] > positions[None, :])
    slot_rank = jnp.sum(same_owner.astype(jnp.int32), axis=1)
    slot_index = owners * capacity + slot_rank
    request = jnp.full((label_count * capacity,), -1, jnp.int32).at[slot_index].set(local_ids)
    request = request.reshape(label_count, capacity)
    incoming = lax.all_to_all(request, "label", split_axis=0, concat_axis=0, tiled=True)
    incoming_flat = incoming.reshape(-1)
    doc_panel = lax.all_gather(doc_embed, "label", axis=0, tiled=True)
    offsets = jnp.arange(tile_size, dtype=jnp.int32)
    valid = (incoming_flat >= 0).astype(jnp.float32)
    owned = classifier[jnp.maximum(incoming_flat, 0)]
    tile_rows = owned.reshape(incoming_flat.shape[0] * tile_size, emb_width)
    global_ids = lax.axis_index("label") * tiles_dev + jnp.maximum(incoming_flat, 0)
    label_ids = (global_ids[:, None] * tile_size + offsets[None, :]).reshape(-1)
    live = jnp.repeat(valid, tile_size)
    score_grad, loss_sum = score_blocks(doc_panel, positives, tile_rows, label_ids, live)
    tile_grads = slot_grads(score_grad, doc_panel, tile_size)
    own_grad = accumulate(tile_grads, incoming_flat, tiles_dev)
    doc_sum = lax.psum_scatter(
        jnp.dot(score_grad, tile_rows, preferred_element_type=jnp.float32),
        "label",
        scatter_dimension=0,
        tiled=True,
    )
    class_grad = lax.psum_scatter(
        own_grad.astype(jnp.bfloat16), "doc", scatter_dimension=0, tiled=True
    ).astype(jnp.float32)
    loss_all = lax.psum(loss_sum, ("label", "doc"))
    entry_total = doc_panel.shape[0] * doc_count * label_count * listed * tile_size
    mean_loss = loss_all / entry_total
    return (doc_sum.astype(jnp.bfloat16), class_grad, mean_loss)


def solution(mesh):
    placed = (
        P(("doc", "label"), None),
        P("label", None, None),
        P("doc", "label", None),
        P("doc", None),
    )
    return jax.shard_map(
        per_device,
        mesh=mesh,
        in_specs=placed,
        out_specs=(P(("doc", "label"), None), P(("label", "doc"), None, None), P()),
        check_vma=False,
    )
```

profile of v0, /device:TPU:0, one launch (start us, length us, event | category | flops | bytes accessed | tf_op | source)
XLA Modules:
  0.0 177.5 jit_solution(109552988579558486)
XLA Ops:
  7.2 0.8 and_select_fusion
  8.2 0.7 fusion.14
  8.8 0.7 scatter_custom_fusion
  9.5 0.7 all_to_all.6
  10.2 7.3 %all-to-all-start = ((s32[8,1,8]{2,1,0:T(1,128)}), s32[8,1,8]{2,1,0:T(1,128)S(1)}, u32[]{:S(2)}, u32[]{:S(2)}) async-start(s32[8,1,8]{2,1,0:T(1,128)} %bitcast.6), calls=%async_computation | async-start | bytes 8192 | tf_op jit(solution)/shard_map/all_to_all | solution.py:79
  17.5 1.0 slice_bitcast_fusion.7
  18.5 31.3 %all_gather.3 = bf16[128,768]{1,0:T(8,128)(2,1)S(1)} all-gather(bf16[16,768]{1,0:T(8,128)(2,1)} %param.6), channel_id=1, replica_groups=mesh['label'=8,'doc'=4] {'label'}, dimensions={0}, use_global_device_ids=true | all-gather | bytes 221184 | tf_op jit(solution)/shard_map/all_gather | solution.py:81
  50.4 0.7 fusion.17
  51.6 3.6 %gather_fusion = bf16[64,64,768]{2,1,0:T(8,128)(2,1)} fusion(bf16[32,64,768]{2,1,0:T(8,128)(2,1)S(1)} %copy-done, s32[1024]{0:T(1024)S(1)} %pad_clamp_fusion), kind=kCustom, calls=%fused_computation | custom fusion | bytes 12583168 | tf_op jit(solution)/shard_map/gather | solution.py:84
  55.2 7.0 %fusion.9 = (f32[]{:T(128)}, bf16[128,4096]{0,1:T(8,128)(2,1)S(1)}) fusion(f32[4096]{0:T(1024)S(1)} %mul.71, s32[128]{0:T(128)S(1)} %get-tuple-element.107, s32[128]{0:T(128)S(1)} %get-tuple-element.108, s32[128]{0:T(128)S(1)} %get-tuple-element.102, s32[128]{0:T(128)S(1)} %get-tuple-element.103, s32[128]{0:T(128)S(1)} %get-tuple-element.104, ...), kind=kOutput, calls=%fused_computation.14 | convolution fusion | flops 826277888 | bytes 7589892 | tf_op jit(solution)/shard_map/while/body/eval_jaxpr/dot_general | solution.py:18
  62.1 1.0 copy-done.2
  63.1 1.8 %fusion.18 = f32[128,768]{1,0:T(8,128)} fusion(bf16[128,4096]{0,1:T(8,128)(2,1)S(1)} %get-tuple-element.145, bf16[4096,768]{1,0:T(8,128)(2,1)S(1)} %bitcast.83), kind=kOutput, calls=%fused_computation.54 | convolution fusion | flops 805306368 | bytes 7733248 | tf_op jit(solution)/shard_map/dot_general | solution.py:93
  65.0 15.6 %while.2 = (s32[]{:T(128)}, bf16[4,1024,768]{2,1,0:T(8,128)(2,1)}, s32[4]{0:T(128)S(1)}, bf16[128,4096]{0,1:T(8,128)(2,1)}, bf16[128,768]{1,0:T(8,128)(2,1)S(1)}...) while((s32[]{:T(128)}, bf16[4,1024,768]{2,1,0:T(8,128)(2,1)}, s32[4]{0:T(128)S(1)}, ...), condition=%wide.region_4.5_spmd, body=%wide.region_3.4_spmd.sunk | while | flops 202113024 | bytes 2031783 | solution.py:48
  66.3 2.7 %bitcast_dynamic-update-slice_fusion.2 = bf16[4,1024,768]{2,1,0:T(8,128)(2,1)} fusion(bf16[4,1024,768]{2,1,0:T(8,128)(2,1)} %get-tuple-element.152, s32[]{:T(128)S(6)} %copy.34, bf16[128,768]{1,0:T(8,128)(2,1)S(1)} %get-tuple-element.164, bf16[128,4096]{0,1:T(8,128)(2,1)} %get-tuple-element.163, s32[]{:T(128)S(6)} %select_n.68), kind=kOutput, calls=%fused_computation.3.clone.1 | convolution fusion | flops 202113024 | bytes 2031624 | tf_op jit(solution)/shard_map/while/body/eval_jaxpr/dot_general | solution.py:43
  70.2 2.7 %bitcast_dynamic-update-slice_fusion.2 = bf16[4,1024,768]{2,1,0:T(8,128)(2,1)} fusion(bf16[4,1024,768]{2,1,0:T(8,128)(2,1)} %get-tuple-element.152, s32[]{:T(128)S(6)} %copy.34, bf16[128,768]{1,0:T(8,128)(2,1)S(1)} %get-tuple-element.164, bf16[128,4096]{0,1:T(8,128)(2,1)} %get-tuple-element.163, s32[]{:T(128)S(6)} %select_n.68), kind=kOutput, calls=%fused_computation.3.clone.1 | convolution fusion | flops 202113024 | bytes 2031624 | tf_op jit(solution)/shard_map/while/body/eval_jaxpr/dot_general | solution.py:43
  74.1 2.7 %bitcast_dynamic-update-slice_fusion.2 = bf16[4,1024,768]{2,1,0:T(8,128)(2,1)} fusion(bf16[4,1024,768]{2,1,0:T(8,128)(2,1)} %get-tuple-element.152, s32[]{:T(128)S(6)} %copy.34, bf16[128,768]{1,0:T(8,128)(2,1)S(1)} %get-tuple-element.164, bf16[128,4096]{0,1:T(8,128)(2,1)} %get-tuple-element.163, s32[]{:T(128)S(6)} %select_n.68), kind=kOutput, calls=%fused_computation.3.clone.1 | convolution fusion | flops 202113024 | bytes 2031624 | tf_op jit(solution)/shard_map/while/body/eval_jaxpr/dot_general | solution.py:43
  78.0 2.7 %bitcast_dynamic-update-slice_fusion.2 = bf16[4,1024,768]{2,1,0:T(8,128)(2,1)} fusion(bf16[4,1024,768]{2,1,0:T(8,128)(2,1)} %get-tuple-element.152, s32[]{:T(128)S(6)} %copy.34, bf16[128,768]{1,0:T(8,128)(2,1)S(1)} %get-tuple-element.164, bf16[128,4096]{0,1:T(8,128)(2,1)} %get-tuple-element.163, s32[]{:T(128)S(6)} %select_n.68), kind=kOutput, calls=%fused_computation.3.clone.1 | convolution fusion | flops 202113024 | bytes 2031624 | tf_op jit(solution)/shard_map/while/body/eval_jaxpr/dot_general | solution.py:43
  80.7 9.0 %reshape_reshape.3 = bf16[64,49152]{1,0:T(8,128)(2,1)} reshape(bf16[4,1024,768]{2,1,0:T(8,128)(2,1)} %get-tuple-element.54) | data formatting | bytes 12582912 | tf_op jit(solution)/shard_map/reshape;reshape | solution.py:57
  89.6 3.8 %convert_bitcast_fusion = bf16[64,4,8,768]{3,2,1,0:T(8,128)(2,1)S(1)} fusion(bf16[8,64,8,768]{3,2,1,0:T(8,128)(2,1)} %bitcast.81, s32[64]{0:T(128)S(1)} %reshape.202), kind=kOutput, calls=%fused_computation.11 | convolution fusion | flops 202901504 | bytes 9437440 | tf_op jit(solution)/shard_map/dot_general | solution.py:58
  93.4 1.9 %copy.24 = bf16[64,4,8,768]{3,2,0,1:T(8,128)(2,1)} copy(bf16[64,4,8,768]{3,2,1,0:T(8,128)(2,1)S(1)} %convert_bitcast_fusion) | data formatting | bytes 6291456
  95.3 40.0 %psum.7 = f32[]{:T(128)} all-reduce(f32[]{:T(128)} %get-tuple-element.99), channel_id=1, replica_groups=mesh['label'=8,'doc'=4] {'label','doc'}, use_global_device_ids=true, to_apply=%region_7.8 | all-reduce | flops 1 | bytes 8 | tf_op jit(solution)/shard_map/psum | solution.py:101
  135.9 1.4 convert_element_type.66
  137.4 29.8 %reduce-scatter.7.cloned.1.call-done = bf16[8,49152]{1,0:T(8,128)(2,1)} async-done(((bf16[32,49152]{1,0:T(8,128)(2,1)}), bf16[8,49152]{1,0:T(8,128)(2,1)}) %reduce-scatter.7.cloned.1.call-update) | async-done | bytes 786448
  167.1 2.4 %copy.19 = f32[8,64,768]{2,1,0:T(8,128)} copy(bf16[8,64,768]{2,0,1:T(8,128)(2,1)} %bitcast.85) | data formatting | bytes 2359296
  (29 shorter events, 3.7 us)
Async XLA Ops:
  7.2 44.4 %copy-start = (bf16[32,64,768]{2,1,0:T(8,128)(2,1)S(1)}, bf16[32,64,768]{2,1,0:T(8,128)(2,1)}, u32[]{:S(2)}) copy-start(bf16[32,64,768]{2,1,0:T(8,128)(2,1)} %param.7) | copy-start | bytes 9437188
  10.2 39.7 %all-to-all-start = ((s32[8,1,8]{2,1,0:T(1,128)}), s32[8,1,8]{2,1,0:T(1,128)S(1)}, u32[]{:S(2)}, u32[]{:S(2)}) async-start(s32[8,1,8]{2,1,0:T(1,128)} %bitcast.6), calls=%async_computation | async-start | bytes 8192 | tf_op jit(solution)/shard_map/all_to_all | solution.py:79
  17.5 118.5 %reduce-scatter.5.cloned.1.call-start = ((), (), s32[]{:S(2)}) async-start(), calls=%async_computation.3 | async-start | bytes 442368 | tf_op jit(solution)/shard_map/reduce_scatter | solution.py:92
  55.2 7.9 %copy-start.1 = (bf16[64,64,768]{2,1,0:T(8,128)(2,1)S(1)}, bf16[64,64,768]{2,1,0:T(8,128)(2,1)}, u32[]{:S(2)}) copy-start(bf16[64,64,768]{2,1,0:T(8,128)(2,1)} %gather_fusion) | copy-start | bytes 18874372
  62.1 1.0 copy-start.2
  65.0 102.2 %reduce-scatter.7.cloned.1.call-start = ((), (), s32[]{:S(2)}) async-start(), calls=%async_computation.4 | async-start | bytes 3932160
Sparse Core Ops, SparseCore 0:
  65.1 62.4 reduce-scatter.4
  130.1 36.9 reduce-scatter.6
where the time goes:
time: 178 us
  blocking collectives  71.3 us (40%)
  waiting for transfers between devices  29.8 us (17%)
  local copies, waits for them, and re-layouts  23.4 us (13%)
  matrix products  23.2 us (13%)
  between operations  15.9 us (9%)
  starting transfers between devices  7.36 us (4%)
  other arithmetic  3.86 us (2%)
  loops' own time  2.64 us (1%)
    psum x1, blocking collectives, per_device(): loss_all = lax.psum(loss_sum, ('label', 'doc'))  40 us
    all_gather x1, blocking collectives, per_device(): doc_panel = lax.all_gather(doc_embed, 'label', axis=0, tiled=True)  31.3 us
    unnamed x3, waiting for transfers between devices  29.8 us
    dot_general x4, matrix products, group_one(): lax.dot_general(row_part, doc_panel, (((0,), (0,)), ((), ())), preferred_...  10.7 us
    another operation x1, local copies, waits for them, and re-layouts, accumulate(): tile_grads.reshape(slot_total, tile_grads.shape[1] * tile_grads.shape[2])  8.96 us
    all_to_all x1, starting transfers between devices, per_device(): lax.all_to_all(request, 'label', split_axis=0, concat_axis=0, tiled=True)  7.28 us
    dot_general x1, matrix products, score_one(): lax.dot_general(row_block, tile_rows, (((1,), (1,)), ((), ())), preferred...  6.96 us
    unnamed x8, local copies, waits for them, and re-layouts  5.29 us
  transfers between devices with their start and end apart: 3, of which 1 were waited for; matrix products, arithmetic and copies ran while one was open for 17% of the time, Pallas kernels for 0%

commit v1 on v0

v1 whole, which is shorter than its diff:
```python
import functools

import jax
import jax.numpy as jnp
from jax import lax
from jax.experimental import pallas as pl
from jax.experimental.pallas import tpu as pltpu
from jax.sharding import PartitionSpec as P

LANES = 128


def flip(size, bit):
    return [(i, i ^ bit) for i in range(size)]


def set_counts(panel, owner, tiles_dev, width, picks):
    rows = panel.shape[0]
    ranks = panel[:, width:].astype(jnp.float32).reshape(rows // 16, 16, LANES)
    flat = jnp.sum(ranks, axis=0)
    first = owner * tiles_dev
    row_ids = lax.broadcasted_iota(jnp.int32, (16, LANES), 0)
    mine = jnp.where(row_ids == first // LANES, flat, 0.0)
    lane_ids = lax.broadcasted_iota(jnp.int32, (LANES, picks.shape[1]), 0)
    spread = (lane_ids == first % LANES + picks).astype(jnp.bfloat16)
    spread_rows = jnp.dot(mine.astype(jnp.bfloat16), spread, preferred_element_type=jnp.float32)
    return jnp.sum(spread_rows, axis=0, keepdims=True)


def score_set(panel, docs, pos_ref, rows, owner, half, core, dims):
    tiles_dev, tile, group, x_half = dims
    labels = rows.shape[0]
    column = lax.broadcasted_iota(jnp.int32, (1, labels), 1)
    slot = column // tile
    local = ((half * x_half + slot // group) * 2 + core) * group + slot % group
    counts = set_counts(panel, owner, tiles_dev, docs.shape[1], local)
    label_ids = (owner * tiles_dev + local) * tile + column % tile
    scores = lax.dot_general(
        docs, rows, (((1,), (1,)), ((), ())), preferred_element_type=jnp.float32
    )
    hit = pos_ref[:, 0:1] == label_ids
    for k in range(1, pos_ref.shape[1]):
        hit = hit | (pos_ref[:, k : k + 1] == label_ids)
    target = hit.astype(jnp.float32)
    small = jnp.exp(-jnp.abs(scores))
    losses = (jnp.maximum(scores, 0.0) + jnp.log1p(small) - target * scores) * counts
    share = 1.0 / (1.0 + small)
    sigmoid = jnp.where(scores >= 0.0, share, small * share)
    weight = ((sigmoid - target) * (counts * 0.125)).astype(jnp.bfloat16)
    return weight, jnp.sum(losses).reshape(1, 1)


def label_grad(weight, docs):
    return lax.dot_general(
        weight, docs, (((0,), (0,)), ((), ())), preferred_element_type=jnp.float32
    )


def first_kernel(dims, width, where_ref, panel_ref, pos_ref, rows_ref, grad_ref, weight_ref, loss_ref):
    panel = panel_ref[...]
    docs = panel[:, :width]
    rows = rows_ref[...].reshape(grad_ref.shape[0], width)
    weight, loss = score_set(
        panel, docs, pos_ref, rows, where_ref[0], where_ref[1], where_ref[2], dims
    )
    grad_ref[...] = label_grad(weight, docs).astype(grad_ref.dtype)
    weight_ref[...] = weight
    loss_ref[...] = loss


def second_kernel(
    dims, width, where_ref, panel_ref, pos_ref, rows_ref, old_rows_ref, old_weight_ref, old_loss_ref,
    grad_ref, part_ref, loss_ref,
):
    panel = panel_ref[...]
    docs = panel[:, :width]
    labels = grad_ref.shape[0]
    rows = rows_ref[...].reshape(labels, width)
    old_rows = old_rows_ref[...].reshape(labels, width)
    weight, loss = score_set(
        panel, docs, pos_ref, rows, where_ref[0], where_ref[1], where_ref[2], dims
    )
    grad_ref[...] = label_grad(weight, docs).astype(grad_ref.dtype)
    part_ref[...] = jnp.dot(weight, rows, preferred_element_type=jnp.float32) + jnp.dot(
        old_weight_ref[...], old_rows, preferred_element_type=jnp.float32
    )
    loss_ref[...] = loss + old_loss_ref[...]


def third_kernel(
    dims, width, where_ref, panel_ref, pos_ref, rows_ref, kept_rows_ref, part_ref, old_loss_ref,
    grad_ref, kept_ref, send_ref,
):
    panel = panel_ref[...]
    docs = panel[:, :width]
    labels = grad_ref.shape[0]
    owner, half, core = where_ref[0], where_ref[1], where_ref[2]
    rows = rows_ref[...].reshape(labels, width)
    weight, loss = score_set(panel, docs, pos_ref, rows, owner, half, core, dims)
    grad_ref[...] = label_grad(weight, docs).astype(grad_ref.dtype)
    part = part_ref[...] + jnp.dot(weight, rows, preferred_element_type=jnp.float32)
    kept_rows = kept_rows_ref[...].reshape(labels, width)
    weight, kept_loss = score_set(panel, docs, pos_ref, kept_rows, owner, half, 1 - core, dims)
    kept_ref[...] = label_grad(weight, docs)
    part = part + jnp.dot(weight, kept_rows, preferred_element_type=jnp.float32)
    send_ref[:, :width] = part.astype(jnp.bfloat16)
    total = loss + kept_loss + old_loss_ref[...]
    top = total.astype(jnp.bfloat16).astype(jnp.float32)
    mid = (total - top).astype(jnp.bfloat16).astype(jnp.float32)
    low = total - top - mid
    lanes = lax.broadcasted_iota(jnp.int32, (send_ref.shape[0], LANES), 1)
    terms = jnp.where(lanes == 0, top, jnp.where(lanes == 1, mid, jnp.where(lanes == 2, low, 0.0)))
    send_ref[:, width:] = terms.astype(jnp.bfloat16)


def per_device(doc_embed, classifier, shortlist, positives):
    label_count = lax.axis_size("label")
    doc_count = lax.axis_size("doc")
    tiles_dev, tile, width = classifier.shape
    doc_dev = doc_embed.shape[0]
    x_count = doc_count // 2
    x_half = x_count // 2
    group = tiles_dev // doc_count
    labels = x_half * group * tile
    block = doc_dev * label_count
    listed = shortlist.size
    owner = lax.axis_index("label")
    place = lax.axis_index("doc")
    core = place % 2
    high = place // 2 // x_half
    dims = (tiles_dev, tile, group, x_half)

    cells = lax.broadcasted_iota(jnp.int32, (16, LANES, listed), 0) * LANES
    cells = cells + lax.broadcasted_iota(jnp.int32, (16, LANES, listed), 1)
    marks = jnp.any(cells == shortlist.reshape(1, 1, listed), axis=2).astype(jnp.bfloat16)
    panel = jnp.concatenate([doc_embed, marks], axis=1)
    bit = 1
    while bit < label_count:
        panel = panel.reshape(1, -1, panel.shape[-1])
        other = lax.ppermute(panel, "label", flip(label_count, bit))
        panel = jnp.concatenate([panel, other], axis=0)
        bit *= 2
    stages = label_count.bit_length() - 1
    panel = panel.reshape((2,) * stages + (doc_dev, width + LANES))
    panel = panel.reshape(block, width + LANES)

    order = lax.iota(jnp.int32, label_count) ^ owner
    wanted = positives.reshape(label_count, doc_dev, positives.shape[1])[order]
    wanted = wanted.reshape(block, positives.shape[1])

    sets = classifier.reshape(2, x_half, 2, group * tile, width)
    full = pl.BlockSpec(memory_space=pltpu.VMEM)

    def rows_spec(swap_half, swap_core):
        def index(i, where):
            half = where[1] if not swap_half else 1 - where[1]
            side = where[2] if not swap_core else 1 - where[2]
            return (half, 0, side, 0, 0)

        return pl.BlockSpec((1, x_half, 1, group * tile, width), index)

    def whole(shape):
        return pl.BlockSpec(shape, lambda i, where: (0,) * len(shape))

    params = pltpu.CompilerParams(vmem_limit_bytes=40 * 1024 * 1024)
    f32, bf16 = jnp.float32, jnp.bfloat16
    shape = jax.ShapeDtypeStruct

    def cost(sets_scored, dots):
        return pl.CostEstimate(
            flops=2 * block * labels * width * dots,
            bytes_accessed=labels * width * 4 * sets_scored,
            transcendentals=3 * block * labels * sets_scored,
        )

    grad_shape = (labels, width)
    panel_spec = whole(panel.shape)
    pos_spec = whole(wanted.shape)
    where = jnp.stack([owner, 1 - high, 1 - core]).astype(jnp.int32)
    grad_a, weight_a, loss_a = pl.pallas_call(
        functools.partial(first_kernel, dims, width),
        grid_spec=pltpu.PrefetchScalarGridSpec(
            num_scalar_prefetch=1,
            grid=(1,),
            in_specs=[panel_spec, pos_spec, rows_spec(False, False)],
            out_specs=[whole(grad_shape), whole((block, labels)), whole((1, 1))],
        ),
        out_shape=[shape(grad_shape, bf16), shape((block, labels), bf16), shape((1, 1), f32)],
        compiler_params=params,
        cost_estimate=cost(1, 2),
    )(where, panel, wanted, sets)
    from_core_a = lax.ppermute(grad_a, "doc", flip(doc_count, 1))

    where = jnp.stack([owner, 1 - high, core]).astype(jnp.int32)
    grad_b, part, loss_b = pl.pallas_call(
        functools.partial(second_kernel, dims, width),
        grid_spec=pltpu.PrefetchScalarGridSpec(
            num_scalar_prefetch=1,
            grid=(1,),
            in_specs=[
                panel_spec, pos_spec, rows_spec(False, False), rows_spec(False, True),
                whole((block, labels)), whole((1, 1)),
            ],
            out_specs=[whole(grad_shape), whole((block, width)), whole((1, 1))],
        ),
        out_shape=[shape(grad_shape, bf16), shape((block, width), f32), shape((1, 1), f32)],
        compiler_params=params,
        cost_estimate=cost(1, 4),
    )(where, panel, wanted, sets, sets, weight_a, loss_a)
    to_x = (grad_b.astype(f32) + from_core_a.astype(f32)).astype(bf16)
    to_x, part = lax.optimization_barrier((to_x, part))
    from_x = lax.ppermute(to_x, "doc", flip(doc_count, doc_count // 2))

    where = jnp.stack([owner, high, 1 - core]).astype(jnp.int32)
    grad_c, kept, send = pl.pallas_call(
        functools.partial(third_kernel, dims, width),
        grid_spec=pltpu.PrefetchScalarGridSpec(
            num_scalar_prefetch=1,
            grid=(1,),
            in_specs=[
                panel_spec, pos_spec, rows_spec(False, False), rows_spec(False, True),
                whole((block, width)), whole((1, 1)),
            ],
            out_specs=[whole(grad_shape), whole(grad_shape), whole((block, width + LANES))],
        ),
        out_shape=[
            shape(grad_shape, bf16), shape(grad_shape, f32), shape((block, width + LANES), bf16)
        ],
        compiler_params=params,
        cost_estimate=cost(2, 6),
    )(where, panel, wanted, sets, sets, part, loss_b)
    from_core_c = lax.ppermute(grad_c, "doc", flip(doc_count, 1))
    kept = kept + from_core_c.astype(f32)

    send = send.reshape(label_count, doc_dev, width + LANES)[order]
    parts = lax.all_to_all(send, "label", split_axis=0, concat_axis=0, tiled=True)
    summed = jnp.sum(parts.astype(f32), axis=0)
    doc_grad = summed[:, :width].astype(bf16)
    loss = jnp.sum(summed[0:1, width : width + 3], axis=1)
    loss = loss + lax.ppermute(loss, "doc", flip(doc_count, 1))
    step = doc_count // 2
    while step > 1:
        loss = loss + lax.ppermute(loss, "doc", flip(doc_count, step))
        step //= 2

    class_grad = kept + from_x.astype(f32)
    class_grad = class_grad.reshape(x_half, group * tile, width)
    step = x_half // 2
    place_x = place // 2
    while step >= 1:
        pairs = class_grad.reshape(2, step, group * tile, width)
        mine = place_x // step % 2
        away = lax.dynamic_index_in_dim(pairs, 1 - mine, 0, keepdims=False)
        stay = lax.dynamic_index_in_dim(pairs, mine, 0, keepdims=False)
        got = lax.ppermute(away.astype(bf16), "doc", flip(doc_count, 2 * step))
        class_grad = stay + got.astype(f32)
        step //= 2
    class_grad = class_grad.reshape(group, tile, width)
    entry_total = block * doc_count * label_count * listed * tile
    return doc_grad, class_grad, loss[0] / entry_total


def solution(mesh):
    placed = (
        P(("doc", "label"), None),
        P("label", None, None),
        P("doc", "label", None),
        P("doc", None),
    )
    return jax.shard_map(
        per_device,
        mesh=mesh,
        in_specs=placed,
        out_specs=(P(("doc", "label"), None), P(("label", "doc"), None, None), P()),
        check_vma=False,
    )
```

time: 178 us -> 58.9 us (0.33)
  blocking collectives: 71.3 us -> 14.4 us
  matrix products: 23.2 us -> 0 us
  waiting for transfers between devices: 29.8 us -> 8.48 us
  local copies, waits for them, and re-layouts: 23.4 us -> 4.48 us
  between operations: 15.9 us -> 3.75 us
  Pallas kernels: 0 us -> 7.72 us
  starting transfers between devices: 7.36 us -> 13.5 us
  loops' own time: 2.64 us -> 0 us
  other arithmetic: 3.86 us -> 6.21 us
    psum x1 -> x0, blocking collectives: 40 us -> none  [per_device(): loss_all = lax.psum(loss_sum, ('label', 'doc'))]
    all_gather x1 -> x0, blocking collectives: 31.3 us -> none  [per_device(): doc_panel = lax.all_gather(doc_embed, 'label', axis=0, tiled=True)]
    unnamed x3 -> x0, waiting for transfers between devices: 29.8 us -> none
    dot_general x7 -> x0, matrix products: 23.2 us -> none  [the longest x4 10.7 us: group_one(): lax.dot_general(row_part, doc_panel, (((0,), (0,)), ((), ())), preferred_...]
    all_to_all x0 -> x1, blocking collectives: none -> 14.4 us  [per_device(): lax.all_to_all(send, 'label', split_axis=0, concat_axis=0, tiled=True)]
    ppermute x0 -> x8, starting transfers between devices: none -> 13.5 us  [the longest x3 8.21 us: per_device(): other = lax.ppermute(panel, 'label', flip(label_count, bit))]
    another operation x1 -> x0, local copies, waits for them, and re-layouts: 8.96 us -> none  [accumulate(): tile_grads.reshape(slot_total, tile_grads.shape[1] * tile_grads.shape[2])]
    ppermute x0 -> x8, waiting for transfers between devices: none -> 8.48 us  [the longest x3 5.27 us: per_device(): other = lax.ppermute(panel, 'label', flip(label_count, bit))]
  transfers between devices with their start and end apart: 3 -> 8, of which waited for: 1 -> 5; matrix products, arithmetic and copies ran while one was open for 17% -> 6% of each run, Pallas kernels for 0% -> 10%
where the time goes in v1:
time: 58.9 us; the launch traced here: 58.5 us
  blocking collectives  14.4 us (24%)
  starting transfers between devices  13.5 us (23%)
  waiting for transfers between devices  8.48 us (14%)
  Pallas kernels  7.72 us (13%)
  other arithmetic  6.21 us (11%)
  local copies, waits for them, and re-layouts  4.48 us (8%)
  between operations  3.75 us (6%)
    all_to_all x1, blocking collectives, per_device(): lax.all_to_all(send, 'label', split_axis=0, concat_axis=0, tiled=True)  14.4 us
    ppermute x3, starting transfers between devices, per_device(): other = lax.ppermute(panel, 'label', flip(label_count, bit))  8.21 us
    ppermute x3, waiting for transfers between devices, per_device(): other = lax.ppermute(panel, 'label', flip(label_count, bit))  5.27 us
    pallas_call x1, Pallas kernels, per_device(): pl.pallas_call(functools.partial(third_kernel, dims, width), grid_spec=pl...  3.34 us
    ppermute x1, starting transfers between devices, per_device(): from_x = lax.ppermute(to_x, 'doc', flip(doc_count, doc_count // 2))  3.06 us
    add x1, other arithmetic, per_device(): class_grad = kept + from_x.astype(f32)  2.72 us
    pallas_call x1, Pallas kernels, per_device(): pl.pallas_call(functools.partial(second_kernel, dims, width), grid_spec=p...  2.54 us
    ppermute x1, starting transfers between devices, per_device(): loss = loss + lax.ppermute(loss, 'doc', flip(doc_count, step))  1.89 us
  transfers between devices with their start and end apart: 8, of which 5 were waited for; matrix products, arithmetic and copies ran while one was open for 6% of the time, Pallas kernels for 10%

profile of v1, /device:TPU:0, one launch (start us, length us, event | category | flops | bytes accessed | tf_op | source)
XLA Modules:
  0.0 58.5 jit_solution(9921582140927058691)
XLA Ops:
  0.6 0.8 %fusion = pred[16,128]{1,0:T(8,128)(4,1)S(1)} fusion(s32[32]{0:T(128)} %bitcast.38, s32[16]{0:T(128)S(1)} %iota_multiply_fusion), kind=kLoop, calls=%fused_computation.6 | loop fusion | flops 194560 | bytes 2240 | tf_op jit(solution)/shard_map/reduce_or | solution.py:135
  1.4 0.7 %maximum_bitcast_fusion = bf16[1,16,896]{2,1,0:T(8,128)(2,1)S(1)} fusion(bf16[16,128]{1,0:T(8,128)(2,1)S(1)} %convert_element_type.22, bf16[16,768]{1,0:T(8,128)(2,1)} %param.4), kind=kLoop, calls=%fused_computation.11 | loop fusion | flops 57344 | bytes 57344 | tf_op jit(solution)/shard_map/reshape | solution.py:139
  2.2 3.0 %collective-permute-start = (bf16[1,16,896]{2,1,0:T(8,128)(2,1)S(1)}, bf16[1,16,896]{2,1,0:T(8,128)(2,1)S(1)}, u32[]{:S(2)}, u32[]{:S(2)}) collective-permute-start(bf16[1,16,896]{2,1,0:T(8,128)(2,1)S(1)} %maximum_bitcast_fusion), channel_id=1, source_target_pairs={{0,4},{4,0},{8,12},{12,8},{16,20},{20,16},{24,28},{28,24},{1,5},{5... | collective-permute-start | bytes 86024 | tf_op jit(solution)/shard_map/ppermute | solution.py:140
  5.2 1.8 %collective-permute-done = bf16[1,16,896]{2,1,0:T(8,128)(2,1)S(1)} collective-permute-done((bf16[1,16,896]{2,1,0:T(8,128)(2,1)S(1)}, bf16[1,16,896]{2,1,0:T(8,128)(2,1)S(1)}, u32[]{:S(2)}, u32[]{:S(2)}) %collective-permute-start) | collective-permute-done | bytes 28704 | tf_op jit(solution)/shard_map/ppermute | solution.py:140
  7.0 2.1 %collective-permute-start.1 = (bf16[1,32,896]{2,1,0:T(8,128)(2,1)S(1)}, bf16[1,32,896]{2,1,0:T(8,128)(2,1)S(1)}, u32[]{:S(2)}, u32[]{:S(2)}) collective-permute-start(bf16[1,32,896]{2,1,0:T(8,128)(2,1)S(1)} %bitcast.36), channel_id=1, source_target_pairs={{0,8},{4,12},{8,0},{12,4},{16,24},{20,28},{24,16},{28,20},{1,9},{5... | collective-permute-start | bytes 172040 | tf_op jit(solution)/shard_map/ppermute | solution.py:140
  9.2 2.2 %collective-permute-done.1 = bf16[1,32,896]{2,1,0:T(8,128)(2,1)S(1)} collective-permute-done((bf16[1,32,896]{2,1,0:T(8,128)(2,1)S(1)}, bf16[1,32,896]{2,1,0:T(8,128)(2,1)S(1)}, u32[]{:S(2)}, u32[]{:S(2)}) %collective-permute-start.1) | collective-permute-done | bytes 57376 | tf_op jit(solution)/shard_map/ppermute | solution.py:140
  11.3 3.1 %collective-permute-start.2 = (bf16[1,64,896]{2,1,0:T(8,128)(2,1)S(1)}, bf16[1,64,896]{2,1,0:T(8,128)(2,1)S(1)}, u32[]{:S(2)}, u32[]{:S(2)}) collective-permute-start(bf16[1,64,896]{2,1,0:T(8,128)(2,1)S(1)} %bitcast.34), channel_id=1, source_target_pairs={{0,16},{4,20},{8,24},{12,28},{16,0},{20,4},{24,8},{28,12},{1,17},{... | collective-permute-start | bytes 344072 | tf_op jit(solution)/shard_map/ppermute | solution.py:140
  14.4 0.8 %reshape.49 = s32[8,16,8]{1,0,2:T(8,128)S(1)} reshape(s32[128,8]{0,1:T(8,128)} %param.7) | data formatting | bytes 8192 | tf_op jit(solution)/shard_map/reshape | solution.py:148
  15.2 0.6 gather_fusion
  15.9 1.3 %collective-permute-done.2 = bf16[1,64,896]{2,1,0:T(8,128)(2,1)S(1)} collective-permute-done((bf16[1,64,896]{2,1,0:T(8,128)(2,1)S(1)}, bf16[1,64,896]{2,1,0:T(8,128)(2,1)S(1)}, u32[]{:S(2)}, u32[]{:S(2)}) %collective-permute-start.2) | collective-permute-done | bytes 114720 | tf_op jit(solution)/shard_map/ppermute | solution.py:140
  17.3 1.9 %copy-done = bf16[32,64,768]{2,1,0:T(8,128)(2,1)S(1)} copy-done((bf16[32,64,768]{2,1,0:T(8,128)(2,1)S(1)}, bf16[32,64,768]{2,1,0:T(8,128)(2,1)}, u32[]{:S(2)}) %copy-start) | copy-done | bytes 3145752
  19.1 1.8 %shard_map.67 = (bf16[512,768]{1,0:T(8,128)(2,1)S(1)}, bf16[128,512]{1,0:T(8,128)(2,1)S(1)}, f32[1,1]{1,0:T(1,128)}) custom-call(s32[3]{0:T(128)S(1)} %get-tuple-element.26.where_ref, bf16[128,896]{1,0:T(8,128)(2,1)S(1)} %bitcast.26, s32[128,8]{1,0:T(8,128)S(1)} %bitcast.29, bf16[2,1,2,512,768]{4,3,2,1,0:T(8,128)(2,1)S(1)} %bitcast.21), custom_call_target="tpu_custom_call" | custom-call | flops 201326592 | bytes 1572864 | tf_op jit(solution)/shard_map/pallas_call | solution.py:180
  21.1 2.5 %shard_map.68 = (bf16[512,768]{1,0:T(8,128)(2,1)S(1)}, f32[128,768]{1,0:T(8,128)S(1)}, f32[1,1]{1,0:T(1,128)}) custom-call(s32[3]{0:T(128)S(1)} %pad_add_fusion.where_ref, bf16[128,896]{1,0:T(8,128)(2,1)S(1)} %bitcast.27, s32[128,8]{1,0:T(8,128)S(1)} %bitcast.30, bf16[2,1,2,512,768]{4,3,2,1,0:T(8,128)(2,1)S(1)} %bitcast.22, ...), custom_call_target="tpu_custom_call" | custom-call | flops 402653184 | bytes 1572864 | tf_op jit(solution)/shard_map/pallas_call | solution.py:195
  23.6 1.1 %add_convert_fusion = bf16[512,768]{1,0:T(8,128)(2,1)} fusion(bf16[512,768]{1,0:T(8,128)(2,1)S(1)} %collective-permute-done.3, bf16[512,768]{1,0:T(8,128)(2,1)S(1)} %get-tuple-element.16), kind=kLoop, calls=%fused_computation.3 | loop fusion | flops 1572864 | bytes 2359296 | tf_op jit(solution)/shard_map/convert_element_type | solution.py:210
  24.7 3.1 %collective-permute-start.5 = (bf16[512,768]{1,0:T(8,128)(2,1)}, bf16[512,768]{1,0:T(8,128)(2,1)}, u32[]{:S(2)}, u32[]{:S(2)}) collective-permute-start(bf16[512,768]{1,0:T(8,128)(2,1)} %add_convert_fusion), channel_id=1, source_target_pairs={{0,2},{1,3},{2,0},{3,1},{4,6},{5,7},{6,4},{7,5},{8,10},{9,11},{10,... | collective-permute-start | bytes 2359304 | tf_op jit(solution)/shard_map/ppermute | solution.py:212
  27.8 3.3 %shard_map.69 = (bf16[512,768]{1,0:T(8,128)(2,1)S(1)}, f32[512,768]{1,0:T(8,128)S(1)}, bf16[128,896]{1,0:T(8,128)(2,1)S(1)}) custom-call(s32[3]{0:T(128)S(1)} %get-tuple-element.25.where_ref, bf16[128,896]{1,0:T(8,128)(2,1)S(1)} %bitcast.28, s32[128,8]{1,0:T(8,128)S(1)} %bitcast.31, bf16[2,1,2,512,768]{4,3,2,1,0:T(8,128)(2,1)S(1)} %bitcast.24, ...), custom_call_target="tpu_custom_call" | custom-call | flops 603979776 | bytes 3145728 | tf_op jit(solution)/shard_map/pallas_call | solution.py:215
  31.4 0.6 gather_fusion.1
  32.0 14.4 %all_to_all.5 = bf16[8,16,896]{2,1,0:T(8,128)(2,1)S(1)} all-to-all(bf16[8,16,896]{2,1,0:T(8,128)(2,1)S(1)} %gather_fusion.1), channel_id=1, replica_groups=mesh['label'=8,'doc'=4] {'label'}, dimensions={0} | all-to-all | bytes 458752 | tf_op jit(solution)/shard_map/all_to_all | solution.py:236
  46.4 0.6 %slice.17 = bf16[16,768]{1,0:T(8,128)(2,1)} slice(f32[16,896]{1,0:T(8,128)S(1)} %convert_reduce_fusion), slice={[0:16], [0:768]} | slice | bytes 49152 | tf_op jit(solution)/shard_map/slice | solution.py:238
  47.0 0.6 %slice_reduce_fusion = f32[]{:T(128)} fusion(f32[16,896]{1,0:T(8,128)S(1)} %convert_reduce_fusion), kind=kLoop, calls=%fused_computation.15 | loop fusion | flops 2 | bytes 16 | tf_op jit(solution)/shard_map/reduce_sum | solution.py:239
  47.6 1.4 %collective-permute-done.6 = f32[1]{0:T(128)} collective-permute-done((f32[1]{0:T(128)}, f32[1]{0:T(128)}, u32[]{:S(2)}, u32[]{:S(2)}) %collective-permute-start.6) | collective-permute-done | bytes 36 | tf_op jit(solution)/shard_map/ppermute | solution.py:240
  50.3 1.9 %collective-permute-start.7 = (f32[1]{0:T(128)}, f32[1]{0:T(128)}, u32[]{:S(2)}, u32[]{:S(2)}) collective-permute-start(f32[1]{0:T(128)} %add.41), channel_id=1, source_target_pairs={{0,2},{1,3},{2,0},{3,1},{4,6},{5,7},{6,4},{7,5},{8,10},{9,11},{10,... | collective-permute-start | bytes 20 | tf_op jit(solution)/shard_map/ppermute | solution.py:243
  52.2 1.8 %collective-permute-done.7 = f32[1]{0:T(128)} collective-permute-done((f32[1]{0:T(128)}, f32[1]{0:T(128)}, u32[]{:S(2)}, u32[]{:S(2)}) %collective-permute-start.7) | collective-permute-done | bytes 36 | tf_op jit(solution)/shard_map/ppermute | solution.py:243
  54.7 2.7 %convert_add_fusion = f32[512,768]{1,0:T(8,128)} fusion(bf16[512,768]{1,0:T(8,128)(2,1)} %collective-permute-done.5, f32[512,768]{1,0:T(8,128)S(1)} %get-tuple-element.22, bf16[512,768]{1,0:T(8,128)(2,1)} %collective-permute-done.4), kind=kLoop, calls=%fused_computation.2 | loop fusion | flops 1572864 | bytes 4718592 | tf_op jit(solution)/shard_map/add | solution.py:246
  (21 shorter events, 0.7 us)
Async XLA Ops:
  2.2 4.8 %collective-permute-start = (bf16[1,16,896]{2,1,0:T(8,128)(2,1)S(1)}, bf16[1,16,896]{2,1,0:T(8,128)(2,1)S(1)}, u32[]{:S(2)}, u32[]{:S(2)}) collective-permute-start(bf16[1,16,896]{2,1,0:T(8,128)(2,1)S(1)} %maximum_bitcast_fusion), channel_id=1, source_target_pairs={{0,4},{4,0},{8,12},{12,8},{16,20},{20,16},{24,28},{28,24},{1,5},{5... | collective-permute-start | bytes 86024 | tf_op jit(solution)/shard_map/ppermute | solution.py:140
  7.0 4.3 %collective-permute-start.1 = (bf16[1,32,896]{2,1,0:T(8,128)(2,1)S(1)}, bf16[1,32,896]{2,1,0:T(8,128)(2,1)S(1)}, u32[]{:S(2)}, u32[]{:S(2)}) collective-permute-start(bf16[1,32,896]{2,1,0:T(8,128)(2,1)S(1)} %bitcast.36), channel_id=1, source_target_pairs={{0,8},{4,12},{8,0},{12,4},{16,24},{20,28},{24,16},{28,20},{1,9},{5... | collective-permute-start | bytes 172040 | tf_op jit(solution)/shard_map/ppermute | solution.py:140
  11.3 5.9 %collective-permute-start.2 = (bf16[1,64,896]{2,1,0:T(8,128)(2,1)S(1)}, bf16[1,64,896]{2,1,0:T(8,128)(2,1)S(1)}, u32[]{:S(2)}, u32[]{:S(2)}) collective-permute-start(bf16[1,64,896]{2,1,0:T(8,128)(2,1)S(1)} %bitcast.34), channel_id=1, source_target_pairs={{0,16},{4,20},{8,24},{12,28},{16,0},{20,4},{24,8},{28,12},{1,17},{... | collective-permute-start | bytes 344072 | tf_op jit(solution)/shard_map/ppermute | solution.py:140
  17.2 1.9 %copy-start = (bf16[32,64,768]{2,1,0:T(8,128)(2,1)S(1)}, bf16[32,64,768]{2,1,0:T(8,128)(2,1)}, u32[]{:S(2)}) copy-start(bf16[32,64,768]{2,1,0:T(8,128)(2,1)} %param.5) | copy-start | bytes 9437188
  19.1 1.9 %copy-start.1 = (bf16[32,64,768]{2,1,0:T(8,128)(2,1)S(1)}, bf16[32,64,768]{2,1,0:T(8,128)(2,1)}, u32[]{:S(2)}) copy-start(bf16[32,64,768]{2,1,0:T(8,128)(2,1)} %param.5) | copy-start | bytes 9437188
  21.0 2.6 %collective-permute-start.3 = (bf16[512,768]{1,0:T(8,128)(2,1)S(1)}, bf16[512,768]{1,0:T(8,128)(2,1)S(1)}, u32[]{:S(2)}, u32[]{:S(2)}) collective-permute-start(bf16[512,768]{1,0:T(8,128)(2,1)S(1)} %get-tuple-element.17), channel_id=1, source_target_pairs={{0,1},{1,0},{2,3},{3,2},{4,5},{5,4},{6,7},{7,6},{8,9},{9,8},{10,11... | collective-permute-start | bytes 2359304 | tf_op jit(solution)/shard_map/ppermute | solution.py:192
  24.7 29.9 %collective-permute-start.5 = (bf16[512,768]{1,0:T(8,128)(2,1)}, bf16[512,768]{1,0:T(8,128)(2,1)}, u32[]{:S(2)}, u32[]{:S(2)}) collective-permute-start(bf16[512,768]{1,0:T(8,128)(2,1)} %add_convert_fusion), channel_id=1, source_target_pairs={{0,2},{1,3},{2,0},{3,1},{4,6},{5,7},{6,4},{7,5},{8,10},{9,11},{10,... | collective-permute-start | bytes 2359304 | tf_op jit(solution)/shard_map/ppermute | solution.py:212
  31.1 23.5 %collective-permute-start.4 = (bf16[512,768]{1,0:T(8,128)(2,1)S(1)}, bf16[512,768]{1,0:T(8,128)(2,1)}, u32[]{:S(2)}, u32[]{:S(2)}) collective-permute-start(bf16[512,768]{1,0:T(8,128)(2,1)S(1)} %get-tuple-element.23), channel_id=1, source_target_pairs={{0,1},{1,0},{2,3},{3,2},{4,5},{5,4},{6,7},{7,6},{8,9},{9,8},{10,11... | collective-permute-start | bytes 2359304 | tf_op jit(solution)/shard_map/ppermute | solution.py:232
  47.6 1.4 %collective-permute-start.6 = (f32[1]{0:T(128)}, f32[1]{0:T(128)}, u32[]{:S(2)}, u32[]{:S(2)}) collective-permute-start(f32[1]{0:T(128)} %bitcast.15), channel_id=1, source_target_pairs={{0,1},{1,0},{2,3},{3,2},{4,5},{5,4},{6,7},{7,6},{8,9},{9,8},{10,11... | collective-permute-start | bytes 20 | tf_op jit(solution)/shard_map/ppermute | solution.py:240
  50.3 3.7 %collective-permute-start.7 = (f32[1]{0:T(128)}, f32[1]{0:T(128)}, u32[]{:S(2)}, u32[]{:S(2)}) collective-permute-start(f32[1]{0:T(128)} %add.41), channel_id=1, source_target_pairs={{0,2},{1,3},{2,0},{3,1},{4,6},{5,7},{6,4},{7,5},{8,10},{9,11},{10,... | collective-permute-start | bytes 20 | tf_op jit(solution)/shard_map/ppermute | solution.py:243

commit v2 on v0

v2 whole, which is shorter than its diff:
```python
import functools

import jax
import jax.numpy as jnp
from jax import lax
from jax.experimental import pallas as pl
from jax.experimental.pallas import tpu as pltpu
from jax.sharding import PartitionSpec as P

LANES = 128
F32, BF16 = jnp.float32, jnp.bfloat16
VMEM = pl.BlockSpec(memory_space=pltpu.VMEM)
HBM = pl.BlockSpec(memory_space=pltpu.HBM)
CHUNKS = 4


def flip(size, bit):
    return [(i, i ^ bit) for i in range(size)]


class Plan:
    def __init__(self, tiles_dev, tile, width, doc_count, label_count, doc_dev):
        self.tiles_dev, self.tile, self.width = tiles_dev, tile, width
        self.x_half = doc_count // 4
        self.group = tiles_dev // doc_count
        self.labels = self.x_half * self.group * tile
        self.block = doc_dev * label_count

    def local_tiles(self, half, core):
        column = lax.broadcasted_iota(jnp.int32, (1, self.labels), 1)
        slot = column // self.tile
        first = (half * self.x_half + slot // self.group) * 2 + core
        return first * self.group + slot % self.group

    def place(self):
        place = lax.axis_index("doc")
        return place // 2 // self.x_half, place % 2

    def order(self, half, core):
        return (1 - half, 1 - core), (1 - half, core), (half, 1 - core), (half, core)

    def rows(self, rows_ref, half, core):
        return rows_ref[half, :, core].reshape(self.labels, self.width)


def ready_kernel(plan, pos_ref, target_ref):
    owner = lax.axis_index("label")
    column = lax.broadcasted_iota(jnp.int32, (1, plan.labels), 1)
    for half in range(2):
        for core in range(2):
            local = plan.local_tiles(half, core)
            label_ids = (owner * plan.tiles_dev + local) * plan.tile + column % plan.tile
            hit = pos_ref[:, 0:1] == label_ids
            for k in range(1, pos_ref.shape[1]):
                hit = hit | (pos_ref[:, k : k + 1] == label_ids)
            target_ref[half, core] = hit.astype(F32).astype(BF16)


def listed_counts(plan, panel_ref):
    marks = panel_ref[:, plan.width :].astype(F32)
    flat = jnp.sum(marks.reshape(plan.block // 16, 16, LANES), axis=0)
    first = lax.axis_index("label") * plan.tiles_dev
    row_ids = lax.broadcasted_iota(jnp.int32, (16, LANES), 0)
    return jnp.where(row_ids == first // LANES, flat, 0.0).astype(BF16)


def set_weights(plan, mine, docs, rows, target, half, core):
    first = lax.axis_index("label") * plan.tiles_dev % LANES
    lane_ids = lax.broadcasted_iota(jnp.int32, (LANES, plan.labels), 0)
    spread = (lane_ids == first + plan.local_tiles(half, core)).astype(F32).astype(BF16)
    counts = jnp.sum(jnp.dot(mine, spread, preferred_element_type=F32), axis=0, keepdims=True)
    scores = lax.dot_general(docs, rows, (((1,), (1,)), ((), ())), preferred_element_type=F32)
    target = target.astype(F32)
    small = jnp.exp(-jnp.abs(scores))
    above = 1.0 + small
    share = 1.0 / above
    log_above = jnp.log(above) + (small - (above - 1.0)) * share
    losses = jnp.maximum(scores, 0.0) + log_above - target * scores
    losses = jnp.sum(losses, axis=0, keepdims=True) * counts
    lane_losses = losses[:, :LANES]
    for start in range(LANES, plan.labels, LANES):
        lane_losses = lane_losses + losses[:, start : start + LANES]
    sigmoid = jnp.where(scores >= 0.0, share, small * share)
    weight = ((sigmoid - target) * (counts * 0.125)).astype(BF16)
    return weight, lane_losses


def label_grad(weight, docs):
    return lax.dot_general(weight, docs, (((0,), (0,)), ((), ())), preferred_element_type=F32)


def first_kernel(plan, panel_ref, rows_ref, target_ref, grad_ref, weight_ref, loss_ref):
    half, core = plan.place()
    docs = panel_ref[:, : plan.width]
    mine = listed_counts(plan, panel_ref)
    losses = jnp.zeros((1, LANES), F32)
    for i, (h, c) in enumerate(plan.order(half, core)):
        weight, more = set_weights(
            plan, mine, docs, plan.rows(rows_ref, h, c), target_ref[h, c], h, c
        )
        weight_ref[i] = weight
        losses = losses + more
        if i == 0:
            grad_ref[...] = label_grad(weight, docs).astype(BF16)
    loss_ref[...] = losses


def second_kernel(plan, panel_ref, weight_ref, core_ref, near_ref, far_ref):
    grad = label_grad(weight_ref[1], panel_ref[:, : plan.width]) + core_ref[...].astype(F32)
    grad = grad.astype(BF16)
    near_ref[...] = grad[: plan.labels // 2]
    far_ref[...] = grad[plan.labels // 2 :]


def third_kernel(
    plan, panel_ref, rows_ref, weight_ref, loss_ref, grad_ref, kept_ref, send_ref
):
    half, core = plan.place()
    docs = panel_ref[:, : plan.width]
    part = jnp.zeros((plan.block, plan.width), F32)
    for i, (h, c) in enumerate(plan.order(half, core)):
        rows = plan.rows(rows_ref, h, c)
        part = part + jnp.dot(weight_ref[i], rows, preferred_element_type=F32)
    send_ref[:, : plan.width] = part.astype(BF16)
    loss = loss_ref[...]
    top = loss.astype(BF16).astype(F32)
    mid = (loss - top).astype(BF16).astype(F32)
    row = lax.broadcasted_iota(jnp.int32, (plan.block, LANES), 0) % 16
    terms = jnp.where(row == 0, top, jnp.where(row == 1, mid, jnp.where(row == 2, loss - top - mid, 0.0)))
    send_ref[:, plan.width :] = terms.astype(BF16)
    grad_ref[...] = label_grad(weight_ref[2], docs).astype(BF16)
    kept_ref[...] = label_grad(weight_ref[3], docs)


def sum_kernel(start, *refs):
    kept_ref, core_ref, x_ref = refs[:3]
    out_hbm, total_ref, sems = refs[-3:]
    count = x_ref.shape[0] // CHUNKS
    copies = []
    for i in range(CHUNKS):
        near, far = pl.ds(i * count, count), pl.ds(start + i * count, count)
        total_ref[near] = kept_ref[far] + core_ref[far].astype(F32) + x_ref[near].astype(F32)
        copy = pltpu.make_async_copy(total_ref.at[near], out_hbm.at[far], sems.at[i])
        copy.start()
        copies.append(copy)
    for copy in copies:
        copy.wait()


def doc_kernel(scale, parts_ref, doc_ref, loss_ref):
    total = jnp.sum(parts_ref[...].astype(F32), axis=0)
    width = doc_ref.shape[1]
    doc_ref[...] = total[:, :width].astype(BF16)
    loss_ref[...] = jnp.full(loss_ref.shape, jnp.sum(total[:, width:]) * scale, F32)


def per_device(doc_embed, classifier, shortlist, positives):
    label_count = lax.axis_size("label")
    doc_count = lax.axis_size("doc")
    tiles_dev, tile, width = classifier.shape
    doc_dev = doc_embed.shape[0]
    plan = Plan(tiles_dev, tile, width, doc_count, label_count, doc_dev)
    block, labels, x_half, group = plan.block, plan.labels, plan.x_half, plan.group
    listed = shortlist.size
    owner = lax.axis_index("label")
    place = lax.axis_index("doc")
    shape = jax.ShapeDtypeStruct
    params = pltpu.CompilerParams(vmem_limit_bytes=16 * 1024 * 1024)

    def cost(dots, scored):
        return pl.CostEstimate(
            flops=2 * block * labels * width * dots,
            bytes_accessed=2 * labels * width * dots,
            transcendentals=3 * block * labels * scored,
        )

    cells = lax.broadcasted_iota(jnp.int32, (16, LANES, listed), 0) * LANES
    cells = cells + lax.broadcasted_iota(jnp.int32, (16, LANES, listed), 1)
    marks = jnp.any(cells == shortlist.reshape(1, 1, listed), axis=2).astype(BF16)
    panel = lax.optimization_barrier(jnp.concatenate([doc_embed, marks], axis=1))
    bit = 1
    while bit < label_count:
        other = lax.ppermute(panel, "label", flip(label_count, bit))
        upper = owner // bit % 2 == 1
        panel = jnp.where(
            upper, jnp.concatenate([other, panel], 0), jnp.concatenate([panel, other], 0)
        )
        if bit == 1:
            early = jnp.abs(panel[0:1, :width]) < jnp.inf
            flat = jnp.where(early, classifier.reshape(-1, width), 0)
        bit *= 2

    rows = flat.reshape(2, x_half, 2, group * tile, width)
    target = pl.pallas_call(
        functools.partial(ready_kernel, plan),
        in_specs=[VMEM],
        out_specs=VMEM,
        out_shape=shape((2, 2, block, labels), BF16),
        compiler_params=params,
        cost_estimate=cost(2, 0),
    )(positives)

    grad_shape = (labels, width)
    grad_a, weights, loss = pl.pallas_call(
        functools.partial(first_kernel, plan),
        in_specs=[VMEM] * 3,
        out_specs=[VMEM] * 3,
        out_shape=[shape(grad_shape, BF16), shape((4, block, labels), BF16), shape((1, LANES), F32)],
        compiler_params=params,
        cost_estimate=cost(5, 4),
    )(panel, rows, target)
    step = doc_count // 2
    from_core_a = lax.ppermute(grad_a, "doc", flip(doc_count, 1))
    half_rows = labels // 2
    grad_c, kept, send = pl.pallas_call(
        functools.partial(third_kernel, plan),
        in_specs=[VMEM] * 4,
        out_specs=[VMEM] * 3,
        out_shape=[
            shape(grad_shape, BF16), shape(grad_shape, F32), shape((block, width + LANES), BF16)
        ],
        compiler_params=params,
        cost_estimate=cost(6, 0),
    )(panel, rows, weights, loss)
    from_core_c = lax.ppermute(grad_c, "doc", flip(doc_count, 1))
    weights, kept, send = lax.optimization_barrier((weights, kept, send))
    to_x = pl.pallas_call(
        functools.partial(second_kernel, plan),
        in_specs=[VMEM] * 3,
        out_specs=[VMEM] * 2,
        out_shape=[shape((half_rows, width), BF16)] * 2,
        compiler_params=params,
        cost_estimate=cost(1, 0),
    )(panel, weights, from_core_a)
    from_x = [lax.ppermute(half, "doc", flip(doc_count, step)) for half in to_x]
    entry_total = block * doc_count * label_count * listed * tile

    def exchange(send):
        send = send.reshape(label_count, doc_dev, width + LANES)
        parts = lax.all_to_all(send, "label", split_axis=0, concat_axis=0, tiled=True)
        doc_grad, loss = pl.pallas_call(
            functools.partial(doc_kernel, 1.0 / entry_total),
            in_specs=[VMEM],
            out_specs=[VMEM, VMEM],
            out_shape=[shape((doc_dev, width), BF16), shape((1, LANES), F32)],
            compiler_params=params,
        )(parts)
        return doc_grad, loss

    def nothing(send):
        return jnp.zeros((doc_dev, width), BF16), jnp.zeros((1, LANES), F32)

    send, *to_x = lax.optimization_barrier((send, *to_x))
    doc_grad, loss = lax.cond(shortlist[0, 0, 0] >= 0, exchange, nothing, send)
    bit = 1
    while bit < doc_count:
        loss = loss + lax.ppermute(loss, "doc", flip(doc_count, bit))
        bit *= 2
    mean_loss = loss[0, 0]

    class_grad = []
    for i in range(2):
        class_grad = [
            pl.pallas_call(
                functools.partial(sum_kernel, i * half_rows),
                in_specs=[VMEM] * 3 + [HBM] * i,
                out_specs=HBM,
                out_shape=shape(grad_shape, F32),
                scratch_shapes=[
                    pltpu.VMEM((half_rows, width), F32), pltpu.SemaphoreType.DMA((CHUNKS,))
                ],
                input_output_aliases={3: 0} if i else {},
                compiler_params=params,
                cost_estimate=cost(1, 0),
            )(kept, from_core_c, from_x[i], *class_grad)
        ]
    class_grad = class_grad[0].reshape(x_half, group * tile, width)
    step = x_half // 2
    while step >= 1:
        pairs = class_grad.reshape(2, step, group * tile, width)
        mine = place // 2 // step % 2
        away = lax.dynamic_index_in_dim(pairs, 1 - mine, 0, keepdims=False)
        stay = lax.dynamic_index_in_dim(pairs, mine, 0, keepdims=False)
        got = lax.ppermute(away.astype(BF16), "doc", flip(doc_count, 2 * step))
        class_grad = stay + got.astype(F32)
        step //= 2
    return doc_grad, class_grad.reshape(group, tile, width), mean_loss


def solution(mesh):
    placed = (
        P(("doc", "label"), None),
        P("label", None, None),
        P("doc", "label", None),
        P("doc", None),
    )
    return jax.shard_map(
        per_device,
        mesh=mesh,
        in_specs=placed,
        out_specs=(P(("doc", "label"), None), P(("label", "doc"), None, None), P()),
        check_vma=False,
    )
```

time: 178 us -> 48.4 us (0.27)
  blocking collectives: 71.3 us -> 14.4 us
  waiting for transfers between devices: 29.8 us -> 6.5 us
  matrix products: 23.2 us -> 0 us
  local copies, waits for them, and re-layouts: 23.4 us -> 0.79 us
  between operations: 15.9 us -> 0.77 us
  Pallas kernels: 0 us -> 8.88 us
  starting transfers between devices: 7.36 us -> 12.4 us
  loops' own time: 2.64 us -> 0.02 us
    psum x1 -> x0, blocking collectives: 40 us -> none  [per_device(): loss_all = lax.psum(loss_sum, ('label', 'doc'))]
    all_gather x1 -> x0, blocking collectives: 31.3 us -> none  [per_device(): doc_panel = lax.all_gather(doc_embed, 'label', axis=0, tiled=True)]
    unnamed x3 -> x0, waiting for transfers between devices: 29.8 us -> none
    dot_general x7 -> x0, matrix products: 23.2 us -> none  [the longest x4 10.7 us: group_one(): lax.dot_general(row_part, doc_panel, (((0,), (0,)), ((), ())), preferred_...]
    all_to_all x0 -> x1, blocking collectives: none -> 14.4 us  [exchange(): lax.all_to_all(send, 'label', split_axis=0, concat_axis=0, tiled=True)]
    ppermute x0 -> x9, starting transfers between devices: none -> 12.4 us  [the longest x3 7.53 us: per_device(): other = lax.ppermute(panel, 'label', flip(label_count, bit))]
    another operation x1 -> x0, local copies, waits for them, and re-layouts: 8.96 us -> none  [accumulate(): tile_grads.reshape(slot_total, tile_grads.shape[1] * tile_grads.shape[2])]
    pallas_call x0 -> x7, Pallas kernels: none -> 8.88 us  [the longest x1 2.1 us: per_device(): pl.pallas_call(functools.partial(first_kernel, plan), in_specs=[VMEM] * 3...]
  transfers between devices with their start and end apart: 3 -> 9, of which waited for: 1 -> 4; matrix products, arithmetic and copies ran while one was open for 17% -> 7% of each run, Pallas kernels for 0% -> 12%
where the time goes in v2:
time: 48.4 us; the launch traced here: 48.1 us
  blocking collectives  14.4 us (30%)
  starting transfers between devices  12.4 us (26%)
  Pallas kernels  8.88 us (18%)
  waiting for transfers between devices  6.5 us (13%)
  other arithmetic  4.26 us (9%)
  local copies, waits for them, and re-layouts  0.79 us (2%)
  between operations  0.77 us (2%)
    all_to_all x1, blocking collectives, exchange(): lax.all_to_all(send, 'label', split_axis=0, concat_axis=0, tiled=True)  14.4 us
    ppermute x3, starting transfers between devices, per_device(): other = lax.ppermute(panel, 'label', flip(label_count, bit))  7.53 us
    ppermute x3, waiting for transfers between devices, per_device(): other = lax.ppermute(panel, 'label', flip(label_count, bit))  3.32 us
    ppermute x2, waiting for transfers between devices, per_device(): loss = loss + lax.ppermute(loss, 'doc', flip(doc_count, bit))  3.16 us
    ppermute x2, starting transfers between devices, per_device(): from_x = [lax.ppermute(half, 'doc', flip(doc_count, step)) for half in to_x]  2.87 us
    select_n x1, other arithmetic, per_device(): flat = jnp.where(early, classifier.reshape(-1, width), 0)  2.1 us
    pallas_call x1, Pallas kernels, per_device(): pl.pallas_call(functools.partial(first_kernel, plan), in_specs=[VMEM] * 3...  2.1 us
    pallas_call x2, Pallas kernels, per_device(): pl.pallas_call(functools.partial(sum_kernel, i * half_rows), in_specs=[VM...  1.87 us
  transfers between devices with their start and end apart: 9, of which 4 were waited for; matrix products, arithmetic and copies ran while one was open for 7% of the time, Pallas kernels for 12%

profile of v2, /device:TPU:0, one launch (start us, length us, event | category | flops | bytes accessed | tf_op | source)
XLA Modules:
  0.0 48.1 jit_solution(8010882693489684444)
XLA Ops:
  0.6 0.8 %fusion = pred[16,128]{1,0:T(8,128)(4,1)S(1)} fusion(s32[32]{0:T(128)} %bitcast.11, s32[16]{0:T(128)S(1)} %iota_multiply_fusion), kind=kLoop, calls=%fused_computation.2 | loop fusion | flops 194560 | bytes 2240 | tf_op jit(solution)/shard_map/reduce_or | solution.py:179
  1.4 0.7 %pad_maximum_fusion = bf16[16,896]{1,0:T(8,128)(2,1)S(1)} fusion(bf16[16,128]{1,0:T(8,128)(2,1)S(1)} %convert_element_type.13, bf16[16,768]{1,0:T(8,128)(2,1)} %param.6), kind=kLoop, calls=%fused_computation.6 | loop fusion | flops 57344 | bytes 57344 | tf_op jit(solution)/shard_map/concatenate | solution.py:180
  2.2 3.0 %collective-permute-start = (bf16[16,896]{1,0:T(8,128)(2,1)S(1)}, bf16[16,896]{1,0:T(8,128)(2,1)S(1)}, u32[]{:S(2)}, u32[]{:S(2)}) collective-permute-start(bf16[16,896]{1,0:T(8,128)(2,1)S(1)} %pad_maximum_fusion), channel_id=1, source_target_pairs={{0,4},{4,0},{8,12},{12,8},{16,20},{20,16},{24,28},{28,24},{1,5},{5... | collective-permute-start | bytes 86024 | tf_op jit(solution)/shard_map/ppermute | solution.py:183
  5.2 0.8 %copy.9.pos_ref = s32[128,8]{1,0:T(8,128)S(1)} copy(s32[128,8]{0,1:T(8,128)} %param.9) | data formatting | bytes 8192 | tf_op args[3]
  5.9 1.4 %shard_map.67.target_ref = bf16[2,2,128,512]{3,2,1,0:T(8,128)(2,1)S(1)} custom-call(s32[128,8]{1,0:T(8,128)S(1)} %copy.9.pos_ref), custom_call_target="tpu_custom_call" | custom-call | flops 201326592 | bytes 1572864 | tf_op jit(solution)/shard_map/pallas_call | solution.py:194
  7.4 1.8 %collective-permute-start.1 = (bf16[32,896]{1,0:T(8,128)(2,1)S(1)}, bf16[32,896]{1,0:T(8,128)(2,1)S(1)}, u32[]{:S(2)}, u32[]{:S(2)}) collective-permute-start(bf16[32,896]{1,0:T(8,128)(2,1)S(1)} %maximum_select_fusion.2), channel_id=1, source_target_pairs={{0,8},{4,12},{8,0},{12,4},{16,24},{20,28},{24,16},{28,20},{1,9},{5... | collective-permute-start | bytes 172040 | tf_op jit(solution)/shard_map/ppermute | solution.py:183
  9.2 2.4 %collective-permute-done.1 = bf16[32,896]{1,0:T(8,128)(2,1)S(1)} collective-permute-done((bf16[32,896]{1,0:T(8,128)(2,1)S(1)}, bf16[32,896]{1,0:T(8,128)(2,1)S(1)}, u32[]{:S(2)}, u32[]{:S(2)}) %collective-permute-start.1) | collective-permute-done | bytes 57376 | tf_op jit(solution)/shard_map/ppermute | solution.py:183
  11.7 2.8 %collective-permute-start.2 = (bf16[64,896]{1,0:T(8,128)(2,1)S(1)}, bf16[64,896]{1,0:T(8,128)(2,1)S(1)}, u32[]{:S(2)}, u32[]{:S(2)}) collective-permute-start(bf16[64,896]{1,0:T(8,128)(2,1)S(1)} %maximum_select_fusion.1), channel_id=1, source_target_pairs={{0,16},{4,20},{8,24},{12,28},{16,0},{20,4},{24,8},{28,12},{1,17},{... | collective-permute-start | bytes 344072 | tf_op jit(solution)/shard_map/ppermute | solution.py:183
  14.4 2.1 %broadcast_select_fusion.rows_ref = bf16[2,1,2,512,768]{4,3,2,1,0:T(8,128)(2,1)S(1)} fusion(bf16[2,1,2,512,768]{4,3,2,1,0:T(8,128)(2,1)} %bitcast.9, pred[768]{0:T(1024)(128)(4,1)S(1)} %compare_reduce_fusion), kind=kLoop, calls=%fused_computation | loop fusion | flops 1572864 | bytes 6292224 | tf_op jit(solution)/shard_map/jit(_where)/select_n | solution.py:190
  16.5 0.9 %collective-permute-done.2 = bf16[64,896]{1,0:T(8,128)(2,1)S(1)} collective-permute-done((bf16[64,896]{1,0:T(8,128)(2,1)S(1)}, bf16[64,896]{1,0:T(8,128)(2,1)S(1)}, u32[]{:S(2)}, u32[]{:S(2)}) %collective-permute-start.2) | collective-permute-done | bytes 114720 | tf_op jit(solution)/shard_map/ppermute | solution.py:183
  17.5 2.1 %shard_map.68 = (bf16[512,768]{1,0:T(8,128)(2,1)S(1)}, bf16[4,128,512]{2,1,0:T(8,128)(2,1)S(1)}, f32[1,128]{1,0:T(1,128)S(1)}) custom-call(bf16[128,896]{1,0:T(8,128)(2,1)S(1)} %maximum_select_fusion.panel_ref, bf16[2,1,2,512,768]{4,3,2,1,0:T(8,128)(2,1)S(1)} %broadcast_select_fusion.rows_ref, bf16[2,2,128,512]{3,2,1,0:T(8,128)(2,1)S(1)} %shard_map.67.target_ref), custom_call_target="tpu_custom_call" | custom-call | flops 503316480 | bytes 3932160 | tf_op jit(solution)/shard_map/pallas_call | solution.py:204
  19.7 1.8 %shard_map.69 = (bf16[512,768]{1,0:T(8,128)(2,1)}, f32[512,768]{1,0:T(8,128)S(1)}, bf16[128,896]{1,0:T(8,128)(2,1)}) custom-call(bf16[128,896]{1,0:T(8,128)(2,1)S(1)} %maximum_select_fusion.panel_ref, bf16[2,1,2,512,768]{4,3,2,1,0:T(8,128)(2,1)S(1)} %broadcast_select_fusion.rows_ref, bf16[4,128,512]{2,1,0:T(8,128)(2,1)S(1)} %get-tuple-element.23.weight_ref, ...), custom_call_target="tpu_custom_call" | custom-call | flops 603979776 | bytes 4718592 | tf_op jit(solution)/shard_map/pallas_call | solution.py:215
  21.5 0.5 collective-permute-start.4
  22.0 1.1 %shard_map.70 = (bf16[256,768]{1,0:T(8,128)(2,1)}, bf16[256,768]{1,0:T(8,128)(2,1)S(1)}) custom-call(bf16[128,896]{1,0:T(8,128)(2,1)S(1)} %maximum_select_fusion.panel_ref, bf16[4,128,512]{2,1,0:T(8,128)(2,1)S(1)} %get-tuple-element.23.weight_ref, bf16[512,768]{1,0:T(8,128)(2,1)S(1)} %collective-permute-done.3.core_ref), custom_call_target="tpu_custom_call" | custom-call | flops 100663296 | bytes 786432 | tf_op jit(solution)/shard_map/pallas_call | solution.py:227
  23.0 2.8 %collective-permute-start.6 = (bf16[256,768]{1,0:T(8,128)(2,1)}, bf16[256,768]{1,0:T(8,128)(2,1)S(1)}, u32[]{:S(2)}, u32[]{:S(2)}) collective-permute-start(bf16[256,768]{1,0:T(8,128)(2,1)} %get-tuple-element.25), channel_id=1, source_target_pairs={{0,2},{1,3},{2,0},{3,1},{4,6},{5,7},{6,4},{7,5},{8,10},{9,11},{10,... | collective-permute-start | bytes 1179656 | tf_op jit(solution)/shard_map/ppermute | solution.py:235
  25.9 15.0 %conditional.1 = ((bf16[16,768]{1,0:T(8,128)(2,1)}, f32[1,128]{1,0:T(1,128)S(1)})) conditional(s32[]{:T(128)} %bitcast.1, () %tuple.17, bf16[128,896]{1,0:T(8,128)(2,1)} %get-tuple-element.27), branch_computations={%region_1.2_spmd, %region_2.3_spmd} | conditional | bytes 458760 | solution.py:254
  25.9 14.4 %all_to_all.4.parts_ref = bf16[8,16,896]{2,1,0:T(8,128)(2,1)S(1)} all-to-all(bf16[8,16,896]{2,1,0:T(8,128)(2,1)} %bitcast.10), channel_id=1, replica_groups=mesh['label'=8,'doc'=4] {'label'}, dimensions={0} | all-to-all | bytes 458752 | tf_op jit(solution)/shard_map/cond/branch_1_fun/all_to_all | solution.py:240
  40.3 0.6 %branch_1_fun.1 = (bf16[16,768]{1,0:T(8,128)(2,1)}, f32[1,128]{1,0:T(1,128)S(1)}) custom-call(bf16[8,16,896]{2,1,0:T(8,128)(2,1)S(1)} %all_to_all.4.parts_ref), custom_call_target="tpu_custom_call" | custom-call | tf_op jit(solution)/shard_map/cond/branch_1_fun/pallas_call | solution.py:241
  41.0 1.1 %collective-permute-done.7 = f32[1,128]{1,0:T(1,128)S(1)} collective-permute-done((f32[1,128]{1,0:T(1,128)S(1)}, f32[1,128]{1,0:T(1,128)S(1)}, u32[]{:S(2)}, u32[]{:S(2)}) %collective-permute-start.7) | collective-permute-done | bytes 544 | tf_op jit(solution)/shard_map/ppermute | solution.py:257
  42.1 1.5 %collective-permute-start.8 = (f32[1,128]{1,0:T(1,128)S(1)}, f32[1,128]{1,0:T(1,128)S(1)}, u32[]{:S(2)}, u32[]{:S(2)}) collective-permute-start(f32[1,128]{1,0:T(1,128)S(1)} %add.26), channel_id=1, source_target_pairs={{0,2},{1,3},{2,0},{3,1},{4,6},{5,7},{6,4},{7,5},{8,10},{9,11},{10,... | collective-permute-start | bytes 1544 | tf_op jit(solution)/shard_map/ppermute | solution.py:257
  43.6 2.0 %collective-permute-done.8 = f32[1,128]{1,0:T(1,128)S(1)} collective-permute-done((f32[1,128]{1,0:T(1,128)S(1)}, f32[1,128]{1,0:T(1,128)S(1)}, u32[]{:S(2)}, u32[]{:S(2)}) %collective-permute-start.8) | collective-permute-done | bytes 544 | tf_op jit(solution)/shard_map/ppermute | solution.py:257
  45.6 0.5 %add.27 = f32[1,128]{1,0:T(1,128)} add(f32[1,128]{1,0:T(1,128)S(1)} %add.26, f32[1,128]{1,0:T(1,128)S(1)} %collective-permute-done.8) | non-fusion elementwise | flops 128 | bytes 1536 | tf_op jit(solution)/shard_map/add | solution.py:257
  46.2 0.9 %shard_map.71.refs_3_ = f32[512,768]{1,0:T(8,128)} custom-call(f32[512,768]{1,0:T(8,128)S(1)} %get-tuple-element.29.refs_0_, bf16[512,768]{1,0:T(8,128)(2,1)S(1)} %collective-permute-done.4.refs_1_, bf16[256,768]{1,0:T(8,128)(2,1)S(1)} %collective-permute-done.6.refs_2_), custom_call_target="tpu_custom_call" | custom-call | flops 100663296 | bytes 786432 | tf_op jit(solution)/shard_map/pallas_call | solution.py:264
  47.1 0.9 %shard_map.72 = f32[512,768]{1,0:T(8,128)} custom-call(f32[512,768]{1,0:T(8,128)S(1)} %get-tuple-element.29.refs_0_, bf16[512,768]{1,0:T(8,128)(2,1)S(1)} %collective-permute-done.4.refs_1_, bf16[256,768]{1,0:T(8,128)(2,1)S(1)} %collective-permute-done.5.refs_2_, f32[512,768]{1,0:T(8,128)} %shard_map.71.refs_3_), custom_call_target="tpu_custom_call", output_to_operand_aliasing={{}: (3, {})} | custom-call | flops 100663296 | bytes 786432 | tf_op jit(solution)/shard_map/pallas_call | solution.py:264
  (17 shorter events, 0.2 us)
Async XLA Ops:
  2.2 5.2 %collective-permute-start = (bf16[16,896]{1,0:T(8,128)(2,1)S(1)}, bf16[16,896]{1,0:T(8,128)(2,1)S(1)}, u32[]{:S(2)}, u32[]{:S(2)}) collective-permute-start(bf16[16,896]{1,0:T(8,128)(2,1)S(1)} %pad_maximum_fusion), channel_id=1, source_target_pairs={{0,4},{4,0},{8,12},{12,8},{16,20},{20,16},{24,28},{28,24},{1,5},{5... | collective-permute-start | bytes 86024 | tf_op jit(solution)/shard_map/ppermute | solution.py:183
  7.4 4.2 %collective-permute-start.1 = (bf16[32,896]{1,0:T(8,128)(2,1)S(1)}, bf16[32,896]{1,0:T(8,128)(2,1)S(1)}, u32[]{:S(2)}, u32[]{:S(2)}) collective-permute-start(bf16[32,896]{1,0:T(8,128)(2,1)S(1)} %maximum_select_fusion.2), channel_id=1, source_target_pairs={{0,8},{4,12},{8,0},{12,4},{16,24},{20,28},{24,16},{28,20},{1,9},{5... | collective-permute-start | bytes 172040 | tf_op jit(solution)/shard_map/ppermute | solution.py:183
  11.7 5.8 %collective-permute-start.2 = (bf16[64,896]{1,0:T(8,128)(2,1)S(1)}, bf16[64,896]{1,0:T(8,128)(2,1)S(1)}, u32[]{:S(2)}, u32[]{:S(2)}) collective-permute-start(bf16[64,896]{1,0:T(8,128)(2,1)S(1)} %maximum_select_fusion.1), channel_id=1, source_target_pairs={{0,16},{4,20},{8,24},{12,28},{16,0},{20,4},{24,8},{28,12},{1,17},{... | collective-permute-start | bytes 344072 | tf_op jit(solution)/shard_map/ppermute | solution.py:183
  19.6 6.3 %copy-start = (s32[1,1,32]{2,1,0:T(1,128)S(1)}, s32[1,1,32]{2,1,0:T(1,128)}, u32[]{:S(2)}) copy-start(s32[1,1,32]{2,1,0:T(1,128)} %param.8) | copy-start | bytes 388
  19.6 2.4 %collective-permute-start.3 = (bf16[512,768]{1,0:T(8,128)(2,1)S(1)}, bf16[512,768]{1,0:T(8,128)(2,1)S(1)}, u32[]{:S(2)}, u32[]{:S(2)}) collective-permute-start(bf16[512,768]{1,0:T(8,128)(2,1)S(1)} %get-tuple-element.24), channel_id=1, source_target_pairs={{0,1},{1,0},{2,3},{3,2},{4,5},{5,4},{6,7},{7,6},{8,9},{9,8},{10,11... | collective-permute-start | bytes 2359304 | tf_op jit(solution)/shard_map/ppermute | solution.py:213
  21.5 24.7 %collective-permute-start.4 = (bf16[512,768]{1,0:T(8,128)(2,1)}, bf16[512,768]{1,0:T(8,128)(2,1)S(1)}, u32[]{:S(2)}, u32[]{:S(2)}) collective-permute-start(bf16[512,768]{1,0:T(8,128)(2,1)} %get-tuple-element.30), channel_id=1, source_target_pairs={{0,1},{1,0},{2,3},{3,2},{4,5},{5,4},{6,7},{7,6},{8,9},{9,8},{10,11... | collective-permute-start | bytes 2359304 | tf_op jit(solution)/shard_map/ppermute | solution.py:225
  23.0 23.1 %collective-permute-start.6 = (bf16[256,768]{1,0:T(8,128)(2,1)}, bf16[256,768]{1,0:T(8,128)(2,1)S(1)}, u32[]{:S(2)}, u32[]{:S(2)}) collective-permute-start(bf16[256,768]{1,0:T(8,128)(2,1)} %get-tuple-element.25), channel_id=1, source_target_pairs={{0,2},{1,3},{2,0},{3,1},{4,6},{5,7},{6,4},{7,5},{8,10},{9,11},{10,... | collective-permute-start | bytes 1179656 | tf_op jit(solution)/shard_map/ppermute | solution.py:235
  25.9 21.3 %collective-permute-start.5 = (bf16[256,768]{1,0:T(8,128)(2,1)S(1)}, bf16[256,768]{1,0:T(8,128)(2,1)S(1)}, u32[]{:S(2)}, u32[]{:S(2)}) collective-permute-start(bf16[256,768]{1,0:T(8,128)(2,1)S(1)} %get-tuple-element.26), channel_id=1, source_target_pairs={{0,2},{1,3},{2,0},{3,1},{4,6},{5,7},{6,4},{7,5},{8,10},{9,11},{10,... | collective-permute-start | bytes 1179656 | tf_op jit(solution)/shard_map/ppermute | solution.py:235
  41.0 1.1 %collective-permute-start.7 = (f32[1,128]{1,0:T(1,128)S(1)}, f32[1,128]{1,0:T(1,128)S(1)}, u32[]{:S(2)}, u32[]{:S(2)}) collective-permute-start(f32[1,128]{1,0:T(1,128)S(1)} %get-tuple-element.31), channel_id=1, source_target_pairs={{0,1},{1,0},{2,3},{3,2},{4,5},{5,4},{6,7},{7,6},{8,9},{9,8},{10,11... | collective-permute-start | bytes 1544 | tf_op jit(solution)/shard_map/ppermute | solution.py:257
  42.1 3.5 %collective-permute-start.8 = (f32[1,128]{1,0:T(1,128)S(1)}, f32[1,128]{1,0:T(1,128)S(1)}, u32[]{:S(2)}, u32[]{:S(2)}) collective-permute-start(f32[1,128]{1,0:T(1,128)S(1)} %add.26), channel_id=1, source_target_pairs={{0,2},{1,3},{2,0},{3,1},{4,6},{5,7},{6,4},{7,5},{8,10},{9,11},{10,... | collective-permute-start | bytes 1544 | tf_op jit(solution)/shard_map/ppermute | solution.py:257

commit v3 on v2

--- a/solution.py
+++ b/solution.py
@@ -11,7 +11,9 @@
 F32, BF16 = jnp.float32, jnp.bfloat16
 VMEM = pl.BlockSpec(memory_space=pltpu.VMEM)
 HBM = pl.BlockSpec(memory_space=pltpu.HBM)
+ANY = pl.BlockSpec(memory_space=pl.ANY)
 CHUNKS = 4
+EXTRA = 16
 
 
 def flip(size, bit):
@@ -89,6 +91,14 @@
     return lax.dot_general(weight, docs, (((0,), (0,)), ((), ())), preferred_element_type=F32)
 
 
+def split_rows(value, count):
+    top = value.astype(BF16).astype(F32)
+    mid = (value - top).astype(BF16).astype(F32)
+    row = lax.broadcasted_iota(jnp.int32, (count, value.shape[1]), 0) % 16
+    low = jnp.where(row == 2, value - top - mid, 0.0)
+    return jnp.where(row == 0, top, jnp.where(row == 1, mid, low)).astype(BF16)
+
+
 def first_kernel(plan, panel_ref, rows_ref, target_ref, grad_ref, weight_ref, loss_ref):
     half, core = plan.place()
     docs = panel_ref[:, : plan.width]
@@ -101,19 +111,30 @@
         weight_ref[i] = weight
         losses = losses + more
         if i == 0:
-            grad_ref[...] = label_grad(weight, docs).astype(BF16)
+            grad_ref[: plan.labels] = label_grad(weight, docs).astype(BF16)
     loss_ref[...] = losses
-
-
-def second_kernel(plan, panel_ref, weight_ref, core_ref, near_ref, far_ref):
-    grad = label_grad(weight_ref[1], panel_ref[:, : plan.width]) + core_ref[...].astype(F32)
-    grad = grad.astype(BF16)
-    near_ref[...] = grad[: plan.labels // 2]
-    far_ref[...] = grad[plan.labels // 2 :]
+    grad_ref[plan.labels :, :LANES] = split_rows(losses, EXTRA)
+    grad_ref[plan.labels :, LANES:] = jnp.zeros((EXTRA, plan.width - LANES), BF16)
+
+
+def second_kernel(
+    plan, panel_ref, weight_ref, core_ref, loss_ref, send_in, near_ref, far_ref, send_ref, terms, sem
+):
+    theirs = core_ref[plan.labels :, :LANES].astype(F32)
+    losses = loss_ref[...] + jnp.sum(theirs, axis=0, keepdims=True)
+    terms[...] = split_rows(losses, plan.block)
+    copy = pltpu.make_async_copy(terms, send_ref.at[:, pl.ds(plan.width, LANES)], sem)
+    copy.start()
+    grad = label_grad(weight_ref[1], panel_ref[:, : plan.width])
+    grad = (grad + core_ref[: plan.labels].astype(F32)).astype(BF16)
+    near = near_ref.shape[0]
+    near_ref[...] = grad[:near]
+    far_ref[...] = grad[near:]
+    copy.wait()
 
 
 def third_kernel(
-    plan, panel_ref, rows_ref, weight_ref, loss_ref, grad_ref, kept_ref, send_ref
+    plan, panel_ref, rows_ref, weight_ref, grad_ref, kept_ref, send_ref
 ):
     half, core = plan.place()
     docs = panel_ref[:, : plan.width]
@@ -122,19 +143,12 @@
         rows = plan.rows(rows_ref, h, c)
         part = part + jnp.dot(weight_ref[i], rows, preferred_element_type=F32)
     send_ref[:, : plan.width] = part.astype(BF16)
-    loss = loss_ref[...]
-    top = loss.astype(BF16).astype(F32)
-    mid = (loss - top).astype(BF16).astype(F32)
-    row = lax.broadcasted_iota(jnp.int32, (plan.block, LANES), 0) % 16
-    terms = jnp.where(row == 0, top, jnp.where(row == 1, mid, jnp.where(row == 2, loss - top - mid, 0.0)))
-    send_ref[:, plan.width :] = terms.astype(BF16)
+    send_ref[:, plan.width :] = jnp.zeros((plan.block, LANES), BF16)
     grad_ref[...] = label_grad(weight_ref[2], docs).astype(BF16)
     kept_ref[...] = label_grad(weight_ref[3], docs)
 
 
-def sum_kernel(start, *refs):
-    kept_ref, core_ref, x_ref = refs[:3]
-    out_hbm, total_ref, sems = refs[-3:]
+def add_rows(start, kept_ref, core_ref, x_ref, out_hbm, total_ref, sems):
     count = x_ref.shape[0] // CHUNKS
     copies = []
     for i in range(CHUNKS):
@@ -143,8 +157,24 @@
         copy = pltpu.make_async_copy(total_ref.at[near], out_hbm.at[far], sems.at[i])
         copy.start()
         copies.append(copy)
-    for copy in copies:
+    return copies
+
+
+def near_kernel(kept_ref, core_ref, x_ref, out_hbm, total_ref, sems):
+    for copy in add_rows(0, kept_ref, core_ref, x_ref, out_hbm, total_ref, sems):
         copy.wait()
+
+
+def far_kernel(
+    start, kept_ref, core_ref, x_ref, loss_ref, other_ref, out_in, out_hbm, mean_hbm, total_ref, sems,
+    mean_ref, mean_sem,
+):
+    mean_ref[...] = loss_ref[:, :1] + other_ref[:, :1]
+    mean_copy = pltpu.make_async_copy(mean_ref, mean_hbm, mean_sem)
+    mean_copy.start()
+    for copy in add_rows(start, kept_ref, core_ref, x_ref, out_hbm, total_ref, sems):
+        copy.wait()
+    mean_copy.wait()
 
 
 def doc_kernel(scale, parts_ref, doc_ref, loss_ref):
@@ -165,7 +195,7 @@
     owner = lax.axis_index("label")
     place = lax.axis_index("doc")
     shape = jax.ShapeDtypeStruct
-    params = pltpu.CompilerParams(vmem_limit_bytes=16 * 1024 * 1024)
+    params = pltpu.CompilerParams(vmem_limit_bytes=8 * 1024 * 1024)
 
     def cost(dots, scored):
         return pl.CostEstimate(
@@ -205,33 +235,39 @@
         functools.partial(first_kernel, plan),
         in_specs=[VMEM] * 3,
         out_specs=[VMEM] * 3,
-        out_shape=[shape(grad_shape, BF16), shape((4, block, labels), BF16), shape((1, LANES), F32)],
+        out_shape=[
+            shape((labels + EXTRA, width), BF16), shape((4, block, labels), BF16), shape((1, LANES), F32)
+        ],
         compiler_params=params,
         cost_estimate=cost(5, 4),
     )(panel, rows, target)
     step = doc_count // 2
     from_core_a = lax.ppermute(grad_a, "doc", flip(doc_count, 1))
-    half_rows = labels // 2
+    near = labels * 3 // 4
     grad_c, kept, send = pl.pallas_call(
         functools.partial(third_kernel, plan),
-        in_specs=[VMEM] * 4,
+        in_specs=[VMEM] * 3,
         out_specs=[VMEM] * 3,
         out_shape=[
             shape(grad_shape, BF16), shape(grad_shape, F32), shape((block, width + LANES), BF16)
         ],
         compiler_params=params,
         cost_estimate=cost(6, 0),
-    )(panel, rows, weights, loss)
+    )(panel, rows, weights)
     from_core_c = lax.ppermute(grad_c, "doc", flip(doc_count, 1))
     weights, kept, send = lax.optimization_barrier((weights, kept, send))
-    to_x = pl.pallas_call(
+    *to_x, send = pl.pallas_call(
         functools.partial(second_kernel, plan),
-        in_specs=[VMEM] * 3,
-        out_specs=[VMEM] * 2,
-        out_shape=[shape((half_rows, width), BF16)] * 2,
+        in_specs=[VMEM] * 4 + [ANY],
+        out_specs=[VMEM] * 2 + [ANY],
+        out_shape=[
+            shape((near, width), BF16), shape((labels - near, width), BF16), shape(send.shape, BF16)
+        ],
+        scratch_shapes=[pltpu.VMEM((block, LANES), BF16), pltpu.SemaphoreType.DMA(())],
+        input_output_aliases={4: 2},
         compiler_params=params,
         cost_estimate=cost(1, 0),
-    )(panel, weights, from_core_a)
+    )(panel, weights, from_core_a, loss, send)
     from_x = [lax.ppermute(half, "doc", flip(doc_count, step)) for half in to_x]
     entry_total = block * doc_count * label_count * listed * tile
 
@@ -252,29 +288,37 @@
 
     send, *to_x = lax.optimization_barrier((send, *to_x))
     doc_grad, loss = lax.cond(shortlist[0, 0, 0] >= 0, exchange, nothing, send)
-    bit = 1
+    bit, other = 2, jnp.zeros((1, LANES), F32)
     while bit < doc_count:
-        loss = loss + lax.ppermute(loss, "doc", flip(doc_count, bit))
+        loss = loss + other if bit > 2 else loss
+        other = lax.ppermute(loss, "doc", flip(doc_count, bit))
         bit *= 2
-    mean_loss = loss[0, 0]
-
-    class_grad = []
-    for i in range(2):
-        class_grad = [
-            pl.pallas_call(
-                functools.partial(sum_kernel, i * half_rows),
-                in_specs=[VMEM] * 3 + [HBM] * i,
-                out_specs=HBM,
-                out_shape=shape(grad_shape, F32),
-                scratch_shapes=[
-                    pltpu.VMEM((half_rows, width), F32), pltpu.SemaphoreType.DMA((CHUNKS,))
-                ],
-                input_output_aliases={3: 0} if i else {},
-                compiler_params=params,
-                cost_estimate=cost(1, 0),
-            )(kept, from_core_c, from_x[i], *class_grad)
-        ]
-    class_grad = class_grad[0].reshape(x_half, group * tile, width)
+
+    def scratch(count):
+        return [pltpu.VMEM((count, width), F32), pltpu.SemaphoreType.DMA((CHUNKS,))]
+
+    class_grad = pl.pallas_call(
+        near_kernel,
+        in_specs=[VMEM] * 3,
+        out_specs=HBM,
+        out_shape=shape(grad_shape, F32),
+        scratch_shapes=scratch(near),
+        compiler_params=params,
+        cost_estimate=cost(1, 0),
+    )(kept, from_core_c, from_x[0])
+    class_grad, mean_loss = pl.pallas_call(
+        functools.partial(far_kernel, near),
+        in_specs=[VMEM] * 5 + [HBM],
+        out_specs=[HBM, HBM],
+        out_shape=[shape(grad_shape, F32), shape((1, 1), F32)],
+        scratch_shapes=scratch(labels - near)
+        + [pltpu.VMEM((1, 1), F32), pltpu.SemaphoreType.DMA(())],
+        input_output_aliases={5: 0},
+        compiler_params=params,
+        cost_estimate=cost(1, 0),
+    )(kept, from_core_c, from_x[1], loss, other, class_grad)
+    mean_loss = mean_loss.reshape(())
+    class_grad = class_grad.reshape(x_half, group * tile, width)
     step = x_half // 2
     while step >= 1:
         pairs = class_grad.reshape(2, step, group * tile, width)

time: 48.4 us -> 45.7 us (0.944)
  waiting for transfers between devices: 6.5 us -> 4.36 us
  other arithmetic: 4.26 us -> 3.74 us
    ppermute x2 -> x1, waiting for transfers between devices: 3.16 us -> 0.96 us  [per_device(): other = lax.ppermute(loss, 'doc', flip(doc_count, bit))]
    add x2 -> x0, other arithmetic: 0.52 us -> none  [per_device(): loss = loss + lax.ppermute(loss, 'doc', flip(doc_count, bit))]
    ppermute x2 -> x1, starting transfers between devices: 1.5 us -> 1.49 us  [per_device(): other = lax.ppermute(loss, 'doc', flip(doc_count, bit))]
  transfers between devices with their start and end apart: 9 -> 8, of which waited for: 4 -> 4; matrix products, arithmetic and copies ran while one was open for 7% -> 6% of each run, Pallas kernels for 12% -> 14%
where the time goes in v3:
time: 45.7 us; the launch traced here: 45.4 us
  blocking collectives  14.2 us (31%)
  starting transfers between devices  12.6 us (28%)
  Pallas kernels  9.04 us (20%)
  waiting for transfers between devices  4.36 us (10%)
  other arithmetic  3.74 us (8%)
  local copies, waits for them, and re-layouts  0.79 us (2%)
  between operations  0.76 us (2%)
    all_to_all x1, blocking collectives, exchange(): lax.all_to_all(send, 'label', split_axis=0, concat_axis=0, tiled=True)  14.2 us
    ppermute x3, starting transfers between devices, per_device(): other = lax.ppermute(panel, 'label', flip(label_count, bit))  7.53 us
    ppermute x3, waiting for transfers between devices, per_device(): other = lax.ppermute(panel, 'label', flip(label_count, bit))  3.32 us
    ppermute x2, starting transfers between devices, per_device(): from_x = [lax.ppermute(half, 'doc', flip(doc_count, step)) for half in to_x]  2.99 us
    pallas_call x1, Pallas kernels, per_device(): pl.pallas_call(functools.partial(first_kernel, plan), in_specs=[VMEM] * 3...  2.11 us
    select_n x1, other arithmetic, per_device(): flat = jnp.where(early, classifier.reshape(-1, width), 0)  2.1 us
    pallas_call x1, Pallas kernels, per_device(): pl.pallas_call(functools.partial(third_kernel, plan), in_specs=[VMEM] * 3...  1.76 us
    ppermute x1, starting transfers between devices, per_device(): other = lax.ppermute(loss, 'doc', flip(doc_count, bit))  1.49 us
  transfers between devices with their start and end apart: 8, of which 4 were waited for; matrix products, arithmetic and copies ran while one was open for 6% of the time, Pallas kernels for 14%

profile of v3, /device:TPU:0, one launch (start us, length us, event | category | flops | bytes accessed | tf_op | source)
XLA Modules:
  0.0 45.4 jit_solution(5844371722629495284)
XLA Ops:
  0.6 0.8 %fusion = pred[16,128]{1,0:T(8,128)(4,1)S(1)} fusion(s32[32]{0:T(128)} %bitcast.10, s32[16]{0:T(128)S(1)} %iota_multiply_fusion), kind=kLoop, calls=%fused_computation.2 | loop fusion | flops 194560 | bytes 2240 | tf_op jit(solution)/shard_map/reduce_or | solution.py:209
  1.4 0.7 %pad_maximum_fusion = bf16[16,896]{1,0:T(8,128)(2,1)S(1)} fusion(bf16[16,128]{1,0:T(8,128)(2,1)S(1)} %convert_element_type.13, bf16[16,768]{1,0:T(8,128)(2,1)} %param.6), kind=kLoop, calls=%fused_computation.6 | loop fusion | flops 57344 | bytes 57344 | tf_op jit(solution)/shard_map/concatenate | solution.py:210
  2.2 3.0 %collective-permute-start = (bf16[16,896]{1,0:T(8,128)(2,1)S(1)}, bf16[16,896]{1,0:T(8,128)(2,1)S(1)}, u32[]{:S(2)}, u32[]{:S(2)}) collective-permute-start(bf16[16,896]{1,0:T(8,128)(2,1)S(1)} %pad_maximum_fusion), channel_id=1, source_target_pairs={{0,4},{4,0},{8,12},{12,8},{16,20},{20,16},{24,28},{28,24},{1,5},{5... | collective-permute-start | bytes 86024 | tf_op jit(solution)/shard_map/ppermute | solution.py:213
  5.2 0.8 %copy.10.pos_ref = s32[128,8]{1,0:T(8,128)S(1)} copy(s32[128,8]{0,1:T(8,128)} %param.9) | data formatting | bytes 8192 | tf_op args[3]
  5.9 1.4 %shard_map.67.target_ref = bf16[2,2,128,512]{3,2,1,0:T(8,128)(2,1)S(1)} custom-call(s32[128,8]{1,0:T(8,128)S(1)} %copy.10.pos_ref), custom_call_target="tpu_custom_call" | custom-call | flops 201326592 | bytes 1572864 | tf_op jit(solution)/shard_map/pallas_call | solution.py:224
  7.4 1.8 %collective-permute-start.1 = (bf16[32,896]{1,0:T(8,128)(2,1)S(1)}, bf16[32,896]{1,0:T(8,128)(2,1)S(1)}, u32[]{:S(2)}, u32[]{:S(2)}) collective-permute-start(bf16[32,896]{1,0:T(8,128)(2,1)S(1)} %maximum_select_fusion.2), channel_id=1, source_target_pairs={{0,8},{4,12},{8,0},{12,4},{16,24},{20,28},{24,16},{28,20},{1,9},{5... | collective-permute-start | bytes 172040 | tf_op jit(solution)/shard_map/ppermute | solution.py:213
  9.2 2.4 %collective-permute-done.1 = bf16[32,896]{1,0:T(8,128)(2,1)S(1)} collective-permute-done((bf16[32,896]{1,0:T(8,128)(2,1)S(1)}, bf16[32,896]{1,0:T(8,128)(2,1)S(1)}, u32[]{:S(2)}, u32[]{:S(2)}) %collective-permute-start.1) | collective-permute-done | bytes 57376 | tf_op jit(solution)/shard_map/ppermute | solution.py:213
  11.7 2.8 %collective-permute-start.2 = (bf16[64,896]{1,0:T(8,128)(2,1)S(1)}, bf16[64,896]{1,0:T(8,128)(2,1)S(1)}, u32[]{:S(2)}, u32[]{:S(2)}) collective-permute-start(bf16[64,896]{1,0:T(8,128)(2,1)S(1)} %maximum_select_fusion.1), channel_id=1, source_target_pairs={{0,16},{4,20},{8,24},{12,28},{16,0},{20,4},{24,8},{28,12},{1,17},{... | collective-permute-start | bytes 344072 | tf_op jit(solution)/shard_map/ppermute | solution.py:213
  14.4 2.1 %broadcast_select_fusion.rows_ref = bf16[2,1,2,512,768]{4,3,2,1,0:T(8,128)(2,1)S(1)} fusion(bf16[2,1,2,512,768]{4,3,2,1,0:T(8,128)(2,1)} %bitcast.8, pred[768]{0:T(1024)(128)(4,1)S(1)} %compare_reduce_fusion), kind=kLoop, calls=%fused_computation | loop fusion | flops 1572864 | bytes 6292224 | tf_op jit(solution)/shard_map/jit(_where)/select_n | solution.py:220
  16.5 0.9 %collective-permute-done.2 = bf16[64,896]{1,0:T(8,128)(2,1)S(1)} collective-permute-done((bf16[64,896]{1,0:T(8,128)(2,1)S(1)}, bf16[64,896]{1,0:T(8,128)(2,1)S(1)}, u32[]{:S(2)}, u32[]{:S(2)}) %collective-permute-start.2) | collective-permute-done | bytes 114720 | tf_op jit(solution)/shard_map/ppermute | solution.py:213
  17.5 2.1 %shard_map.68 = (bf16[528,768]{1,0:T(8,128)(2,1)S(1)}, bf16[4,128,512]{2,1,0:T(8,128)(2,1)S(1)}, f32[1,128]{1,0:T(1,128)S(1)}) custom-call(bf16[128,896]{1,0:T(8,128)(2,1)S(1)} %maximum_select_fusion.panel_ref, bf16[2,1,2,512,768]{4,3,2,1,0:T(8,128)(2,1)S(1)} %broadcast_select_fusion.rows_ref, bf16[2,2,128,512]{3,2,1,0:T(8,128)(2,1)S(1)} %shard_map.67.target_ref), custom_call_target="tpu_custom_call" | custom-call | flops 503316480 | bytes 3932160 | tf_op jit(solution)/shard_map/pallas_call | solution.py:234
  19.6 0.1 collective-permute-start.3
  19.7 1.8 %shard_map.69 = (bf16[512,768]{1,0:T(8,128)(2,1)}, f32[512,768]{1,0:T(8,128)S(1)}, bf16[128,896]{1,0:T(8,128)(2,1)S(1)}) custom-call(bf16[128,896]{1,0:T(8,128)(2,1)S(1)} %maximum_select_fusion.panel_ref, bf16[2,1,2,512,768]{4,3,2,1,0:T(8,128)(2,1)S(1)} %broadcast_select_fusion.rows_ref, bf16[4,128,512]{2,1,0:T(8,128)(2,1)S(1)} %get-tuple-element.24.weight_ref), custom_call_target="tpu_custom_call" | custom-call | flops 603979776 | bytes 4718592 | tf_op jit(solution)/shard_map/pallas_call | solution.py:247
  21.4 0.5 %collective-permute-start.4 = (bf16[512,768]{1,0:T(8,128)(2,1)}, bf16[512,768]{1,0:T(8,128)(2,1)S(1)}, u32[]{:S(2)}, u32[]{:S(2)}) collective-permute-start(bf16[512,768]{1,0:T(8,128)(2,1)} %get-tuple-element.34), channel_id=1, source_target_pairs={{0,1},{1,0},{2,3},{3,2},{4,5},{5,4},{6,7},{7,6},{8,9},{9,8},{10,11... | collective-permute-start | bytes 2359304 | tf_op jit(solution)/shard_map/ppermute | solution.py:257
  22.0 1.2 %shard_map.70 = (bf16[384,768]{1,0:T(8,128)(2,1)}, bf16[128,768]{1,0:T(8,128)(2,1)S(1)}, bf16[128,896]{1,0:T(8,128)(2,1)S(1)}) custom-call(bf16[128,896]{1,0:T(8,128)(2,1)S(1)} %maximum_select_fusion.panel_ref, bf16[4,128,512]{2,1,0:T(8,128)(2,1)S(1)} %get-tuple-element.24.weight_ref, ...), custom_call_target="tpu_custom_call", output_to_operand_aliasing={{2}: (4, {})} | custom-call | flops 100663296 | bytes 786432 | tf_op jit(solution)/shard_map/pallas_call | solution.py:259
  23.2 2.9 %collective-permute-start.7 = (bf16[384,768]{1,0:T(8,128)(2,1)}, bf16[384,768]{1,0:T(8,128)(2,1)S(1)}, u32[]{:S(2)}, u32[]{:S(2)}) collective-permute-start(bf16[384,768]{1,0:T(8,128)(2,1)} %get-tuple-element.29), channel_id=1, source_target_pairs={{0,2},{1,3},{2,0},{3,1},{4,6},{5,7},{6,4},{7,5},{8,10},{9,11},{10,... | collective-permute-start | bytes 1769480 | tf_op jit(solution)/shard_map/ppermute | solution.py:271
  26.1 0.1 collective-permute-start.5
  26.3 14.8 %conditional.1 = ((bf16[16,768]{1,0:T(8,128)(2,1)}, f32[1,128]{1,0:T(1,128)S(1)})) conditional(s32[]{:T(128)} %bitcast.1, () %tuple.17, bf16[128,896]{1,0:T(8,128)(2,1)S(1)} %get-tuple-element.31), branch_computations={%region_1.2_spmd, %region_2.3_spmd} | conditional | bytes 458760 | solution.py:290
  26.3 14.2 %all_to_all.4.parts_ref = bf16[8,16,896]{2,1,0:T(8,128)(2,1)S(1)} all-to-all(bf16[8,16,896]{2,1,0:T(8,128)(2,1)S(1)} %bitcast.9), channel_id=1, replica_groups=mesh['label'=8,'doc'=4] {'label'}, dimensions={0} | all-to-all | bytes 458752 | tf_op jit(solution)/shard_map/cond/branch_1_fun/all_to_all | solution.py:276
  40.4 0.6 %branch_1_fun.1 = (bf16[16,768]{1,0:T(8,128)(2,1)}, f32[1,128]{1,0:T(1,128)S(1)}) custom-call(bf16[8,16,896]{2,1,0:T(8,128)(2,1)S(1)} %all_to_all.4.parts_ref), custom_call_target="tpu_custom_call" | custom-call | tf_op jit(solution)/shard_map/cond/branch_1_fun/pallas_call | solution.py:277
  41.1 1.5 %collective-permute-start.6 = (f32[1,128]{1,0:T(1,128)S(1)}, f32[1,128]{1,0:T(1,128)S(1)}, u32[]{:S(2)}, u32[]{:S(2)}) collective-permute-start(f32[1,128]{1,0:T(1,128)S(1)} %get-tuple-element.35.loss_ref), channel_id=1, source_target_pairs={{0,2},{1,3},{2,0},{3,1},{4,6},{5,7},{6,4},{7,5},{8,10},{9,11},{10,... | collective-permute-start | bytes 1544 | tf_op jit(solution)/shard_map/ppermute | solution.py:294
  42.6 1.1 %shard_map.71.out_in = f32[512,768]{1,0:T(8,128)} custom-call(f32[512,768]{1,0:T(8,128)S(1)} %get-tuple-element.33.kept_ref, bf16[512,768]{1,0:T(8,128)(2,1)S(1)} %collective-permute-done.4.core_ref, bf16[384,768]{1,0:T(8,128)(2,1)S(1)} %collective-permute-done.7.x_ref), custom_call_target="tpu_custom_call" | custom-call | flops 100663296 | bytes 786432 | tf_op jit(solution)/shard_map/pallas_call | solution.py:300
  43.7 1.0 %collective-permute-done.6.other_ref = f32[1,128]{1,0:T(1,128)S(1)} collective-permute-done((f32[1,128]{1,0:T(1,128)S(1)}, f32[1,128]{1,0:T(1,128)S(1)}, u32[]{:S(2)}, u32[]{:S(2)}) %collective-permute-start.6) | collective-permute-done | bytes 544 | tf_op jit(solution)/shard_map/ppermute | solution.py:294
  44.6 0.8 %shard_map.72 = (f32[512,768]{1,0:T(8,128)}, f32[1,1]{1,0:T(1,128)}) custom-call(f32[512,768]{1,0:T(8,128)S(1)} %get-tuple-element.33.kept_ref, bf16[512,768]{1,0:T(8,128)(2,1)S(1)} %collective-permute-done.4.core_ref, bf16[128,768]{1,0:T(8,128)(2,1)S(1)} %collective-permute-done.5.x_ref, ...), custom_call_target="tpu_custom_call", output_to_operand_aliasing={{0}: (5, {})} | custom-call | flops 100663296 | bytes 786432 | tf_op jit(solution)/shard_map/pallas_call | solution.py:309
  (13 shorter events, 0.2 us)
Async XLA Ops:
  2.2 5.2 %collective-permute-start = (bf16[16,896]{1,0:T(8,128)(2,1)S(1)}, bf16[16,896]{1,0:T(8,128)(2,1)S(1)}, u32[]{:S(2)}, u32[]{:S(2)}) collective-permute-start(bf16[16,896]{1,0:T(8,128)(2,1)S(1)} %pad_maximum_fusion), channel_id=1, source_target_pairs={{0,4},{4,0},{8,12},{12,8},{16,20},{20,16},{24,28},{28,24},{1,5},{5... | collective-permute-start | bytes 86024 | tf_op jit(solution)/shard_map/ppermute | solution.py:213
  7.4 4.2 %collective-permute-start.1 = (bf16[32,896]{1,0:T(8,128)(2,1)S(1)}, bf16[32,896]{1,0:T(8,128)(2,1)S(1)}, u32[]{:S(2)}, u32[]{:S(2)}) collective-permute-start(bf16[32,896]{1,0:T(8,128)(2,1)S(1)} %maximum_select_fusion.2), channel_id=1, source_target_pairs={{0,8},{4,12},{8,0},{12,4},{16,24},{20,28},{24,16},{28,20},{1,9},{5... | collective-permute-start | bytes 172040 | tf_op jit(solution)/shard_map/ppermute | solution.py:213
  11.7 5.8 %collective-permute-start.2 = (bf16[64,896]{1,0:T(8,128)(2,1)S(1)}, bf16[64,896]{1,0:T(8,128)(2,1)S(1)}, u32[]{:S(2)}, u32[]{:S(2)}) collective-permute-start(bf16[64,896]{1,0:T(8,128)(2,1)S(1)} %maximum_select_fusion.1), channel_id=1, source_target_pairs={{0,16},{4,20},{8,24},{12,28},{16,0},{20,4},{24,8},{28,12},{1,17},{... | collective-permute-start | bytes 344072 | tf_op jit(solution)/shard_map/ppermute | solution.py:213
  19.6 6.6 %copy-start = (s32[1,1,32]{2,1,0:T(1,128)S(1)}, s32[1,1,32]{2,1,0:T(1,128)}, u32[]{:S(2)}) copy-start(s32[1,1,32]{2,1,0:T(1,128)} %param.8) | copy-start | bytes 388
  19.6 2.4 %collective-permute-start.3 = (bf16[528,768]{1,0:T(8,128)(2,1)S(1)}, bf16[528,768]{1,0:T(8,128)(2,1)S(1)}, u32[]{:S(2)}, u32[]{:S(2)}) collective-permute-start(bf16[528,768]{1,0:T(8,128)(2,1)S(1)} %get-tuple-element.25), channel_id=1, source_target_pairs={{0,1},{1,0},{2,3},{3,2},{4,5},{5,4},{6,7},{7,6},{8,9},{9,8},{10,11... | collective-permute-start | bytes 2433032 | tf_op jit(solution)/shard_map/ppermute | solution.py:245
  21.4 21.1 %collective-permute-start.4 = (bf16[512,768]{1,0:T(8,128)(2,1)}, bf16[512,768]{1,0:T(8,128)(2,1)S(1)}, u32[]{:S(2)}, u32[]{:S(2)}) collective-permute-start(bf16[512,768]{1,0:T(8,128)(2,1)} %get-tuple-element.34), channel_id=1, source_target_pairs={{0,1},{1,0},{2,3},{3,2},{4,5},{5,4},{6,7},{7,6},{8,9},{9,8},{10,11... | collective-permute-start | bytes 2359304 | tf_op jit(solution)/shard_map/ppermute | solution.py:257
  23.2 19.3 %collective-permute-start.7 = (bf16[384,768]{1,0:T(8,128)(2,1)}, bf16[384,768]{1,0:T(8,128)(2,1)S(1)}, u32[]{:S(2)}, u32[]{:S(2)}) collective-permute-start(bf16[384,768]{1,0:T(8,128)(2,1)} %get-tuple-element.29), channel_id=1, source_target_pairs={{0,2},{1,3},{2,0},{3,1},{4,6},{5,7},{6,4},{7,5},{8,10},{9,11},{10,... | collective-permute-start | bytes 1769480 | tf_op jit(solution)/shard_map/ppermute | solution.py:271
  26.1 18.5 %collective-permute-start.5 = (bf16[128,768]{1,0:T(8,128)(2,1)S(1)}, bf16[128,768]{1,0:T(8,128)(2,1)S(1)}, u32[]{:S(2)}, u32[]{:S(2)}) collective-permute-start(bf16[128,768]{1,0:T(8,128)(2,1)S(1)} %get-tuple-element.30), channel_id=1, source_target_pairs={{0,2},{1,3},{2,0},{3,1},{4,6},{5,7},{6,4},{7,5},{8,10},{9,11},{10,... | collective-permute-start | bytes 589832 | tf_op jit(solution)/shard_map/ppermute | solution.py:271
  41.1 3.5 %collective-permute-start.6 = (f32[1,128]{1,0:T(1,128)S(1)}, f32[1,128]{1,0:T(1,128)S(1)}, u32[]{:S(2)}, u32[]{:S(2)}) collective-permute-start(f32[1,128]{1,0:T(1,128)S(1)} %get-tuple-element.35.loss_ref), channel_id=1, source_target_pairs={{0,2},{1,3},{2,0},{3,1},{4,6},{5,7},{6,4},{7,5},{8,10},{9,11},{10,... | collective-permute-start | bytes 1544 | tf_op jit(solution)/shard_map/ppermute | solution.py:294

commit v4 on v2

--- a/solution.py
+++ b/solution.py
@@ -8,10 +8,10 @@
 from jax.sharding import PartitionSpec as P
 
 LANES = 128
+EXTRA = 16
 F32, BF16 = jnp.float32, jnp.bfloat16
 VMEM = pl.BlockSpec(memory_space=pltpu.VMEM)
 HBM = pl.BlockSpec(memory_space=pltpu.HBM)
-CHUNKS = 4
 
 
 def flip(size, bit):
@@ -89,60 +89,62 @@
     return lax.dot_general(weight, docs, (((0,), (0,)), ((), ())), preferred_element_type=F32)
 
 
-def first_kernel(plan, panel_ref, rows_ref, target_ref, grad_ref, weight_ref, loss_ref):
+def split_rows(value, count):
+    top = value.astype(BF16).astype(F32)
+    mid = (value - top).astype(BF16).astype(F32)
+    row = lax.broadcasted_iota(jnp.int32, (count, value.shape[1]), 0) % 16
+    low = jnp.where(row == 2, value - top - mid, 0.0)
+    return jnp.where(row == 0, top, jnp.where(row == 1, mid, low)).astype(BF16)
+
+
+def first_kernel(plan, panel_ref, rows_ref, target_ref, far_ref, near_ref, loss_ref):
     half, core = plan.place()
     docs = panel_ref[:, : plan.width]
     mine = listed_counts(plan, panel_ref)
-    losses = jnp.zeros((1, LANES), F32)
+    losses = jnp.zeros(loss_ref.shape, F32)
     for i, (h, c) in enumerate(plan.order(half, core)):
         weight, more = set_weights(
             plan, mine, docs, plan.rows(rows_ref, h, c), target_ref[h, c], h, c
         )
-        weight_ref[i] = weight
+        if i < 2:
+            far_ref[i] = weight
+        else:
+            near_ref[(i - 2) * plan.block : (i - 1) * plan.block] = weight
         losses = losses + more
-        if i == 0:
-            grad_ref[...] = label_grad(weight, docs).astype(BF16)
     loss_ref[...] = losses
-
-
-def second_kernel(plan, panel_ref, weight_ref, core_ref, near_ref, far_ref):
-    grad = label_grad(weight_ref[1], panel_ref[:, : plan.width]) + core_ref[...].astype(F32)
-    grad = grad.astype(BF16)
-    near_ref[...] = grad[: plan.labels // 2]
-    far_ref[...] = grad[plan.labels // 2 :]
-
-
-def third_kernel(
-    plan, panel_ref, rows_ref, weight_ref, loss_ref, grad_ref, kept_ref, send_ref
-):
+    near_ref[2 * plan.block :, :LANES] = split_rows(losses, EXTRA)
+    near_ref[2 * plan.block :, LANES:] = jnp.zeros((EXTRA, plan.labels - LANES), BF16)
+
+
+def send_kernel(plan, far_ref, near_ref, rows_ref, loss_ref, core_ref, send_ref):
     half, core = plan.place()
-    docs = panel_ref[:, : plan.width]
     part = jnp.zeros((plan.block, plan.width), F32)
     for i, (h, c) in enumerate(plan.order(half, core)):
-        rows = plan.rows(rows_ref, h, c)
-        part = part + jnp.dot(weight_ref[i], rows, preferred_element_type=F32)
+        weight = far_ref[i] if i < 2 else near_ref[(i - 2) * plan.block : (i - 1) * plan.block]
+        part = part + jnp.dot(weight, plan.rows(rows_ref, h, c), preferred_element_type=F32)
     send_ref[:, : plan.width] = part.astype(BF16)
-    loss = loss_ref[...]
-    top = loss.astype(BF16).astype(F32)
-    mid = (loss - top).astype(BF16).astype(F32)
-    row = lax.broadcasted_iota(jnp.int32, (plan.block, LANES), 0) % 16
-    terms = jnp.where(row == 0, top, jnp.where(row == 1, mid, jnp.where(row == 2, loss - top - mid, 0.0)))
-    send_ref[:, plan.width :] = terms.astype(BF16)
-    grad_ref[...] = label_grad(weight_ref[2], docs).astype(BF16)
-    kept_ref[...] = label_grad(weight_ref[3], docs)
-
-
-def sum_kernel(start, *refs):
-    kept_ref, core_ref, x_ref = refs[:3]
-    out_hbm, total_ref, sems = refs[-3:]
-    count = x_ref.shape[0] // CHUNKS
+    theirs = core_ref[2 * plan.block :, :LANES].astype(F32)
+    losses = loss_ref[...] + jnp.sum(theirs, axis=0, keepdims=True)
+    send_ref[:, plan.width :] = split_rows(losses, plan.block)
+
+
+def last_kernel(
+    plan, panel_ref, near_ref, panel_c_ref, near_c_ref, panel_x_ref, far_x_ref, panel_xc_ref,
+    far_xc_ref, out_hbm, sum_ref, sems,
+):
     copies = []
-    for i in range(CHUNKS):
-        near, far = pl.ds(i * count, count), pl.ds(start + i * count, count)
-        total_ref[near] = kept_ref[far] + core_ref[far].astype(F32) + x_ref[near].astype(F32)
-        copy = pltpu.make_async_copy(total_ref.at[near], out_hbm.at[far], sems.at[i])
-        copy.start()
-        copies.append(copy)
+    for start in range(0, plan.labels, LANES):
+        part = pl.ds(start, LANES)
+        sum_ref[part] = (
+            label_grad(near_ref[pl.ds(plan.block, plan.block), part], panel_ref[:, : plan.width])
+            + label_grad(near_c_ref[pl.ds(0, plan.block), part], panel_c_ref[:, : plan.width])
+            + label_grad(far_x_ref[1, :, part], panel_x_ref[:, : plan.width])
+            + label_grad(far_xc_ref[0, :, part], panel_xc_ref[:, : plan.width])
+        )
+        copies.append(
+            pltpu.make_async_copy(sum_ref.at[part], out_hbm.at[part], sems.at[len(copies)])
+        )
+        copies[-1].start()
     for copy in copies:
         copy.wait()
 
@@ -165,7 +167,7 @@
     owner = lax.axis_index("label")
     place = lax.axis_index("doc")
     shape = jax.ShapeDtypeStruct
-    params = pltpu.CompilerParams(vmem_limit_bytes=16 * 1024 * 1024)
+    params = pltpu.CompilerParams(vmem_limit_bytes=8 * 1024 * 1024)
 
     def cost(dots, scored):
         return pl.CostEstimate(
@@ -200,81 +202,61 @@
         cost_estimate=cost(2, 0),
     )(positives)
 
-    grad_shape = (labels, width)
-    grad_a, weights, loss = pl.pallas_call(
-        functools.partial(first_kernel, plan),
-        in_specs=[VMEM] * 3,
-        out_specs=[VMEM] * 3,
-        out_shape=[shape(grad_shape, BF16), shape((4, block, labels), BF16), shape((1, LANES), F32)],
-        compiler_params=params,
-        cost_estimate=cost(5, 4),
+    grad_shape, pair_shape = (labels, width), (2, block, labels)
+
+    def kernel(body, count, outs, dots, scored=0, **options):
+        return pl.pallas_call(
+            functools.partial(body, plan),
+            in_specs=[VMEM] * count,
+            out_specs=options.pop("out_specs", [VMEM] * len(outs)),
+            out_shape=outs,
+            compiler_params=params,
+            cost_estimate=cost(dots, scored),
+            **options,
+        )
+
+    near_shape = (2 * block + EXTRA, labels)
+    far, near, loss = kernel(
+        first_kernel, 3, [shape(pair_shape, BF16), shape(near_shape, BF16), shape((1, LANES), F32)],
+        4, 4,
     )(panel, rows, target)
     step = doc_count // 2
-    from_core_a = lax.ppermute(grad_a, "doc", flip(doc_count, 1))
-    half_rows = labels // 2
-    grad_c, kept, send = pl.pallas_call(
-        functools.partial(third_kernel, plan),
-        in_specs=[VMEM] * 4,
-        out_specs=[VMEM] * 3,
-        out_shape=[
-            shape(grad_shape, BF16), shape(grad_shape, F32), shape((block, width + LANES), BF16)
+    near_c = lax.ppermute(near, "doc", flip(doc_count, 1))
+    panel_c = lax.ppermute(panel, "doc", flip(doc_count, 1))
+    far_x = lax.ppermute(far, "doc", flip(doc_count, step))
+    panel_x = lax.ppermute(panel, "doc", flip(doc_count, step))
+    (send,) = kernel(send_kernel, 5, [shape((block, width + LANES), BF16)], 4)(
+        far, near, rows, loss, near_c
+    )
+    send = send.reshape(label_count, doc_dev, width + LANES)
+    parts = lax.all_to_all(send, "label", split_axis=0, concat_axis=0, tiled=True)
+
+    far_xc = lax.ppermute(far_x, "doc", flip(doc_count, 1))
+    panel_xc = lax.ppermute(panel_x, "doc", flip(doc_count, 1))
+    class_grad = kernel(
+        last_kernel, 8, shape(grad_shape, F32), 4,
+        out_specs=HBM,
+        scratch_shapes=[
+            pltpu.VMEM(grad_shape, F32), pltpu.SemaphoreType.DMA((labels // LANES,))
         ],
+    )(panel, near, panel_c, near_c, panel_x, far_x, panel_xc, far_xc)
+
+    parts, class_grad = lax.optimization_barrier((parts, class_grad))
+    entry_total = block * doc_count * label_count * listed * tile
+    doc_grad, loss = pl.pallas_call(
+        functools.partial(doc_kernel, 1.0 / entry_total),
+        in_specs=[VMEM],
+        out_specs=[VMEM, VMEM],
+        out_shape=[shape((doc_dev, width), BF16), shape((1, LANES), F32)],
         compiler_params=params,
-        cost_estimate=cost(6, 0),
-    )(panel, rows, weights, loss)
-    from_core_c = lax.ppermute(grad_c, "doc", flip(doc_count, 1))
-    weights, kept, send = lax.optimization_barrier((weights, kept, send))
-    to_x = pl.pallas_call(
-        functools.partial(second_kernel, plan),
-        in_specs=[VMEM] * 3,
-        out_specs=[VMEM] * 2,
-        out_shape=[shape((half_rows, width), BF16)] * 2,
-        compiler_params=params,
-        cost_estimate=cost(1, 0),
-    )(panel, weights, from_core_a)
-    from_x = [lax.ppermute(half, "doc", flip(doc_count, step)) for half in to_x]
-    entry_total = block * doc_count * label_count * listed * tile
-
-    def exchange(send):
-        send = send.reshape(label_count, doc_dev, width + LANES)
-        parts = lax.all_to_all(send, "label", split_axis=0, concat_axis=0, tiled=True)
-        doc_grad, loss = pl.pallas_call(
-            functools.partial(doc_kernel, 1.0 / entry_total),
-            in_specs=[VMEM],
-            out_specs=[VMEM, VMEM],
-            out_shape=[shape((doc_dev, width), BF16), shape((1, LANES), F32)],
-            compiler_params=params,
-        )(parts)
-        return doc_grad, loss
-
-    def nothing(send):
-        return jnp.zeros((doc_dev, width), BF16), jnp.zeros((1, LANES), F32)
-
-    send, *to_x = lax.optimization_barrier((send, *to_x))
-    doc_grad, loss = lax.cond(shortlist[0, 0, 0] >= 0, exchange, nothing, send)
-    bit = 1
+    )(parts)
+    bit, other = 2, jnp.zeros((1, LANES), F32)
     while bit < doc_count:
-        loss = loss + lax.ppermute(loss, "doc", flip(doc_count, bit))
+        loss = loss + other if bit > 2 else loss
+        other = lax.ppermute(loss, "doc", flip(doc_count, bit))
         bit *= 2
-    mean_loss = loss[0, 0]
-
-    class_grad = []
-    for i in range(2):
-        class_grad = [
-            pl.pallas_call(
-                functools.partial(sum_kernel, i * half_rows),
-                in_specs=[VMEM] * 3 + [HBM] * i,
-                out_specs=HBM,
-                out_shape=shape(grad_shape, F32),
-                scratch_shapes=[
-                    pltpu.VMEM((half_rows, width), F32), pltpu.SemaphoreType.DMA((CHUNKS,))
-                ],
-                input_output_aliases={3: 0} if i else {},
-                compiler_params=params,
-                cost_estimate=cost(1, 0),
-            )(kept, from_core_c, from_x[i], *class_grad)
-        ]
-    class_grad = class_grad[0].reshape(x_half, group * tile, width)
+    mean_loss = (loss + other)[0, 0]
+    class_grad = class_grad.reshape(x_half, group * tile, width)
     step = x_half // 2
     while step >= 1:
         pairs = class_grad.reshape(2, step, group * tile, width)

time: 48.4 us -> 43.4 us (0.90)
  blocking collectives: 14.4 us -> 0 us
  starting transfers between devices: 12.4 us -> 18.8 us
  waiting for transfers between devices: 6.5 us -> 11.3 us
  Pallas kernels: 8.88 us -> 7.1 us
    all_to_all x1 -> x0, blocking collectives: 14.4 us -> none  [exchange(): lax.all_to_all(send, 'label', split_axis=0, concat_axis=0, tiled=True)]
    all_to_all x0 -> x1, starting transfers between devices: none -> 6.16 us  [per_device(): lax.all_to_all(send, 'label', split_axis=0, concat_axis=0, tiled=True)]
    ppermute x6 -> x7, waiting for transfers between devices: 3.17 us -> 7.24 us  [the longest x1 3.7 us: per_device(): panel_x = lax.ppermute(panel, 'doc', flip(doc_count, step))]
    pallas_call x6 -> x4, Pallas kernels: 7.48 us -> 5.69 us  [the longest x1 1.92 us: per_device(): kernel(last_kernel, 8, shape(grad_shape, F32), 4, out_specs=HBM, scratch_...]
    all_to_all x0 -> x1, waiting for transfers between devices: none -> 0.78 us  [per_device(): lax.all_to_all(send, 'label', split_axis=0, concat_axis=0, tiled=True)]
    ppermute x6 -> x7, starting transfers between devices: 4.92 us -> 5.13 us  [the longest x1 2.9 us: per_device(): far_x = lax.ppermute(far, 'doc', flip(doc_count, step))]
  transfers between devices with their start and end apart: 9 -> 11, of which waited for: 4 -> 6; matrix products, arithmetic and copies ran while one was open for 7% -> 7% of each run, Pallas kernels for 12% -> 11%
where the time goes in v4:
time: 43.4 us; the launch traced here: 43 us
  starting transfers between devices  18.8 us (43%)
  waiting for transfers between devices  11.3 us (26%)
  Pallas kernels  7.1 us (16%)
  other arithmetic  4.26 us (10%)
  local copies, waits for them, and re-layouts  0.79 us (2%)
  between operations  0.72 us (2%)
    ppermute x3, starting transfers between devices, per_device(): other = lax.ppermute(panel, 'label', flip(label_count, bit))  7.53 us
    all_to_all x1, starting transfers between devices, per_device(): lax.all_to_all(send, 'label', split_axis=0, concat_axis=0, tiled=True)  6.16 us
    ppermute x1, waiting for transfers between devices, per_device(): panel_x = lax.ppermute(panel, 'doc', flip(doc_count, step))  3.7 us
    ppermute x3, waiting for transfers between devices, per_device(): other = lax.ppermute(panel, 'label', flip(label_count, bit))  3.32 us
    ppermute x1, starting transfers between devices, per_device(): far_x = lax.ppermute(far, 'doc', flip(doc_count, step))  2.9 us
    select_n x1, other arithmetic, per_device(): flat = jnp.where(early, classifier.reshape(-1, width), 0)  2.1 us
    ppermute x1, waiting for transfers between devices, per_device(): other = lax.ppermute(loss, 'doc', flip(doc_count, bit))  2.04 us
    pallas_call x1, Pallas kernels, per_device(): kernel(last_kernel, 8, shape(grad_shape, F32), 4, out_specs=HBM, scratch_...  1.92 us
  transfers between devices with their start and end apart: 11, of which 6 were waited for; matrix products, arithmetic and copies ran while one was open for 7% of the time, Pallas kernels for 11%

profile of v4, /device:TPU:0, one launch (start us, length us, event | category | flops | bytes accessed | tf_op | source)
XLA Modules:
  0.0 43.0 jit_solution(11169642118614384313)
XLA Ops:
  0.6 0.8 %fusion = pred[16,128]{1,0:T(8,128)(4,1)S(1)} fusion(s32[32]{0:T(128)} %bitcast.8, s32[16]{0:T(128)S(1)} %iota_multiply_fusion), kind=kLoop, calls=%fused_computation.2 | loop fusion | flops 194560 | bytes 2240 | tf_op jit(solution)/shard_map/reduce_or | solution.py:181
  1.4 0.7 %pad_maximum_fusion = bf16[16,896]{1,0:T(8,128)(2,1)S(1)} fusion(bf16[16,128]{1,0:T(8,128)(2,1)S(1)} %convert_element_type.5, bf16[16,768]{1,0:T(8,128)(2,1)} %param.4), kind=kLoop, calls=%fused_computation.6 | loop fusion | flops 57344 | bytes 57344 | tf_op jit(solution)/shard_map/concatenate | solution.py:182
  2.2 3.0 %collective-permute-start = (bf16[16,896]{1,0:T(8,128)(2,1)S(1)}, bf16[16,896]{1,0:T(8,128)(2,1)S(1)}, u32[]{:S(2)}, u32[]{:S(2)}) collective-permute-start(bf16[16,896]{1,0:T(8,128)(2,1)S(1)} %pad_maximum_fusion), channel_id=1, source_target_pairs={{0,4},{4,0},{8,12},{12,8},{16,20},{20,16},{24,28},{28,24},{1,5},{5... | collective-permute-start | bytes 86024 | tf_op jit(solution)/shard_map/ppermute | solution.py:185
  5.2 0.8 %copy.8.pos_ref = s32[128,8]{1,0:T(8,128)S(1)} copy(s32[128,8]{0,1:T(8,128)} %param.7) | data formatting | bytes 8192 | tf_op args[3]
  5.9 1.4 %shard_map.67.target_ref = bf16[2,2,128,512]{3,2,1,0:T(8,128)(2,1)S(1)} custom-call(s32[128,8]{1,0:T(8,128)S(1)} %copy.8.pos_ref), custom_call_target="tpu_custom_call" | custom-call | flops 201326592 | bytes 1572864 | tf_op jit(solution)/shard_map/pallas_call | solution.py:196
  7.4 1.8 %collective-permute-start.1 = (bf16[32,896]{1,0:T(8,128)(2,1)S(1)}, bf16[32,896]{1,0:T(8,128)(2,1)S(1)}, u32[]{:S(2)}, u32[]{:S(2)}) collective-permute-start(bf16[32,896]{1,0:T(8,128)(2,1)S(1)} %maximum_select_fusion.2), channel_id=1, source_target_pairs={{0,8},{4,12},{8,0},{12,4},{16,24},{20,28},{24,16},{28,20},{1,9},{5... | collective-permute-start | bytes 172040 | tf_op jit(solution)/shard_map/ppermute | solution.py:185
  9.2 2.4 %collective-permute-done.1 = bf16[32,896]{1,0:T(8,128)(2,1)S(1)} collective-permute-done((bf16[32,896]{1,0:T(8,128)(2,1)S(1)}, bf16[32,896]{1,0:T(8,128)(2,1)S(1)}, u32[]{:S(2)}, u32[]{:S(2)}) %collective-permute-start.1) | collective-permute-done | bytes 57376 | tf_op jit(solution)/shard_map/ppermute | solution.py:185
  11.7 2.8 %collective-permute-start.2 = (bf16[64,896]{1,0:T(8,128)(2,1)S(1)}, bf16[64,896]{1,0:T(8,128)(2,1)S(1)}, u32[]{:S(2)}, u32[]{:S(2)}) collective-permute-start(bf16[64,896]{1,0:T(8,128)(2,1)S(1)} %maximum_select_fusion.1), channel_id=1, source_target_pairs={{0,16},{4,20},{8,24},{12,28},{16,0},{20,4},{24,8},{28,12},{1,17},{... | collective-permute-start | bytes 344072 | tf_op jit(solution)/shard_map/ppermute | solution.py:185
  14.4 2.1 %broadcast_select_fusion.rows_ref = bf16[2,1,2,512,768]{4,3,2,1,0:T(8,128)(2,1)S(1)} fusion(bf16[2,1,2,512,768]{4,3,2,1,0:T(8,128)(2,1)} %bitcast.6, pred[768]{0:T(1024)(128)(4,1)S(1)} %compare_reduce_fusion), kind=kLoop, calls=%fused_computation | loop fusion | flops 1572864 | bytes 6292224 | tf_op jit(solution)/shard_map/jit(_where)/select_n | solution.py:192
  16.5 0.9 %collective-permute-done.2 = bf16[64,896]{1,0:T(8,128)(2,1)S(1)} collective-permute-done((bf16[64,896]{1,0:T(8,128)(2,1)S(1)}, bf16[64,896]{1,0:T(8,128)(2,1)S(1)}, u32[]{:S(2)}, u32[]{:S(2)}) %collective-permute-start.2) | collective-permute-done | bytes 114720 | tf_op jit(solution)/shard_map/ppermute | solution.py:185
  17.5 1.9 %shard_map.68 = (bf16[2,128,512]{2,1,0:T(8,128)(2,1)S(1)}, bf16[272,512]{1,0:T(8,128)(2,1)S(1)}, f32[1,128]{1,0:T(1,128)S(1)}) custom-call(bf16[128,896]{1,0:T(8,128)(2,1)S(1)} %maximum_select_fusion.panel_ref, bf16[2,1,2,512,768]{4,3,2,1,0:T(8,128)(2,1)S(1)} %broadcast_select_fusion.rows_ref, bf16[2,2,128,512]{3,2,1,0:T(8,128)(2,1)S(1)} %shard_map.67.target_ref), custom_call_target="tpu_custom_call" | custom-call | flops 402653184 | bytes 3145728 | tf_op jit(solution)/shard_map/pallas_call | solution.py:219
  19.4 2.9 %collective-permute-start.6 = (bf16[2,128,512]{2,1,0:T(8,128)(2,1)S(1)}, bf16[2,128,512]{2,1,0:T(8,128)(2,1)S(1)}, u32[]{:S(2)}, u32[]{:S(2)}) collective-permute-start(bf16[2,128,512]{2,1,0:T(8,128)(2,1)S(1)} %get-tuple-element.10.far_ref), channel_id=1, source_target_pairs={{0,2},{1,3},{2,0},{3,1},{4,6},{5,7},{6,4},{7,5},{8,10},{9,11},{10,... | collective-permute-start | bytes 786440 | tf_op jit(solution)/shard_map/ppermute | solution.py:226
  22.3 0.1 collective-permute-start.5
  22.4 1.3 %shard_map.69 = bf16[128,896]{1,0:T(8,128)(2,1)} custom-call(bf16[2,128,512]{2,1,0:T(8,128)(2,1)S(1)} %get-tuple-element.10.far_ref, bf16[272,512]{1,0:T(8,128)(2,1)S(1)} %get-tuple-element.11.near_ref, bf16[2,1,2,512,768]{4,3,2,1,0:T(8,128)(2,1)S(1)} %broadcast_select_fusion.rows_ref, f32[1,128]{1,0:T(1,128)S(1)} %get-tuple-element.12.loss_ref, ...), custom_call_target="tpu_custom_call" | custom-call | flops 402653184 | bytes 3145728 | tf_op jit(solution)/shard_map/pallas_call | solution.py:228
  23.7 6.2 %all-to-all-start = ((bf16[8,16,896]{2,1,0:T(8,128)(2,1)}), bf16[8,16,896]{2,1,0:T(8,128)(2,1)S(1)}, u32[]{:S(2)}, u32[]{:S(2)}) async-start(bf16[8,16,896]{2,1,0:T(8,128)(2,1)} %bitcast.2), calls=%async_computation | async-start | bytes 458752 | tf_op jit(solution)/shard_map/all_to_all | solution.py:232
  29.9 0.5 %collective-permute-start.4 = (bf16[128,896]{1,0:T(8,128)(2,1)S(1)}, bf16[128,896]{1,0:T(8,128)(2,1)S(1)}, u32[]{:S(2)}, u32[]{:S(2)}) collective-permute-start(bf16[128,896]{1,0:T(8,128)(2,1)S(1)} %maximum_select_fusion.panel_ref), channel_id=1, source_target_pairs={{0,1},{1,0},{2,3},{3,2},{4,5},{5,4},{6,7},{7,6},{8,9},{9,8},{10,11... | collective-permute-start | bytes 688136 | tf_op jit(solution)/shard_map/ppermute | solution.py:225
  30.4 3.7 %collective-permute-done.5.panel_x_ref = bf16[128,896]{1,0:T(8,128)(2,1)S(1)} collective-permute-done((bf16[128,896]{1,0:T(8,128)(2,1)S(1)}, bf16[128,896]{1,0:T(8,128)(2,1)S(1)}, u32[]{:S(2)}, u32[]{:S(2)}) %collective-permute-start.5) | collective-permute-done | bytes 229408 | tf_op jit(solution)/shard_map/ppermute | solution.py:227
  34.1 1.5 %collective-permute-done.7.panel_xc_ref = bf16[128,896]{1,0:T(8,128)(2,1)S(1)} collective-permute-done((bf16[128,896]{1,0:T(8,128)(2,1)S(1)}, bf16[128,896]{1,0:T(8,128)(2,1)S(1)}, u32[]{:S(2)}, u32[]{:S(2)}) %collective-permute-start.7) | collective-permute-done | bytes 229408 | tf_op jit(solution)/shard_map/ppermute | solution.py:235
  35.6 1.9 %shard_map.70 = f32[512,768]{1,0:T(8,128)} custom-call(bf16[128,896]{1,0:T(8,128)(2,1)S(1)} %maximum_select_fusion.panel_ref, bf16[272,512]{1,0:T(8,128)(2,1)S(1)} %get-tuple-element.11.near_ref, bf16[128,896]{1,0:T(8,128)(2,1)S(1)} %collective-permute-done.4.panel_c_ref, bf16[272,512]{1,0:T(8,128)(2,1)S(1)} %collective-permute-done.3.core_ref.near_c_ref, ...), custom_call_target="tpu_custom_call" | custom-call | flops 402653184 | bytes 3145728 | tf_op jit(solution)/shard_map/pallas_call | solution.py:236
  37.6 0.8 %all-to-all-done.parts_ref = bf16[8,16,896]{2,1,0:T(8,128)(2,1)S(1)} async-done(((bf16[8,16,896]{2,1,0:T(8,128)(2,1)}), bf16[8,16,896]{2,1,0:T(8,128)(2,1)S(1)}, u32[]{:S(2)}, u32[]{:S(2)}) %all-to-all-start) | async-done | bytes 229408 | tf_op jit(solution)/shard_map/all_to_all | solution.py:232
  38.3 0.6 %shard_map.71 = (bf16[16,768]{1,0:T(8,128)(2,1)}, f32[1,128]{1,0:T(1,128)S(1)}) custom-call(bf16[8,16,896]{2,1,0:T(8,128)(2,1)S(1)} %all-to-all-done.parts_ref), custom_call_target="tpu_custom_call" | custom-call | tf_op jit(solution)/shard_map/pallas_call | solution.py:246
  39.0 1.5 %collective-permute-start.9 = (f32[1,128]{1,0:T(1,128)S(1)}, f32[1,128]{1,0:T(1,128)S(1)}, u32[]{:S(2)}, u32[]{:S(2)}) collective-permute-start(f32[1,128]{1,0:T(1,128)S(1)} %get-tuple-element.16), channel_id=1, source_target_pairs={{0,2},{1,3},{2,0},{3,1},{4,6},{5,7},{6,4},{7,5},{8,10},{9,11},{10,... | collective-permute-start | bytes 1544 | tf_op jit(solution)/shard_map/ppermute | solution.py:256
  40.5 2.0 %collective-permute-done.9 = f32[1,128]{1,0:T(1,128)S(1)} collective-permute-done((f32[1,128]{1,0:T(1,128)S(1)}, f32[1,128]{1,0:T(1,128)S(1)}, u32[]{:S(2)}, u32[]{:S(2)}) %collective-permute-start.9) | collective-permute-done | bytes 544 | tf_op jit(solution)/shard_map/ppermute | solution.py:256
  42.5 0.5 %add.23 = f32[1,128]{1,0:T(1,128)} add(f32[1,128]{1,0:T(1,128)S(1)} %get-tuple-element.16, f32[1,128]{1,0:T(1,128)S(1)} %collective-permute-done.9) | non-fusion elementwise | flops 128 | bytes 1536 | tf_op jit(solution)/shard_map/add | solution.py:258
  (14 shorter events, 0.3 us)
Async XLA Ops:
  2.2 5.2 %collective-permute-start = (bf16[16,896]{1,0:T(8,128)(2,1)S(1)}, bf16[16,896]{1,0:T(8,128)(2,1)S(1)}, u32[]{:S(2)}, u32[]{:S(2)}) collective-permute-start(bf16[16,896]{1,0:T(8,128)(2,1)S(1)} %pad_maximum_fusion), channel_id=1, source_target_pairs={{0,4},{4,0},{8,12},{12,8},{16,20},{20,16},{24,28},{28,24},{1,5},{5... | collective-permute-start | bytes 86024 | tf_op jit(solution)/shard_map/ppermute | solution.py:185
  7.4 4.2 %collective-permute-start.1 = (bf16[32,896]{1,0:T(8,128)(2,1)S(1)}, bf16[32,896]{1,0:T(8,128)(2,1)S(1)}, u32[]{:S(2)}, u32[]{:S(2)}) collective-permute-start(bf16[32,896]{1,0:T(8,128)(2,1)S(1)} %maximum_select_fusion.2), channel_id=1, source_target_pairs={{0,8},{4,12},{8,0},{12,4},{16,24},{20,28},{24,16},{28,20},{1,9},{5... | collective-permute-start | bytes 172040 | tf_op jit(solution)/shard_map/ppermute | solution.py:185
  11.7 5.8 %collective-permute-start.2 = (bf16[64,896]{1,0:T(8,128)(2,1)S(1)}, bf16[64,896]{1,0:T(8,128)(2,1)S(1)}, u32[]{:S(2)}, u32[]{:S(2)}) collective-permute-start(bf16[64,896]{1,0:T(8,128)(2,1)S(1)} %maximum_select_fusion.1), channel_id=1, source_target_pairs={{0,16},{4,20},{8,24},{12,28},{16,0},{20,4},{24,8},{28,12},{1,17},{... | collective-permute-start | bytes 344072 | tf_op jit(solution)/shard_map/ppermute | solution.py:185
  19.3 3.1 %collective-permute-start.3 = (bf16[272,512]{1,0:T(8,128)(2,1)S(1)}, bf16[272,512]{1,0:T(8,128)(2,1)S(1)}, u32[]{:S(2)}, u32[]{:S(2)}) collective-permute-start(bf16[272,512]{1,0:T(8,128)(2,1)S(1)} %get-tuple-element.11.near_ref), channel_id=1, source_target_pairs={{0,1},{1,0},{2,3},{3,2},{4,5},{5,4},{6,7},{7,6},{8,9},{9,8},{10,11... | collective-permute-start | bytes 835592 | tf_op jit(solution)/shard_map/ppermute | solution.py:224
  19.4 10.4 %collective-permute-start.6 = (bf16[2,128,512]{2,1,0:T(8,128)(2,1)S(1)}, bf16[2,128,512]{2,1,0:T(8,128)(2,1)S(1)}, u32[]{:S(2)}, u32[]{:S(2)}) collective-permute-start(bf16[2,128,512]{2,1,0:T(8,128)(2,1)S(1)} %get-tuple-element.10.far_ref), channel_id=1, source_target_pairs={{0,2},{1,3},{2,0},{3,1},{4,6},{5,7},{6,4},{7,5},{8,10},{9,11},{10,... | collective-permute-start | bytes 786440 | tf_op jit(solution)/shard_map/ppermute | solution.py:226
  22.3 11.8 %collective-permute-start.5 = (bf16[128,896]{1,0:T(8,128)(2,1)S(1)}, bf16[128,896]{1,0:T(8,128)(2,1)S(1)}, u32[]{:S(2)}, u32[]{:S(2)}) collective-permute-start(bf16[128,896]{1,0:T(8,128)(2,1)S(1)} %maximum_select_fusion.panel_ref), channel_id=1, source_target_pairs={{0,2},{1,3},{2,0},{3,1},{4,6},{5,7},{6,4},{7,5},{8,10},{9,11},{10,... | collective-permute-start | bytes 688136 | tf_op jit(solution)/shard_map/ppermute | solution.py:227
  23.7 14.7 %all-to-all-start = ((bf16[8,16,896]{2,1,0:T(8,128)(2,1)}), bf16[8,16,896]{2,1,0:T(8,128)(2,1)S(1)}, u32[]{:S(2)}, u32[]{:S(2)}) async-start(bf16[8,16,896]{2,1,0:T(8,128)(2,1)} %bitcast.2), calls=%async_computation | async-start | bytes 458752 | tf_op jit(solution)/shard_map/all_to_all | solution.py:232
  29.9 5.8 %collective-permute-start.8 = (bf16[2,128,512]{2,1,0:T(8,128)(2,1)S(1)}, bf16[2,128,512]{2,1,0:T(8,128)(2,1)S(1)}, u32[]{:S(2)}, u32[]{:S(2)}) collective-permute-start(bf16[2,128,512]{2,1,0:T(8,128)(2,1)S(1)} %collective-permute-done.6.far_x_ref), channel_id=1, source_target_pairs={{0,1},{1,0},{2,3},{3,2},{4,5},{5,4},{6,7},{7,6},{8,9},{9,8},{10,11... | collective-permute-start | bytes 786440 | tf_op jit(solution)/shard_map/ppermute | solution.py:234
  29.9 4.2 %collective-permute-start.4 = (bf16[128,896]{1,0:T(8,128)(2,1)S(1)}, bf16[128,896]{1,0:T(8,128)(2,1)S(1)}, u32[]{:S(2)}, u32[]{:S(2)}) collective-permute-start(bf16[128,896]{1,0:T(8,128)(2,1)S(1)} %maximum_select_fusion.panel_ref), channel_id=1, source_target_pairs={{0,1},{1,0},{2,3},{3,2},{4,5},{5,4},{6,7},{7,6},{8,9},{9,8},{10,11... | collective-permute-start | bytes 688136 | tf_op jit(solution)/shard_map/ppermute | solution.py:225
  34.1 1.5 %collective-permute-start.7 = (bf16[128,896]{1,0:T(8,128)(2,1)S(1)}, bf16[128,896]{1,0:T(8,128)(2,1)S(1)}, u32[]{:S(2)}, u32[]{:S(2)}) collective-permute-start(bf16[128,896]{1,0:T(8,128)(2,1)S(1)} %collective-permute-done.5.panel_x_ref), channel_id=1, source_target_pairs={{0,1},{1,0},{2,3},{3,2},{4,5},{5,4},{6,7},{7,6},{8,9},{9,8},{10,11... | collective-permute-start | bytes 688136 | tf_op jit(solution)/shard_map/ppermute | solution.py:235
  39.0 3.5 %collective-permute-start.9 = (f32[1,128]{1,0:T(1,128)S(1)}, f32[1,128]{1,0:T(1,128)S(1)}, u32[]{:S(2)}, u32[]{:S(2)}) collective-permute-start(f32[1,128]{1,0:T(1,128)S(1)} %get-tuple-element.16), channel_id=1, source_target_pairs={{0,2},{1,3},{2,0},{3,1},{4,6},{5,7},{6,4},{7,5},{8,10},{9,11},{10,... | collective-permute-start | bytes 1544 | tf_op jit(solution)/shard_map/ppermute | solution.py:256

commit v5 on v4

--- a/solution.py
+++ b/solution.py
@@ -149,11 +149,14 @@
         copy.wait()
 
 
-def doc_kernel(scale, parts_ref, doc_ref, loss_ref):
-    total = jnp.sum(parts_ref[...].astype(F32), axis=0)
+def doc_kernel(parts_ref, doc_ref):
     width = doc_ref.shape[1]
-    doc_ref[...] = total[:, :width].astype(BF16)
-    loss_ref[...] = jnp.full(loss_ref.shape, jnp.sum(total[:, width:]) * scale, F32)
+    doc_ref[...] = jnp.sum(parts_ref[:, :, :width].astype(F32), axis=0).astype(BF16)
+
+
+def loss_kernel(scale, parts_ref, loss_ref):
+    total = jnp.sum(parts_ref[:, :, parts_ref.shape[2] - LANES :].astype(F32), axis=0)
+    loss_ref[...] = jnp.full(loss_ref.shape, jnp.sum(total) * scale, F32)
 
 
 def per_device(doc_embed, classifier, shortlist, positives):
@@ -243,11 +246,11 @@
 
     parts, class_grad = lax.optimization_barrier((parts, class_grad))
     entry_total = block * doc_count * label_count * listed * tile
-    doc_grad, loss = pl.pallas_call(
-        functools.partial(doc_kernel, 1.0 / entry_total),
+    loss = pl.pallas_call(
+        functools.partial(loss_kernel, 1.0 / entry_total),
         in_specs=[VMEM],
-        out_specs=[VMEM, VMEM],
-        out_shape=[shape((doc_dev, width), BF16), shape((1, LANES), F32)],
+        out_specs=VMEM,
+        out_shape=shape((1, LANES), F32),
         compiler_params=params,
     )(parts)
     bit, other = 2, jnp.zeros((1, LANES), F32)
@@ -255,6 +258,14 @@
         loss = loss + other if bit > 2 else loss
         other = lax.ppermute(loss, "doc", flip(doc_count, bit))
         bit *= 2
+    doc_grad = pl.pallas_call(
+        doc_kernel,
+        in_specs=[VMEM],
+        out_specs=VMEM,
+        out_shape=shape((doc_dev, width), BF16),
+        compiler_params=params,
+    )(parts)
+    doc_grad, other = lax.optimization_barrier((doc_grad, other))
     mean_loss = (loss + other)[0, 0]
     class_grad = class_grad.reshape(x_half, group * tile, width)
     step = x_half // 2

time: 43.4 us -> 42.9 us (0.988)
  waiting for transfers between devices: 11.3 us -> 10.7 us
    ppermute x1, waiting for transfers between devices: 2.04 us -> 1.41 us  [per_device(): other = lax.ppermute(loss, 'doc', flip(doc_count, bit))]
  transfers between devices with their start and end apart: 11 -> 11, of which waited for: 6 -> 6; matrix products, arithmetic and copies ran while one was open for 7% -> 7% of each run, Pallas kernels for 11% -> 12%
where the time goes in v5:
time: 42.9 us; the launch traced here: 42.6 us
  starting transfers between devices  18.9 us (44%)
  waiting for transfers between devices  10.7 us (25%)
  Pallas kernels  7.22 us (17%)
  other arithmetic  4.26 us (10%)
  local copies, waits for them, and re-layouts  0.79 us (2%)
  between operations  0.73 us (2%)
    ppermute x3, starting transfers between devices, per_device(): other = lax.ppermute(panel, 'label', flip(label_count, bit))  7.53 us
    all_to_all x1, starting transfers between devices, per_device(): lax.all_to_all(send, 'label', split_axis=0, concat_axis=0, tiled=True)  6.16 us
    ppermute x1, waiting for transfers between devices, per_device(): panel_x = lax.ppermute(panel, 'doc', flip(doc_count, step))  3.7 us
    ppermute x3, waiting for transfers between devices, per_device(): other = lax.ppermute(panel, 'label', flip(label_count, bit))  3.32 us
    ppermute x1, starting transfers between devices, per_device(): far_x = lax.ppermute(far, 'doc', flip(doc_count, step))  2.9 us
    select_n x1, other arithmetic, per_device(): flat = jnp.where(early, classifier.reshape(-1, width), 0)  2.1 us
    pallas_call x1, Pallas kernels, per_device(): kernel(last_kernel, 8, shape(grad_shape, F32), 4, out_specs=HBM, scratch_...  1.92 us
    pallas_call x1, Pallas kernels, per_device(): kernel(first_kernel, 3, [shape(pair_shape, BF16), shape(near_shape, BF16)...  1.86 us
  transfers between devices with their start and end apart: 11, of which 6 were waited for; matrix products, arithmetic and copies ran while one was open for 7% of the time, Pallas kernels for 12%

profile of v5, /device:TPU:0, one launch (start us, length us, event | category | flops | bytes accessed | tf_op | source)
XLA Modules:
  0.0 42.6 jit_solution(5174382998545854169)
XLA Ops:
  0.6 0.8 %fusion = pred[16,128]{1,0:T(8,128)(4,1)S(1)} fusion(s32[32]{0:T(128)} %bitcast.8, s32[16]{0:T(128)S(1)} %iota_multiply_fusion), kind=kLoop, calls=%fused_computation.2 | loop fusion | flops 194560 | bytes 2240 | tf_op jit(solution)/shard_map/reduce_or | solution.py:184
  1.4 0.7 %pad_maximum_fusion = bf16[16,896]{1,0:T(8,128)(2,1)S(1)} fusion(bf16[16,128]{1,0:T(8,128)(2,1)S(1)} %convert_element_type.5, bf16[16,768]{1,0:T(8,128)(2,1)} %param.4), kind=kLoop, calls=%fused_computation.6 | loop fusion | flops 57344 | bytes 57344 | tf_op jit(solution)/shard_map/concatenate | solution.py:185
  2.2 3.0 %collective-permute-start = (bf16[16,896]{1,0:T(8,128)(2,1)S(1)}, bf16[16,896]{1,0:T(8,128)(2,1)S(1)}, u32[]{:S(2)}, u32[]{:S(2)}) collective-permute-start(bf16[16,896]{1,0:T(8,128)(2,1)S(1)} %pad_maximum_fusion), channel_id=1, source_target_pairs={{0,4},{4,0},{8,12},{12,8},{16,20},{20,16},{24,28},{28,24},{1,5},{5... | collective-permute-start | bytes 86024 | tf_op jit(solution)/shard_map/ppermute | solution.py:188
  5.2 0.8 %copy.8.pos_ref = s32[128,8]{1,0:T(8,128)S(1)} copy(s32[128,8]{0,1:T(8,128)} %param.7) | data formatting | bytes 8192 | tf_op args[3]
  5.9 1.4 %shard_map.67.target_ref = bf16[2,2,128,512]{3,2,1,0:T(8,128)(2,1)S(1)} custom-call(s32[128,8]{1,0:T(8,128)S(1)} %copy.8.pos_ref), custom_call_target="tpu_custom_call" | custom-call | flops 201326592 | bytes 1572864 | tf_op jit(solution)/shard_map/pallas_call | solution.py:199
  7.4 1.8 %collective-permute-start.1 = (bf16[32,896]{1,0:T(8,128)(2,1)S(1)}, bf16[32,896]{1,0:T(8,128)(2,1)S(1)}, u32[]{:S(2)}, u32[]{:S(2)}) collective-permute-start(bf16[32,896]{1,0:T(8,128)(2,1)S(1)} %maximum_select_fusion.2), channel_id=1, source_target_pairs={{0,8},{4,12},{8,0},{12,4},{16,24},{20,28},{24,16},{28,20},{1,9},{5... | collective-permute-start | bytes 172040 | tf_op jit(solution)/shard_map/ppermute | solution.py:188
  9.2 2.4 %collective-permute-done.1 = bf16[32,896]{1,0:T(8,128)(2,1)S(1)} collective-permute-done((bf16[32,896]{1,0:T(8,128)(2,1)S(1)}, bf16[32,896]{1,0:T(8,128)(2,1)S(1)}, u32[]{:S(2)}, u32[]{:S(2)}) %collective-permute-start.1) | collective-permute-done | bytes 57376 | tf_op jit(solution)/shard_map/ppermute | solution.py:188
  11.7 2.8 %collective-permute-start.2 = (bf16[64,896]{1,0:T(8,128)(2,1)S(1)}, bf16[64,896]{1,0:T(8,128)(2,1)S(1)}, u32[]{:S(2)}, u32[]{:S(2)}) collective-permute-start(bf16[64,896]{1,0:T(8,128)(2,1)S(1)} %maximum_select_fusion.1), channel_id=1, source_target_pairs={{0,16},{4,20},{8,24},{12,28},{16,0},{20,4},{24,8},{28,12},{1,17},{... | collective-permute-start | bytes 344072 | tf_op jit(solution)/shard_map/ppermute | solution.py:188
  14.4 2.1 %broadcast_select_fusion.rows_ref = bf16[2,1,2,512,768]{4,3,2,1,0:T(8,128)(2,1)S(1)} fusion(bf16[2,1,2,512,768]{4,3,2,1,0:T(8,128)(2,1)} %bitcast.6, pred[768]{0:T(1024)(128)(4,1)S(1)} %compare_reduce_fusion), kind=kLoop, calls=%fused_computation | loop fusion | flops 1572864 | bytes 6292224 | tf_op jit(solution)/shard_map/jit(_where)/select_n | solution.py:195
  16.5 0.9 %collective-permute-done.2 = bf16[64,896]{1,0:T(8,128)(2,1)S(1)} collective-permute-done((bf16[64,896]{1,0:T(8,128)(2,1)S(1)}, bf16[64,896]{1,0:T(8,128)(2,1)S(1)}, u32[]{:S(2)}, u32[]{:S(2)}) %collective-permute-start.2) | collective-permute-done | bytes 114720 | tf_op jit(solution)/shard_map/ppermute | solution.py:188
  17.5 1.9 %shard_map.68 = (bf16[2,128,512]{2,1,0:T(8,128)(2,1)S(1)}, bf16[272,512]{1,0:T(8,128)(2,1)S(1)}, f32[1,128]{1,0:T(1,128)S(1)}) custom-call(bf16[128,896]{1,0:T(8,128)(2,1)S(1)} %maximum_select_fusion.panel_ref, bf16[2,1,2,512,768]{4,3,2,1,0:T(8,128)(2,1)S(1)} %broadcast_select_fusion.rows_ref, bf16[2,2,128,512]{3,2,1,0:T(8,128)(2,1)S(1)} %shard_map.67.target_ref), custom_call_target="tpu_custom_call" | custom-call | flops 402653184 | bytes 3145728 | tf_op jit(solution)/shard_map/pallas_call | solution.py:222
  19.4 2.9 %collective-permute-start.6 = (bf16[2,128,512]{2,1,0:T(8,128)(2,1)S(1)}, bf16[2,128,512]{2,1,0:T(8,128)(2,1)S(1)}, u32[]{:S(2)}, u32[]{:S(2)}) collective-permute-start(bf16[2,128,512]{2,1,0:T(8,128)(2,1)S(1)} %get-tuple-element.10.far_ref), channel_id=1, source_target_pairs={{0,2},{1,3},{2,0},{3,1},{4,6},{5,7},{6,4},{7,5},{8,10},{9,11},{10,... | collective-permute-start | bytes 786440 | tf_op jit(solution)/shard_map/ppermute | solution.py:229
  22.4 1.3 %shard_map.69 = bf16[128,896]{1,0:T(8,128)(2,1)} custom-call(bf16[2,128,512]{2,1,0:T(8,128)(2,1)S(1)} %get-tuple-element.10.far_ref, bf16[272,512]{1,0:T(8,128)(2,1)S(1)} %get-tuple-element.11.near_ref, bf16[2,1,2,512,768]{4,3,2,1,0:T(8,128)(2,1)S(1)} %broadcast_select_fusion.rows_ref, f32[1,128]{1,0:T(1,128)S(1)} %get-tuple-element.12.loss_ref, ...), custom_call_target="tpu_custom_call" | custom-call | flops 402653184 | bytes 3145728 | tf_op jit(solution)/shard_map/pallas_call | solution.py:231
  23.7 6.2 %all-to-all-start = ((bf16[8,16,896]{2,1,0:T(8,128)(2,1)}), bf16[8,16,896]{2,1,0:T(8,128)(2,1)S(1)}, u32[]{:S(2)}, u32[]{:S(2)}) async-start(bf16[8,16,896]{2,1,0:T(8,128)(2,1)} %bitcast.2), calls=%async_computation | async-start | bytes 458752 | tf_op jit(solution)/shard_map/all_to_all | solution.py:235
  29.9 0.5 %collective-permute-start.4 = (bf16[128,896]{1,0:T(8,128)(2,1)S(1)}, bf16[128,896]{1,0:T(8,128)(2,1)S(1)}, u32[]{:S(2)}, u32[]{:S(2)}) collective-permute-start(bf16[128,896]{1,0:T(8,128)(2,1)S(1)} %maximum_select_fusion.panel_ref), channel_id=1, source_target_pairs={{0,1},{1,0},{2,3},{3,2},{4,5},{5,4},{6,7},{7,6},{8,9},{9,8},{10,11... | collective-permute-start | bytes 688136 | tf_op jit(solution)/shard_map/ppermute | solution.py:228
  30.4 3.7 %collective-permute-done.5.panel_x_ref = bf16[128,896]{1,0:T(8,128)(2,1)S(1)} collective-permute-done((bf16[128,896]{1,0:T(8,128)(2,1)S(1)}, bf16[128,896]{1,0:T(8,128)(2,1)S(1)}, u32[]{:S(2)}, u32[]{:S(2)}) %collective-permute-start.5) | collective-permute-done | bytes 229408 | tf_op jit(solution)/shard_map/ppermute | solution.py:230
  34.1 1.5 %collective-permute-done.7.panel_xc_ref = bf16[128,896]{1,0:T(8,128)(2,1)S(1)} collective-permute-done((bf16[128,896]{1,0:T(8,128)(2,1)S(1)}, bf16[128,896]{1,0:T(8,128)(2,1)S(1)}, u32[]{:S(2)}, u32[]{:S(2)}) %collective-permute-start.7) | collective-permute-done | bytes 229408 | tf_op jit(solution)/shard_map/ppermute | solution.py:238
  35.6 1.9 %shard_map.70 = f32[512,768]{1,0:T(8,128)} custom-call(bf16[128,896]{1,0:T(8,128)(2,1)S(1)} %maximum_select_fusion.panel_ref, bf16[272,512]{1,0:T(8,128)(2,1)S(1)} %get-tuple-element.11.near_ref, bf16[128,896]{1,0:T(8,128)(2,1)S(1)} %collective-permute-done.4.panel_c_ref, bf16[272,512]{1,0:T(8,128)(2,1)S(1)} %collective-permute-done.3.core_ref.near_c_ref, ...), custom_call_target="tpu_custom_call" | custom-call | flops 402653184 | bytes 3145728 | tf_op jit(solution)/shard_map/pallas_call | solution.py:239
  37.6 0.8 %all-to-all-done.parts_ref = bf16[8,16,896]{2,1,0:T(8,128)(2,1)S(1)} async-done(((bf16[8,16,896]{2,1,0:T(8,128)(2,1)}), bf16[8,16,896]{2,1,0:T(8,128)(2,1)S(1)}, u32[]{:S(2)}, u32[]{:S(2)}) %all-to-all-start) | async-done | bytes 229408 | tf_op jit(solution)/shard_map/all_to_all | solution.py:235
  38.3 0.1 shard_map.72
  38.5 1.6 %collective-permute-start.9 = (f32[1,128]{1,0:T(1,128)S(1)}, f32[1,128]{1,0:T(1,128)S(1)}, u32[]{:S(2)}, u32[]{:S(2)}) collective-permute-start(f32[1,128]{1,0:T(1,128)S(1)} %shard_map.72), channel_id=1, source_target_pairs={{0,2},{1,3},{2,0},{3,1},{4,6},{5,7},{6,4},{7,5},{8,10},{9,11},{10,... | collective-permute-start | bytes 1544 | tf_op jit(solution)/shard_map/ppermute | solution.py:259
  40.0 0.6 %shard_map.71 = bf16[16,768]{1,0:T(8,128)(2,1)} custom-call(bf16[8,16,896]{2,1,0:T(8,128)(2,1)S(1)} %all-to-all-done.parts_ref), custom_call_target="tpu_custom_call" | custom-call | tf_op jit(solution)/shard_map/pallas_call | solution.py:261
  40.7 1.4 %collective-permute-done.9 = f32[1,128]{1,0:T(1,128)S(1)} collective-permute-done((f32[1,128]{1,0:T(1,128)S(1)}, f32[1,128]{1,0:T(1,128)S(1)}, u32[]{:S(2)}, u32[]{:S(2)}) %collective-permute-start.9) | collective-permute-done | bytes 544 | tf_op jit(solution)/shard_map/ppermute | solution.py:259
  42.1 0.5 %add.23 = f32[1,128]{1,0:T(1,128)} add(f32[1,128]{1,0:T(1,128)S(1)} %shard_map.72, f32[1,128]{1,0:T(1,128)S(1)} %collective-permute-done.9) | non-fusion elementwise | flops 128 | bytes 1536 | tf_op jit(solution)/shard_map/add | solution.py:269
  (15 shorter events, 0.4 us)
Async XLA Ops:
  2.2 5.2 %collective-permute-start = (bf16[16,896]{1,0:T(8,128)(2,1)S(1)}, bf16[16,896]{1,0:T(8,128)(2,1)S(1)}, u32[]{:S(2)}, u32[]{:S(2)}) collective-permute-start(bf16[16,896]{1,0:T(8,128)(2,1)S(1)} %pad_maximum_fusion), channel_id=1, source_target_pairs={{0,4},{4,0},{8,12},{12,8},{16,20},{20,16},{24,28},{28,24},{1,5},{5... | collective-permute-start | bytes 86024 | tf_op jit(solution)/shard_map/ppermute | solution.py:188
  7.4 4.2 %collective-permute-start.1 = (bf16[32,896]{1,0:T(8,128)(2,1)S(1)}, bf16[32,896]{1,0:T(8,128)(2,1)S(1)}, u32[]{:S(2)}, u32[]{:S(2)}) collective-permute-start(bf16[32,896]{1,0:T(8,128)(2,1)S(1)} %maximum_select_fusion.2), channel_id=1, source_target_pairs={{0,8},{4,12},{8,0},{12,4},{16,24},{20,28},{24,16},{28,20},{1,9},{5... | collective-permute-start | bytes 172040 | tf_op jit(solution)/shard_map/ppermute | solution.py:188
  11.7 5.8 %collective-permute-start.2 = (bf16[64,896]{1,0:T(8,128)(2,1)S(1)}, bf16[64,896]{1,0:T(8,128)(2,1)S(1)}, u32[]{:S(2)}, u32[]{:S(2)}) collective-permute-start(bf16[64,896]{1,0:T(8,128)(2,1)S(1)} %maximum_select_fusion.1), channel_id=1, source_target_pairs={{0,16},{4,20},{8,24},{12,28},{16,0},{20,4},{24,8},{28,12},{1,17},{... | collective-permute-start | bytes 344072 | tf_op jit(solution)/shard_map/ppermute | solution.py:188
  19.3 3.1 %collective-permute-start.3 = (bf16[272,512]{1,0:T(8,128)(2,1)S(1)}, bf16[272,512]{1,0:T(8,128)(2,1)S(1)}, u32[]{:S(2)}, u32[]{:S(2)}) collective-permute-start(bf16[272,512]{1,0:T(8,128)(2,1)S(1)} %get-tuple-element.11.near_ref), channel_id=1, source_target_pairs={{0,1},{1,0},{2,3},{3,2},{4,5},{5,4},{6,7},{7,6},{8,9},{9,8},{10,11... | collective-permute-start | bytes 835592 | tf_op jit(solution)/shard_map/ppermute | solution.py:227
  19.4 10.4 %collective-permute-start.6 = (bf16[2,128,512]{2,1,0:T(8,128)(2,1)S(1)}, bf16[2,128,512]{2,1,0:T(8,128)(2,1)S(1)}, u32[]{:S(2)}, u32[]{:S(2)}) collective-permute-start(bf16[2,128,512]{2,1,0:T(8,128)(2,1)S(1)} %get-tuple-element.10.far_ref), channel_id=1, source_target_pairs={{0,2},{1,3},{2,0},{3,1},{4,6},{5,7},{6,4},{7,5},{8,10},{9,11},{10,... | collective-permute-start | bytes 786440 | tf_op jit(solution)/shard_map/ppermute | solution.py:229
  22.3 11.8 %collective-permute-start.5 = (bf16[128,896]{1,0:T(8,128)(2,1)S(1)}, bf16[128,896]{1,0:T(8,128)(2,1)S(1)}, u32[]{:S(2)}, u32[]{:S(2)}) collective-permute-start(bf16[128,896]{1,0:T(8,128)(2,1)S(1)} %maximum_select_fusion.panel_ref), channel_id=1, source_target_pairs={{0,2},{1,3},{2,0},{3,1},{4,6},{5,7},{6,4},{7,5},{8,10},{9,11},{10,... | collective-permute-start | bytes 688136 | tf_op jit(solution)/shard_map/ppermute | solution.py:230
  23.7 14.7 %all-to-all-start = ((bf16[8,16,896]{2,1,0:T(8,128)(2,1)}), bf16[8,16,896]{2,1,0:T(8,128)(2,1)S(1)}, u32[]{:S(2)}, u32[]{:S(2)}) async-start(bf16[8,16,896]{2,1,0:T(8,128)(2,1)} %bitcast.2), calls=%async_computation | async-start | bytes 458752 | tf_op jit(solution)/shard_map/all_to_all | solution.py:235
  29.9 5.8 %collective-permute-start.8 = (bf16[2,128,512]{2,1,0:T(8,128)(2,1)S(1)}, bf16[2,128,512]{2,1,0:T(8,128)(2,1)S(1)}, u32[]{:S(2)}, u32[]{:S(2)}) collective-permute-start(bf16[2,128,512]{2,1,0:T(8,128)(2,1)S(1)} %collective-permute-done.6.far_x_ref), channel_id=1, source_target_pairs={{0,1},{1,0},{2,3},{3,2},{4,5},{5,4},{6,7},{7,6},{8,9},{9,8},{10,11... | collective-permute-start | bytes 786440 | tf_op jit(solution)/shard_map/ppermute | solution.py:237
  29.9 4.2 %collective-permute-start.4 = (bf16[128,896]{1,0:T(8,128)(2,1)S(1)}, bf16[128,896]{1,0:T(8,128)(2,1)S(1)}, u32[]{:S(2)}, u32[]{:S(2)}) collective-permute-start(bf16[128,896]{1,0:T(8,128)(2,1)S(1)} %maximum_select_fusion.panel_ref), channel_id=1, source_target_pairs={{0,1},{1,0},{2,3},{3,2},{4,5},{5,4},{6,7},{7,6},{8,9},{9,8},{10,11... | collective-permute-start | bytes 688136 | tf_op jit(solution)/shard_map/ppermute | solution.py:228
  34.1 1.5 %collective-permute-start.7 = (bf16[128,896]{1,0:T(8,128)(2,1)S(1)}, bf16[128,896]{1,0:T(8,128)(2,1)S(1)}, u32[]{:S(2)}, u32[]{:S(2)}) collective-permute-start(bf16[128,896]{1,0:T(8,128)(2,1)S(1)} %collective-permute-done.5.panel_x_ref), channel_id=1, source_target_pairs={{0,1},{1,0},{2,3},{3,2},{4,5},{5,4},{6,7},{7,6},{8,9},{9,8},{10,11... | collective-permute-start | bytes 688136 | tf_op jit(solution)/shard_map/ppermute | solution.py:238
  38.5 3.6 %collective-permute-start.9 = (f32[1,128]{1,0:T(1,128)S(1)}, f32[1,128]{1,0:T(1,128)S(1)}, u32[]{:S(2)}, u32[]{:S(2)}) collective-permute-start(f32[1,128]{1,0:T(1,128)S(1)} %shard_map.72), channel_id=1, source_target_pairs={{0,2},{1,3},{2,0},{3,1},{4,6},{5,7},{6,4},{7,5},{8,10},{9,11},{10,... | collective-permute-start | bytes 1544 | tf_op jit(solution)/shard_map/ppermute | solution.py:259

commit v6 on v5

--- a/solution.py
+++ b/solution.py
@@ -8,7 +8,7 @@
 from jax.sharding import PartitionSpec as P
 
 LANES = 128
-EXTRA = 16
+EXTRA = 48
 F32, BF16 = jnp.float32, jnp.bfloat16
 VMEM = pl.BlockSpec(memory_space=pltpu.VMEM)
 HBM = pl.BlockSpec(memory_space=pltpu.HBM)
@@ -97,49 +97,64 @@
     return jnp.where(row == 0, top, jnp.where(row == 1, mid, low)).astype(BF16)
 
 
-def first_kernel(plan, panel_ref, rows_ref, target_ref, far_ref, near_ref, loss_ref):
+def first_kernel(
+    plan, panel_ref, rows_ref, target_ref, far_ref, near_ref, own_ref, loss_ref
+):
     half, core = plan.place()
-    docs = panel_ref[:, : plan.width]
+    width, labels, block = plan.width, plan.labels, plan.block
+    docs = panel_ref[:, :width]
     mine = listed_counts(plan, panel_ref)
     losses = jnp.zeros(loss_ref.shape, F32)
+    far_ref[:, :width] = docs
+    near_ref[:block, :width] = docs
     for i, (h, c) in enumerate(plan.order(half, core)):
         weight, more = set_weights(
             plan, mine, docs, plan.rows(rows_ref, h, c), target_ref[h, c], h, c
         )
         if i < 2:
-            far_ref[i] = weight
+            far_ref[:, width + i * labels : width + (i + 1) * labels] = weight
+        elif i == 2:
+            near_ref[:block, width:] = weight
         else:
-            near_ref[(i - 2) * plan.block : (i - 1) * plan.block] = weight
+            own_ref[...] = weight
         losses = losses + more
     loss_ref[...] = losses
-    near_ref[2 * plan.block :, :LANES] = split_rows(losses, EXTRA)
-    near_ref[2 * plan.block :, LANES:] = jnp.zeros((EXTRA, plan.labels - LANES), BF16)
-
-
-def send_kernel(plan, far_ref, near_ref, rows_ref, loss_ref, core_ref, send_ref):
+    near_ref[block:, :LANES] = split_rows(losses, EXTRA)
+    near_ref[block:, LANES:] = jnp.zeros((EXTRA, width + labels - LANES), BF16)
+
+
+def send_kernel(plan, far_ref, near_ref, own_ref, rows_ref, loss_ref, core_ref, send_ref):
     half, core = plan.place()
-    part = jnp.zeros((plan.block, plan.width), F32)
+    width, labels, block = plan.width, plan.labels, plan.block
+    part = jnp.zeros((block, width), F32)
     for i, (h, c) in enumerate(plan.order(half, core)):
-        weight = far_ref[i] if i < 2 else near_ref[(i - 2) * plan.block : (i - 1) * plan.block]
+        if i < 2:
+            weight = far_ref[:, width + i * labels : width + (i + 1) * labels]
+        else:
+            weight = near_ref[:block, width:] if i == 2 else own_ref[...]
         part = part + jnp.dot(weight, plan.rows(rows_ref, h, c), preferred_element_type=F32)
-    send_ref[:, : plan.width] = part.astype(BF16)
-    theirs = core_ref[2 * plan.block :, :LANES].astype(F32)
+    send_ref[:, :, :width] = part.astype(BF16).reshape(block // 16, 16, width)
+    theirs = core_ref[block : block + 16, :LANES].astype(F32)
     losses = loss_ref[...] + jnp.sum(theirs, axis=0, keepdims=True)
-    send_ref[:, plan.width :] = split_rows(losses, plan.block)
+    send_ref[:, :, width:] = split_rows(losses, block).reshape(block // 16, 16, LANES)
 
 
 def last_kernel(
-    plan, panel_ref, near_ref, panel_c_ref, near_c_ref, panel_x_ref, far_x_ref, panel_xc_ref,
-    far_xc_ref, out_hbm, sum_ref, sems,
+    plan, panel_ref, own_ref, core_ref, x_ref, xc_ref, parts_ref, out_hbm, doc_hbm,
+    sum_ref, doc_ref, sems,
 ):
-    copies = []
-    for start in range(0, plan.labels, LANES):
+    width, labels, block = plan.width, plan.labels, plan.block
+    doc_ref[...] = jnp.sum(parts_ref[:, :, :width].astype(F32), axis=0).astype(BF16)
+    copies = [pltpu.make_async_copy(doc_ref, doc_hbm, sems.at[0])]
+    copies[0].start()
+    for start in range(0, labels, LANES):
+        first, second = width + start, width + labels + start
         part = pl.ds(start, LANES)
         sum_ref[part] = (
-            label_grad(near_ref[pl.ds(plan.block, plan.block), part], panel_ref[:, : plan.width])
-            + label_grad(near_c_ref[pl.ds(0, plan.block), part], panel_c_ref[:, : plan.width])
-            + label_grad(far_x_ref[1, :, part], panel_x_ref[:, : plan.width])
-            + label_grad(far_xc_ref[0, :, part], panel_xc_ref[:, : plan.width])
+            label_grad(own_ref[:, start : start + LANES], panel_ref[:, :width])
+            + label_grad(core_ref[:block, first : first + LANES], core_ref[:block, :width])
+            + label_grad(x_ref[:, second : second + LANES], x_ref[:, :width])
+            + label_grad(xc_ref[:, first : first + LANES], xc_ref[:, :width])
         )
         copies.append(
             pltpu.make_async_copy(sum_ref.at[part], out_hbm.at[part], sems.at[len(copies)])
@@ -147,11 +162,6 @@
         copies[-1].start()
     for copy in copies:
         copy.wait()
-
-
-def doc_kernel(parts_ref, doc_ref):
-    width = doc_ref.shape[1]
-    doc_ref[...] = jnp.sum(parts_ref[:, :, :width].astype(F32), axis=0).astype(BF16)
 
 
 def loss_kernel(scale, parts_ref, loss_ref):
@@ -205,7 +215,7 @@
         cost_estimate=cost(2, 0),
     )(positives)
 
-    grad_shape, pair_shape = (labels, width), (2, block, labels)
+    grad_shape = (labels, width)
 
     def kernel(body, count, outs, dots, scored=0, **options):
         return pl.pallas_call(
@@ -218,33 +228,36 @@
             **options,
         )
 
-    near_shape = (2 * block + EXTRA, labels)
-    far, near, loss = kernel(
-        first_kernel, 3, [shape(pair_shape, BF16), shape(near_shape, BF16), shape((1, LANES), F32)],
+    far, near, own, loss = kernel(
+        first_kernel, 3,
+        [
+            shape((block, width + 2 * labels), BF16), shape((block + EXTRA, width + labels), BF16),
+            shape((block, labels), BF16), shape((1, LANES), F32),
+        ],
         4, 4,
     )(panel, rows, target)
     step = doc_count // 2
-    near_c = lax.ppermute(near, "doc", flip(doc_count, 1))
-    panel_c = lax.ppermute(panel, "doc", flip(doc_count, 1))
-    far_x = lax.ppermute(far, "doc", flip(doc_count, step))
-    panel_x = lax.ppermute(panel, "doc", flip(doc_count, step))
-    (send,) = kernel(send_kernel, 5, [shape((block, width + LANES), BF16)], 4)(
-        far, near, rows, loss, near_c
+    from_core = lax.ppermute(near, "doc", flip(doc_count, 1))
+    from_x = lax.ppermute(far, "doc", flip(doc_count, step))
+    (send,) = kernel(send_kernel, 6, [shape((label_count, doc_dev, width + LANES), BF16)], 4)(
+        far, near, own, rows, loss, from_core
     )
-    send = send.reshape(label_count, doc_dev, width + LANES)
-    parts = lax.all_to_all(send, "label", split_axis=0, concat_axis=0, tiled=True)
-
-    far_xc = lax.ppermute(far_x, "doc", flip(doc_count, 1))
-    panel_xc = lax.ppermute(panel_x, "doc", flip(doc_count, 1))
-    class_grad = kernel(
-        last_kernel, 8, shape(grad_shape, F32), 4,
-        out_specs=HBM,
+
+    def exchange(send):
+        return lax.all_to_all(send, "label", split_axis=0, concat_axis=0, tiled=True)
+
+    parts = lax.cond(shortlist[0, 0, 0] >= 0, exchange, jnp.zeros_like, send)
+    parts, from_x = lax.optimization_barrier((parts, from_x))
+    over_core = lax.ppermute(from_x, "doc", flip(doc_count, 1))
+    class_grad, doc_grad = kernel(
+        last_kernel, 6, [shape(grad_shape, F32), shape((doc_dev, width), BF16)], 4,
+        out_specs=[HBM, HBM],
         scratch_shapes=[
-            pltpu.VMEM(grad_shape, F32), pltpu.SemaphoreType.DMA((labels // LANES,))
+            pltpu.VMEM(grad_shape, F32), pltpu.VMEM((doc_dev, width), BF16),
+            pltpu.SemaphoreType.DMA((labels // LANES + 1,)),
         ],
-    )(panel, near, panel_c, near_c, panel_x, far_x, panel_xc, far_xc)
-
-    parts, class_grad = lax.optimization_barrier((parts, class_grad))
+    )(panel, own, from_core, from_x, over_core, parts)
+
     entry_total = block * doc_count * label_count * listed * tile
     loss = pl.pallas_call(
         functools.partial(loss_kernel, 1.0 / entry_total),
@@ -258,14 +271,7 @@
         loss = loss + other if bit > 2 else loss
         other = lax.ppermute(loss, "doc", flip(doc_count, bit))
         bit *= 2
-    doc_grad = pl.pallas_call(
-        doc_kernel,
-        in_specs=[VMEM],
-        out_specs=VMEM,
-        out_shape=shape((doc_dev, width), BF16),
-        compiler_params=params,
-    )(parts)
-    doc_grad, other = lax.optimization_barrier((doc_grad, other))
+    class_grad, other = lax.optimization_barrier((class_grad, other))
     mean_loss = (loss + other)[0, 0]
     class_grad = class_grad.reshape(x_half, group * tile, width)
     step = x_half // 2

time: 42.9 us -> 42 us (0.979)
  blocking collectives: 0 us -> 14.4 us
  waiting for transfers between devices: 10.7 us -> 3.44 us
  starting transfers between devices: 18.9 us -> 12.1 us
  Pallas kernels: 7.22 us -> 5.94 us
    all_to_all x0 -> x1, blocking collectives: none -> 14.4 us  [exchange(): lax.all_to_all(send, 'label', split_axis=0, concat_axis=0, tiled=True)]
    all_to_all x1 -> x0, starting transfers between devices: 6.16 us -> none  [per_device(): lax.all_to_all(send, 'label', split_axis=0, concat_axis=0, tiled=True)]
    ppermute x6 -> x3, waiting for transfers between devices: 5.19 us -> 0.12 us  [the longest x1 0.12 us: per_device(): over_core = lax.ppermute(from_x, 'doc', flip(doc_count, 1))]
    ppermute x1, waiting for transfers between devices: 1.41 us -> 0.01 us  [per_device(): other = lax.ppermute(loss, 'doc', flip(doc_count, bit))]
    pallas_call x4 -> x3, Pallas kernels: 5.69 us -> 4.41 us  [the longest x1 1.93 us: per_device(): kernel(last_kernel, 6, [shape(grad_shape, F32), shape((doc_dev, width), B...]
    all_to_all x1 -> x0, waiting for transfers between devices: 0.79 us -> none  [per_device(): lax.all_to_all(send, 'label', split_axis=0, concat_axis=0, tiled=True)]
    ppermute x6 -> x3, starting transfers between devices: 3.64 us -> 2.98 us  [the longest x1 2.9 us: per_device(): from_x = lax.ppermute(far, 'doc', flip(doc_count, step))]
  transfers between devices with their start and end apart: 11 -> 7, of which waited for: 6 -> 3; matrix products, arithmetic and copies ran while one was open for 7% -> 7% of each run, Pallas kernels for 12% -> 10%
where the time goes in v6:
time: 42 us; the launch traced here: 41.7 us
  blocking collectives  14.4 us (34%)
  starting transfers between devices  12.1 us (29%)
  Pallas kernels  5.94 us (14%)
  other arithmetic  4.26 us (10%)
  waiting for transfers between devices  3.44 us (8%)
  local copies, waits for them, and re-layouts  0.79 us (2%)
  between operations  0.79 us (2%)
    all_to_all x1, blocking collectives, exchange(): lax.all_to_all(send, 'label', split_axis=0, concat_axis=0, tiled=True)  14.4 us
    ppermute x3, starting transfers between devices, per_device(): other = lax.ppermute(panel, 'label', flip(label_count, bit))  7.53 us
    ppermute x3, waiting for transfers between devices, per_device(): other = lax.ppermute(panel, 'label', flip(label_count, bit))  3.31 us
    ppermute x1, starting transfers between devices, per_device(): from_x = lax.ppermute(far, 'doc', flip(doc_count, step))  2.9 us
    select_n x1, other arithmetic, per_device(): flat = jnp.where(early, classifier.reshape(-1, width), 0)  2.1 us
    pallas_call x1, Pallas kernels, per_device(): kernel(last_kernel, 6, [shape(grad_shape, F32), shape((doc_dev, width), B...  1.93 us
    pallas_call x1, Pallas kernels, per_device(): kernel(first_kernel, 3, [shape((block, width + 2 * labels), BF16), shape(...  1.86 us
    ppermute x1, starting transfers between devices, per_device(): other = lax.ppermute(loss, 'doc', flip(doc_count, bit))  1.56 us
  transfers between devices with their start and end apart: 7, of which 3 were waited for; matrix products, arithmetic and copies ran while one was open for 7% of the time, Pallas kernels for 10%

profile of v6, /device:TPU:0, one launch (start us, length us, event | category | flops | bytes accessed | tf_op | source)
XLA Modules:
  0.0 41.7 jit_solution(2051836174309707290)
XLA Ops:
  0.6 0.8 %fusion = pred[16,128]{1,0:T(8,128)(4,1)S(1)} fusion(s32[32]{0:T(128)} %bitcast.8, s32[16]{0:T(128)S(1)} %iota_multiply_fusion), kind=kLoop, calls=%fused_computation.2 | loop fusion | flops 194560 | bytes 2240 | tf_op jit(solution)/shard_map/reduce_or | solution.py:194
  1.4 0.7 %pad_maximum_fusion = bf16[16,896]{1,0:T(8,128)(2,1)S(1)} fusion(bf16[16,128]{1,0:T(8,128)(2,1)S(1)} %convert_element_type.11, bf16[16,768]{1,0:T(8,128)(2,1)} %param.6), kind=kLoop, calls=%fused_computation.6 | loop fusion | flops 57344 | bytes 57344 | tf_op jit(solution)/shard_map/concatenate | solution.py:195
  2.2 3.0 %collective-permute-start = (bf16[16,896]{1,0:T(8,128)(2,1)S(1)}, bf16[16,896]{1,0:T(8,128)(2,1)S(1)}, u32[]{:S(2)}, u32[]{:S(2)}) collective-permute-start(bf16[16,896]{1,0:T(8,128)(2,1)S(1)} %pad_maximum_fusion), channel_id=1, source_target_pairs={{0,4},{4,0},{8,12},{12,8},{16,20},{20,16},{24,28},{28,24},{1,5},{5... | collective-permute-start | bytes 86024 | tf_op jit(solution)/shard_map/ppermute | solution.py:198
  5.2 0.8 %copy.8.pos_ref = s32[128,8]{1,0:T(8,128)S(1)} copy(s32[128,8]{0,1:T(8,128)} %param.9) | data formatting | bytes 8192 | tf_op args[3]
  5.9 1.4 %shard_map.67.target_ref = bf16[2,2,128,512]{3,2,1,0:T(8,128)(2,1)S(1)} custom-call(s32[128,8]{1,0:T(8,128)S(1)} %copy.8.pos_ref), custom_call_target="tpu_custom_call" | custom-call | flops 201326592 | bytes 1572864 | tf_op jit(solution)/shard_map/pallas_call | solution.py:209
  7.4 1.8 %collective-permute-start.1 = (bf16[32,896]{1,0:T(8,128)(2,1)S(1)}, bf16[32,896]{1,0:T(8,128)(2,1)S(1)}, u32[]{:S(2)}, u32[]{:S(2)}) collective-permute-start(bf16[32,896]{1,0:T(8,128)(2,1)S(1)} %maximum_select_fusion.2), channel_id=1, source_target_pairs={{0,8},{4,12},{8,0},{12,4},{16,24},{20,28},{24,16},{28,20},{1,9},{5... | collective-permute-start | bytes 172040 | tf_op jit(solution)/shard_map/ppermute | solution.py:198
  9.2 2.4 %collective-permute-done.1 = bf16[32,896]{1,0:T(8,128)(2,1)S(1)} collective-permute-done((bf16[32,896]{1,0:T(8,128)(2,1)S(1)}, bf16[32,896]{1,0:T(8,128)(2,1)S(1)}, u32[]{:S(2)}, u32[]{:S(2)}) %collective-permute-start.1) | collective-permute-done | bytes 57376 | tf_op jit(solution)/shard_map/ppermute | solution.py:198
  11.7 2.8 %collective-permute-start.2 = (bf16[64,896]{1,0:T(8,128)(2,1)S(1)}, bf16[64,896]{1,0:T(8,128)(2,1)S(1)}, u32[]{:S(2)}, u32[]{:S(2)}) collective-permute-start(bf16[64,896]{1,0:T(8,128)(2,1)S(1)} %maximum_select_fusion.1), channel_id=1, source_target_pairs={{0,16},{4,20},{8,24},{12,28},{16,0},{20,4},{24,8},{28,12},{1,17},{... | collective-permute-start | bytes 344072 | tf_op jit(solution)/shard_map/ppermute | solution.py:198
  14.4 2.1 %broadcast_select_fusion.rows_ref = bf16[2,1,2,512,768]{4,3,2,1,0:T(8,128)(2,1)S(1)} fusion(bf16[2,1,2,512,768]{4,3,2,1,0:T(8,128)(2,1)} %bitcast.7, pred[768]{0:T(1024)(128)(4,1)S(1)} %compare_reduce_fusion), kind=kLoop, calls=%fused_computation | loop fusion | flops 1572864 | bytes 6292224 | tf_op jit(solution)/shard_map/jit(_where)/select_n | solution.py:205
  16.5 0.0 copy-start
  16.6 0.9 %collective-permute-done.2 = bf16[64,896]{1,0:T(8,128)(2,1)S(1)} collective-permute-done((bf16[64,896]{1,0:T(8,128)(2,1)S(1)}, bf16[64,896]{1,0:T(8,128)(2,1)S(1)}, u32[]{:S(2)}, u32[]{:S(2)}) %collective-permute-start.2) | collective-permute-done | bytes 114720 | tf_op jit(solution)/shard_map/ppermute | solution.py:198
  17.5 1.9 %shard_map.68 = (bf16[128,1792]{1,0:T(8,128)(2,1)S(1)}, bf16[176,1280]{1,0:T(8,128)(2,1)S(1)}, bf16[128,512]{1,0:T(8,128)(2,1)S(1)}, f32[1,128]{1,0:T(1,128)S(1)}) custom-call(bf16[128,896]{1,0:T(8,128)(2,1)S(1)} %maximum_select_fusion.panel_ref, bf16[2,1,2,512,768]{4,3,2,1,0:T(8,128)(2,1)S(1)} %broadcast_select_fusion.rows_ref, ...), custom_call_target="tpu_custom_call" | custom-call | flops 402653184 | bytes 3145728 | tf_op jit(solution)/shard_map/pallas_call | solution.py:231
  19.3 0.1 collective-permute-start.3
  19.4 2.9 %collective-permute-start.4 = (bf16[128,1792]{1,0:T(8,128)(2,1)S(1)}, bf16[128,1792]{1,0:T(8,128)(2,1)S(1)}, u32[]{:S(2)}, u32[]{:S(2)}) collective-permute-start(bf16[128,1792]{1,0:T(8,128)(2,1)S(1)} %get-tuple-element.19.far_ref), channel_id=1, source_target_pairs={{0,2},{1,3},{2,0},{3,1},{4,6},{5,7},{6,4},{7,5},{8,10},{9,11},{10,... | collective-permute-start | bytes 1376264 | tf_op jit(solution)/shard_map/ppermute | solution.py:241
  22.4 0.0 collective-permute-done.3.core_ref
  22.4 0.6 %shard_map.69 = bf16[8,16,896]{2,1,0:T(8,128)(2,1)S(1)} custom-call(bf16[128,1792]{1,0:T(8,128)(2,1)S(1)} %get-tuple-element.19.far_ref, bf16[176,1280]{1,0:T(8,128)(2,1)S(1)} %get-tuple-element.18.near_ref, bf16[128,512]{1,0:T(8,128)(2,1)S(1)} %get-tuple-element.17.own_ref, bf16[2,1,2,512,768]{4,3,2,1,0:T(8,128)(2,1)S(1)} %broadcast_select_fusion.rows_ref, ...), custom_call_target="tpu_custom_call" | custom-call | flops 402653184 | bytes 3145728 | tf_op jit(solution)/shard_map/pallas_call | solution.py:242
  23.0 14.4 %conditional.1 = (bf16[8,16,896]{2,1,0:T(8,128)(2,1)S(1)}) conditional(s32[]{:T(128)} %bitcast.2, () %tuple.16, bf16[8,16,896]{2,1,0:T(8,128)(2,1)S(1)} %shard_map.69), branch_computations={%region_1.2_spmd, %region_2.3_spmd} | conditional | bytes 458760 | solution.py:249
  23.0 14.4 %all_to_all.4 = bf16[8,16,896]{2,1,0:T(8,128)(2,1)S(1)} all-to-all(bf16[8,16,896]{2,1,0:T(8,128)(2,1)S(1)} %param.1), channel_id=1, replica_groups=mesh['label'=8,'doc'=4] {'label'}, dimensions={0} | all-to-all | bytes 458752 | tf_op jit(solution)/shard_map/cond/branch_1_fun/all_to_all | solution.py:247
  37.4 0.1 shard_map.71
  37.6 1.6 %collective-permute-start.6 = (f32[1,128]{1,0:T(1,128)S(1)}, f32[1,128]{1,0:T(1,128)S(1)}, u32[]{:S(2)}, u32[]{:S(2)}) collective-permute-start(f32[1,128]{1,0:T(1,128)S(1)} %shard_map.71), channel_id=1, source_target_pairs={{0,2},{1,3},{2,0},{3,1},{4,6},{5,7},{6,4},{7,5},{8,10},{9,11},{10,... | collective-permute-start | bytes 1544 | tf_op jit(solution)/shard_map/ppermute | solution.py:272
  39.1 0.1 collective-permute-done.5.xc_ref
  39.3 1.9 %shard_map.70 = (f32[512,768]{1,0:T(8,128)}, bf16[16,768]{1,0:T(8,128)(2,1)}) custom-call(bf16[128,896]{1,0:T(8,128)(2,1)S(1)} %maximum_select_fusion.panel_ref, bf16[128,512]{1,0:T(8,128)(2,1)S(1)} %get-tuple-element.17.own_ref, bf16[176,1280]{1,0:T(8,128)(2,1)S(1)} %collective-permute-done.3.core_ref, bf16[128,1792]{1,0:T(8,128)(2,1)S(1)} %collective-permute-done.4.x_ref, ...), custom_call_target="tpu_custom_call" | custom-call | flops 402653184 | bytes 3145728 | tf_op jit(solution)/shard_map/pallas_call | solution.py:252
  41.2 0.0 collective-permute-done.6
  41.2 0.5 %add.23 = f32[1,128]{1,0:T(1,128)} add(f32[1,128]{1,0:T(1,128)S(1)} %shard_map.71, f32[1,128]{1,0:T(1,128)S(1)} %collective-permute-done.6) | non-fusion elementwise | flops 128 | bytes 1536 | tf_op jit(solution)/shard_map/add | solution.py:275
  (10 shorter events, 0.1 us)
Async XLA Ops:
  2.2 5.2 %collective-permute-start = (bf16[16,896]{1,0:T(8,128)(2,1)S(1)}, bf16[16,896]{1,0:T(8,128)(2,1)S(1)}, u32[]{:S(2)}, u32[]{:S(2)}) collective-permute-start(bf16[16,896]{1,0:T(8,128)(2,1)S(1)} %pad_maximum_fusion), channel_id=1, source_target_pairs={{0,4},{4,0},{8,12},{12,8},{16,20},{20,16},{24,28},{28,24},{1,5},{5... | collective-permute-start | bytes 86024 | tf_op jit(solution)/shard_map/ppermute | solution.py:198
  7.4 4.2 %collective-permute-start.1 = (bf16[32,896]{1,0:T(8,128)(2,1)S(1)}, bf16[32,896]{1,0:T(8,128)(2,1)S(1)}, u32[]{:S(2)}, u32[]{:S(2)}) collective-permute-start(bf16[32,896]{1,0:T(8,128)(2,1)S(1)} %maximum_select_fusion.2), channel_id=1, source_target_pairs={{0,8},{4,12},{8,0},{12,4},{16,24},{20,28},{24,16},{28,20},{1,9},{5... | collective-permute-start | bytes 172040 | tf_op jit(solution)/shard_map/ppermute | solution.py:198
  11.7 5.8 %collective-permute-start.2 = (bf16[64,896]{1,0:T(8,128)(2,1)S(1)}, bf16[64,896]{1,0:T(8,128)(2,1)S(1)}, u32[]{:S(2)}, u32[]{:S(2)}) collective-permute-start(bf16[64,896]{1,0:T(8,128)(2,1)S(1)} %maximum_select_fusion.1), channel_id=1, source_target_pairs={{0,16},{4,20},{8,24},{12,28},{16,0},{20,4},{24,8},{28,12},{1,17},{... | collective-permute-start | bytes 344072 | tf_op jit(solution)/shard_map/ppermute | solution.py:198
  16.5 5.8 %copy-start = (s32[1,1,32]{2,1,0:T(1,128)S(1)}, s32[1,1,32]{2,1,0:T(1,128)}, u32[]{:S(2)}) copy-start(s32[1,1,32]{2,1,0:T(1,128)} %param.8) | copy-start | bytes 388
  19.3 3.0 %collective-permute-start.3 = (bf16[176,1280]{1,0:T(8,128)(2,1)S(1)}, bf16[176,1280]{1,0:T(8,128)(2,1)S(1)}, u32[]{:S(2)}, u32[]{:S(2)}) collective-permute-start(bf16[176,1280]{1,0:T(8,128)(2,1)S(1)} %get-tuple-element.18.near_ref), channel_id=1, source_target_pairs={{0,1},{1,0},{2,3},{3,2},{4,5},{5,4},{6,7},{7,6},{8,9},{9,8},{10,11... | collective-permute-start | bytes 1351688 | tf_op jit(solution)/shard_map/ppermute | solution.py:240
  19.4 18.0 %collective-permute-start.4 = (bf16[128,1792]{1,0:T(8,128)(2,1)S(1)}, bf16[128,1792]{1,0:T(8,128)(2,1)S(1)}, u32[]{:S(2)}, u32[]{:S(2)}) collective-permute-start(bf16[128,1792]{1,0:T(8,128)(2,1)S(1)} %get-tuple-element.19.far_ref), channel_id=1, source_target_pairs={{0,2},{1,3},{2,0},{3,1},{4,6},{5,7},{6,4},{7,5},{8,10},{9,11},{10,... | collective-permute-start | bytes 1376264 | tf_op jit(solution)/shard_map/ppermute | solution.py:241
  37.4 1.8 %collective-permute-start.5 = (bf16[128,1792]{1,0:T(8,128)(2,1)S(1)}, bf16[128,1792]{1,0:T(8,128)(2,1)S(1)}, u32[]{:S(2)}, u32[]{:S(2)}) collective-permute-start(bf16[128,1792]{1,0:T(8,128)(2,1)S(1)} %collective-permute-done.4.x_ref), channel_id=1, source_target_pairs={{0,1},{1,0},{2,3},{3,2},{4,5},{5,4},{6,7},{7,6},{8,9},{9,8},{10,11... | collective-permute-start | bytes 1376264 | tf_op jit(solution)/shard_map/ppermute | solution.py:251
  37.6 3.6 %collective-permute-start.6 = (f32[1,128]{1,0:T(1,128)S(1)}, f32[1,128]{1,0:T(1,128)S(1)}, u32[]{:S(2)}, u32[]{:S(2)}) collective-permute-start(f32[1,128]{1,0:T(1,128)S(1)} %shard_map.71), channel_id=1, source_target_pairs={{0,2},{1,3},{2,0},{3,1},{4,6},{5,7},{6,4},{7,5},{8,10},{9,11},{10,... | collective-permute-start | bytes 1544 | tf_op jit(solution)/shard_map/ppermute | solution.py:272
